TPU v7x, 32 devices: a whole 2x2x4 slice. The times are simulated.
32 devices in a mesh: groups: 2 (over y), seq: 4 (over z), tensor: 2 (over x), ctx: 2 (over core).
Axes of the slice: x: 2, y: 2, z: 4, core: 2. Of those that a mesh axis runs over, the one named last changes fastest.
Arguments:
- query_in: bfloat16 [8192, 4096], P(('groups', 'seq', 'ctx'), 'tensor'), parts along dimension 0, may hold values from -6 to 6
- key_in: bfloat16 [8192, 4096], P(('groups', 'seq', 'ctx'), 'tensor'), parts along dimension 0, may hold values from -6 to 6
- value_in: bfloat16 [8192, 4096], P(('groups', 'seq', 'ctx'), 'tensor'), parts along dimension 0, may hold values from -6 to 6
- log_decay: float32 [32, 8192], P('tensor', ('groups', 'seq', 'ctx')), parts along dimension 1, may hold values from -2 to 0
- doc_start: int32 [8192], P(('groups', 'seq', 'ctx')), parts along dimension 0, may hold values 0 or 1
- out_grad: bfloat16 [8192, 4096], P(('groups', 'seq', 'ctx'), 'tensor'), parts along dimension 0, may hold values from -6 to 6
Outputs:
- normed: bfloat16 [8192, 4096], P(('groups', 'seq', 'ctx'), 'tensor'), parts along dimension 0
- query_gradient: bfloat16 [8192, 4096], P(('groups', 'seq', 'ctx'), 'tensor'), parts along dimension 0
- key_gradient: bfloat16 [8192, 4096], P(('groups', 'seq', 'ctx'), 'tensor'), parts along dimension 0
- value_gradient: bfloat16 [8192, 4096], P(('groups', 'seq', 'ctx'), 'tensor'), parts along dimension 0
There are 2 independent parts, one for each index of `groups`. A program takes and returns all parts, laid end to end along the dimension named above; each array names one. Nothing has to cross between parts.
All inputs are finite; a program needn't handle non-finite values. No bound on the sum of `doc_start` on one device may be relied on, other than what follows from the above.
Results may differ from a plain program's by a relative error of at most 0.0071.
Values sent between devices are 32-bit elements; how exact they have to be, the bound alone decides.
No kernel may reach another device: no remote copies, remote signals or barrier semaphores. Data moves between devices by JAX's collectives and lax.ppermute only.
A program may use at most 128 MiB of HBM per device.

v0:
```python
import jax
import jax.numpy as jnp
from jax import lax
from jax.sharding import PartitionSpec as P

BLOCK = 512


EPS = 1e-06


def entering(value, axis, join, neutral, backward):
    count, mine = (lax.axis_size(axis), lax.axis_index(axis))
    pieces = jax.tree.map(lambda part: lax.all_gather(part, axis), value)
    if backward:
        pieces = jax.tree.map(lambda part: part[::-1], pieces)
        mine = count - 1 - mine
    total = jax.tree.map(
        lambda part, zero: jnp.full_like(part, 0) + jnp.asarray(zero, part.dtype), value, neutral
    )

    def turn(position, total):
        longer = join(total, jax.tree.map(lambda part: part[position], pieces))
        return jax.tree.map(lambda new, old: jnp.where(position < mine, new, old), longer, total)

    return lax.fori_loop(0, count - 1, turn, total)


def combine(earlier, later):
    return (earlier[0] * later[0], later[0][:, None, None] * earlier[1] + later[1])


def fold_step(carry_in, inputs):
    gain_now, total_now = carry_in
    passing, state_update = inputs
    return (
        (gain_now * passing, passing[:, None, None] * total_now + state_update),
        (gain_now, total_now),
    )


def forward_carry(element):
    identity = (jnp.ones_like(element[0]), jnp.zeros_like(element[1]))
    incoming = entering(element, ("seq", "ctx"), combine, identity, False)[1]
    return incoming


def backward_carry(element):
    identity = (jnp.ones_like(element[0]), jnp.zeros_like(element[1]))
    outgoing = entering(element, ("seq", "ctx"), combine, identity, True)[1]
    return outgoing


def block_parts(log_rates, starts):
    cumulative = jnp.cumsum(log_rates, axis=2)
    documents = jnp.cumsum(starts, axis=1)
    places = jnp.arange(log_rates.shape[2])
    causal = (documents[:, :, None] == documents[:, None, :]) & (places[:, None] >= places[None, :])
    spread = jnp.where(
        causal[:, None], cumulative[:, :, :, None] - cumulative[:, :, None, :], -1e30
    )
    weights = jnp.exp(spread)
    entering_state = jnp.where(documents[:, None, :] == 0, jnp.exp(cumulative), 0.0)
    leaving_state = jnp.where(
        documents[:, None, :] == documents[:, None, -1:],
        jnp.exp(cumulative[:, :, -1:] - cumulative),
        0.0,
    )
    passing = jnp.where(documents[:, None, -1] == 0, jnp.exp(cumulative[:, :, -1]), 0.0)
    return (
        weights,
        jnp.swapaxes(entering_state, 1, 2)[..., None],
        jnp.swapaxes(leaving_state, 1, 2)[..., None],
        passing,
    )


def local(query_in, key_in, value_in, log_decay, doc_start, out_grad):
    length = query_in.shape[0]
    head_count = log_decay.shape[0]
    head_size = query_in.shape[1] // head_count
    blocks = length // BLOCK

    def split(flat_rows):
        return flat_rows.reshape(blocks, BLOCK, head_count, head_size)

    query_block = split(query_in)
    key_block = split(key_in)
    value_block = split(value_in)
    grad_block = split(out_grad)
    log_rates = jnp.swapaxes(log_decay.reshape(head_count, blocks, BLOCK), 0, 1)
    starts = doc_start.reshape(blocks, BLOCK)
    weights, entering_state, leaving_state, passing = block_parts(log_rates, starts)
    decayed_keys = (key_block * leaving_state).astype(jnp.bfloat16)
    state_update = jnp.einsum(
        "nshk,nshv->nhkv", decayed_keys, value_block, preferred_element_type=jnp.float32
    )
    unit_gain = jnp.ones((head_count,), jnp.float32)
    zero_state = jnp.zeros((head_count, head_size, head_size), jnp.float32)
    (device_gain, device_total), (gains, totals) = lax.scan(
        fold_step, (unit_gain, zero_state), (passing, state_update)
    )
    incoming = forward_carry((device_gain, device_total))
    scores = (
        jnp.einsum("nthd,nshd->nhts", query_block, key_block, preferred_element_type=jnp.float32)
        * weights
    )
    attend_weights = scores.astype(jnp.bfloat16)
    inside = jnp.einsum(
        "nhts,nshd->nthd", attend_weights, value_block, preferred_element_type=jnp.float32
    )
    states = gains[:, :, None, None] * incoming[None] + totals
    state_reduced = states.astype(jnp.bfloat16)
    outside_mask = (
        jnp.einsum(
            "nthk,nhkv->nthv", query_block, state_reduced, preferred_element_type=jnp.float32
        )
        * entering_state
    )
    full_out = inside + outside_mask
    factor = lax.rsqrt(jnp.mean(full_out * full_out, axis=-1, keepdims=True) + EPS)
    normed = (full_out * factor).astype(jnp.bfloat16)
    grad_float = grad_block.astype(jnp.float32)
    gradient_precise = (
        factor * grad_float
        - factor
        * factor
        * factor
        * full_out
        * jnp.mean(grad_float * full_out, axis=-1, keepdims=True)
    ).astype(jnp.bfloat16)
    decayed_queries = (query_block * entering_state).astype(jnp.bfloat16)
    partial_state = jnp.einsum(
        "nthk,nthv->nhkv", decayed_queries, gradient_precise, preferred_element_type=jnp.float32
    )
    (back_gain, back_total), (grad_gains, grad_totals) = lax.scan(
        fold_step, (unit_gain, zero_state), (passing, partial_state), reverse=True
    )
    outgoing = backward_carry((back_gain, back_total))
    dscores = (
        jnp.einsum(
            "nthd,nshd->nhts", gradient_precise, value_block, preferred_element_type=jnp.float32
        )
        * weights
    )
    attend_gradient = dscores.astype(jnp.bfloat16)
    grad_q_in = jnp.einsum(
        "nhts,nshd->nthd", attend_gradient, key_block, preferred_element_type=jnp.float32
    )
    grad_k_in = jnp.einsum(
        "nhts,nthd->nshd", attend_gradient, query_block, preferred_element_type=jnp.float32
    )
    grad_v_in = jnp.einsum(
        "nhts,nthd->nshd", attend_weights, gradient_precise, preferred_element_type=jnp.float32
    )
    grad_states = grad_gains[:, :, None, None] * outgoing[None] + grad_totals
    gradient_reduced = grad_states.astype(jnp.bfloat16)
    query_gradient = (
        grad_q_in
        + jnp.einsum(
            "nthv,nhkv->nthk", gradient_precise, state_reduced, preferred_element_type=jnp.float32
        )
        * entering_state
    )
    key_gradient = (
        grad_k_in
        + jnp.einsum(
            "nshv,nhkv->nshk", value_block, gradient_reduced, preferred_element_type=jnp.float32
        )
        * leaving_state
    )
    value_gradient = (
        grad_v_in
        + jnp.einsum(
            "nshk,nhkv->nshv", key_block, gradient_reduced, preferred_element_type=jnp.float32
        )
        * leaving_state
    )
    width = head_count * head_size
    return (
        normed.reshape(length, width),
        query_gradient.astype(jnp.bfloat16).reshape(length, width),
        key_gradient.astype(jnp.bfloat16).reshape(length, width),
        value_gradient.astype(jnp.bfloat16).reshape(length, width),
    )


def solution(mesh):
    return jax.shard_map(
        local,
        mesh=mesh,
        in_specs=(
            P(("groups", "seq", "ctx"), "tensor"),
            P(("groups", "seq", "ctx"), "tensor"),
            P(("groups", "seq", "ctx"), "tensor"),
            P("tensor", ("groups", "seq", "ctx")),
            P(("groups", "seq", "ctx")),
            P(("groups", "seq", "ctx"), "tensor"),
        ),
        out_specs=(
            P(("groups", "seq", "ctx"), "tensor"),
            P(("groups", "seq", "ctx"), "tensor"),
            P(("groups", "seq", "ctx"), "tensor"),
            P(("groups", "seq", "ctx"), "tensor"),
        ),
        check_vma=False,
    )
```

profile of v0, /device:TPU:0, one launch (start us, length us, event | category | flops | bytes accessed | tf_op | source)
XLA Modules:
  0.0 260.5 jit_solution(11741760661423697429)
XLA Ops:
  7.2 0.0 all-gather.6.cloned.1.call-start
  7.2 0.9 reshape.562
  8.2 1.2 reduce-window.16
  9.3 0.2 slice_reduce_fusion
  9.5 1.0 reduce-window.14
  10.5 0.2 slice_reduce_fusion.1
  10.7 0.6 slice.27
  11.2 0.2 reduce-window.15
  11.4 0.1 broadcast.275
  11.5 0.6 slice.28
  13.4 0.1 broadcast_compare_fusion.1
  13.5 0.1 copy.128
  13.6 0.1 select_bitcast_fusion
  13.8 0.1 select_bitcast_fusion.1
  14.0 0.1 copy.130
  14.1 3.6 %copy.162 = bf16[64,8,16,128]{3,2,1,0:T(8,128)(2,1)} copy(bf16[64,8,16,128]{3,1,2,0:T(8,128)(2,1)} %bitcast.179) | data formatting | bytes 4194304
  17.6 4.3 %copy.129 = bf16[512,16,128]{0,2,1:T(8,128)(2,1)} copy(bf16[512,16,128]{2,1,0:T(8,128)(2,1)} %bitcast.178) | data formatting | bytes 4194304 | tf_op jit(solution)/shard_map/reshape.7
  21.9 3.4 %fusion.25 = f32[16,128,128]{2,1,0:T(8,128)} fusion(bf16[512,16,128]{0,2,1:T(8,128)(2,1)} %copy.129, f32[512,16]{0,1:T(8,128)S(1)} %copy.130, f32[16]{0:T(128)S(1)} %fusion.37, bf16[512,2048]{1,0:T(8,128)(2,1)S(1)} %copy-done), kind=kOutput, calls=%fused_computation.42 | convolution fusion | flops 271843328 | bytes 5275712 | tf_op jit(solution)/shard_map/nshk,nshv->nhkv/dot_general | solution.py:95
  25.3 0.0 all-gather.8.cloned.1.call-start
  25.4 0.1 copy.134
  25.5 0.1 copy.157
  25.6 3.9 %copy.158 = bf16[512,2048]{0,1:T(8,128)(2,1)} copy(bf16[512,2048]{1,0:T(8,128)(2,1)} %param.10) | data formatting | bytes 4194304 | tf_op jit(solution)/shard_map/reshape.6
  29.5 4.1 %copy.135 = f32[512,2048]{0,1:T(8,128)} copy(bf16[512,2048]{1,0:T(8,128)(2,1)} %param.15) | data formatting | bytes 6291456 | tf_op jit(solution)/shard_map/convert_element_type | solution.py:123
  33.7 13.7 %all-gather = f32[8,16,1]{1,2,0:T(1,128)S(1)} all-gather(f32[1,16,1]{1,2,0:T(1,128)S(1)} %get-tuple-element.321), channel_id=2, replica_groups=mesh['groups'=2,'seq'=4,'tensor'=2,'ctx'=2] {'seq','ctx'}, dimensions={0}, use_global_device_ids=true | all-gather | bytes 576 | tf_op jit(solution)/shard_map/all_gather | solution.py:14
  47.4 0.2 fusion.32
  47.6 7.0 %multiply_convert_fusion.1 = bf16[16,512,512]{2,1,0:T(8,128)(2,1)S(1)} fusion(bf16[512,16,128]{0,2,1:T(8,128)(2,1)} %bitcast.173, f32[16,512]{1,0:T(8,128)S(1)} %bitcast_add_fusion.3, pred[512,512]{1,0:T(8,128)(4,1)S(1)} %fusion.32, bf16[512,2048]{1,0:T(8,128)(2,1)} %param.11), kind=kOutput, calls=%fused_computation.7 | convolution fusion | flops 1090519040 | bytes 12877824 | tf_op jit(solution)/shard_map/nthd,nshd->nhts/dot_general | solution.py:105
  54.6 3.2 %copy-done.1 = bf16[16,512,512]{2,1,0:T(8,128)(2,1)} copy-done((bf16[16,512,512]{2,1,0:T(8,128)(2,1)}, bf16[16,512,512]{2,1,0:T(8,128)(2,1)S(1)}, u32[]{:S(2)}) %copy-start.1) | copy-done | bytes 8388632
  57.8 4.8 %fusion.12 = f32[16,512,128]{1,2,0:T(8,128)} fusion(bf16[16,512,512]{2,1,0:T(8,128)(2,1)S(1)} %multiply_convert_fusion.1, bf16[512,2048]{1,0:T(8,128)(2,1)S(1)} %copy-done), kind=kOutput, calls=%fused_computation.29 | convolution fusion | flops 1073741824 | bytes 14680064 | tf_op jit(solution)/shard_map/nhts,nshd->nthd/dot_general | solution.py:109
  62.7 47.6 %all-gather.6.cloned.1.call-done = f32[128,128,128]{2,1,0:T(8,128)} async-done(((f32[16,128,128]{2,1,0:T(8,128)}), f32[128,128,128]{2,1,0:T(8,128)}) %all-gather.6.cloned.1.call-update) | async-done | bytes 8388624 | tf_op jit(solution)/shard_map/all_gather | solution.py:14
  110.2 10.5 %while.18 = (s32[]{:T(128)}, f32[16,128,128]{2,1,0:T(8,128)S(1)}, s32[]{:T(128)}, f32[8,16]{1,0:T(8,128)S(1)}, f32[8,16,128,128]{3,2,1,0:T(8,128)}, /*index=5*/s32[]{:T(128)}, s32[]{:T(128)}) while((s32[]{:T(128)}, f32[16,128,128]{2,1,0:T(8,128)S(1)}, s32[]{:T(128)}, f32[8,16]{1,0:T(8,128)S(1)}, f32[8,16,128,128]{3,2,1,0:T(8,128)}, ...), condition=%wide.region_5.6_spmd.clone, body=%wide.region_4.5_spmd.clone.sunk | while | flops 1048580 | bytes 3146033 | solution.py:26
  110.2 1.5 fusion.60
  111.7 1.5 fusion.60
  113.2 1.5 fusion.60
  114.7 1.5 fusion.60
  116.2 1.5 fusion.60
  117.7 1.5 fusion.60
  119.2 1.5 fusion.60
  120.7 5.7 %multiply_reduce_fusion = (f32[512,16]{0,1:T(8,128)S(1)}, f32[512,16]{0,1:T(8,128)S(1)}, f32[1,512,16,128]{1,3,2,0:T(8,128)S(1)}) fusion(f32[1,512,16,128]{1,3,2,0:T(8,128)} %bitcast.172, f32[512,16]{0,1:T(8,128)S(1)} %copy.134, bf16[512,16,128]{0,2,1:T(8,128)(2,1)} %bitcast.174, f32[16,128,128]{2,1,0:T(8,128)S(1)} %get-tuple-element.234, ...), kind=kOutput, calls=%fused_computation.22 | convolution fusion | flops 274972672 | bytes 15826944 | tf_op jit(solution)/shard_map/nthk,nhkv->nthv/dot_general | solution.py:115
  126.5 3.0 %fusion.10 = (bf16[512,16,128]{0,2,1:T(8,128)(2,1)S(1)}, bf16[1,512,16,128]{1,3,2,0:T(8,128)(2,1)}) fusion(f32[1,512,16,128]{1,3,2,0:T(8,128)S(1)} %get-tuple-element.324, f32[512,16]{0,1:T(8,128)S(1)} %get-tuple-element.325, f32[512,16]{0,1:T(8,128)S(1)} %get-tuple-element.322, f32[512,16]{0,1:T(8,128)S(1)} %get-tuple-element.323, f32[512,2048]{0,1:T(8,128)S(1)} %copy-done.4), kind=kLoop, calls=%fused_computation.27 | loop fusion | flops 7340032 | bytes 12681216 | tf_op jit(solution)/shard_map/reshape.60
  129.5 1.3 copy-done.7
  130.8 1.7 fusion.24
  132.6 3.9 %copy.148 = bf16[512,2048]{1,0:T(8,128)(2,1)} copy(bf16[512,2048]{0,1:T(8,128)(2,1)} %bitcast.180) | data formatting | bytes 4194304
  136.5 6.7 %multiply_convert_fusion = bf16[16,512,512]{2,1,0:T(8,128)(2,1)S(1)} fusion(bf16[512,16,128]{0,2,1:T(8,128)(2,1)} %copy-done.7, f32[16,512]{1,0:T(8,128)S(1)} %copy-done.12, pred[512,512]{1,0:T(8,128)(4,1)S(1)} %fusion.32, bf16[512,2048]{1,0:T(8,128)(2,1)S(1)} %copy-done), kind=kOutput, calls=%fused_computation.6 | convolution fusion | flops 1090519040 | bytes 12877824 | tf_op jit(solution)/shard_map/nthd,nshd->nhts/dot_general | solution.py:141
  143.3 8.1 %fusion.38 = f32[16,512,128]{1,2,0:T(8,128)} fusion(bf16[16,512,512]{2,1,0:T(8,128)(2,1)S(1)} %multiply_convert_fusion, bf16[512,16,128]{0,2,1:T(8,128)(2,1)} %copy.129), kind=kOutput, calls=%fused_computation.71 | convolution fusion | flops 1073741824 | bytes 14680064 | tf_op jit(solution)/shard_map/nhts,nshd->nthd/dot_general | solution.py:147
  151.4 4.4 %fusion.7 = bf16[1,512,16,128]{1,3,2,0:T(8,128)(2,1)} fusion(f32[16,512,128]{1,2,0:T(8,128)} %fusion.38, bf16[512,16,128]{0,2,1:T(8,128)(2,1)S(1)} %copy-done.8, f32[512,16]{0,1:T(8,128)S(1)} %copy.134, f32[16,128,128]{2,1,0:T(8,128)S(1)} %copy-done.3), kind=kOutput, calls=%fused_computation.17 | convolution fusion | flops 271843328 | bytes 9469952 | tf_op jit(solution)/shard_map/nthv,nhkv->nthk/dot_general | solution.py:160
  155.8 4.0 %copy.149 = bf16[512,2048]{1,0:T(8,128)(2,1)} copy(bf16[512,2048]{0,1:T(8,128)(2,1)} %bitcast.181) | data formatting | bytes 4194304
  159.7 7.3 %fusion.39 = f32[16,128,512]{2,1,0:T(8,128)} fusion(bf16[512,16,128]{0,2,1:T(8,128)(2,1)} %copy-done.7, bf16[16,512,512]{2,1,0:T(8,128)(2,1)} %copy-done.1), kind=kOutput, calls=%fused_computation.72 | convolution fusion | flops 1073741824 | bytes 14680064 | tf_op jit(solution)/shard_map/nhts,nthd->nshd/dot_general | solution.py:153
  167.1 46.2 %all-gather.8.cloned.1.call-done = f32[128,128,128]{2,1,0:T(8,128)} async-done(((f32[16,128,128]{2,1,0:T(8,128)}), f32[128,128,128]{2,1,0:T(8,128)}) %all-gather.8.cloned.1.call-update) | async-done | bytes 8388624 | tf_op jit(solution)/shard_map/all_gather | solution.py:14
  213.3 7.7 %rev.7 = f32[8,16,128,128]{3,2,1,0:T(8,128)} reverse(f32[8,16,128,128]{3,2,1,0:T(8,128)} %bitcast.177), dimensions={0} | reverse | bytes 16777216 | tf_op jit(solution)/shard_map/rev | solution.py:16
  221.0 10.5 %while.19 = (s32[]{:T(128)}, f32[16,128,128]{2,1,0:T(8,128)S(1)}, s32[]{:T(128)}, f32[8,16]{1,0:T(8,128)S(1)}, f32[8,16,128,128]{3,2,1,0:T(8,128)}, /*index=5*/s32[]{:T(128)}, s32[]{:T(128)}) while((s32[]{:T(128)}, f32[16,128,128]{2,1,0:T(8,128)S(1)}, s32[]{:T(128)}, f32[8,16]{1,0:T(8,128)S(1)}, f32[8,16,128,128]{3,2,1,0:T(8,128)}, ...), condition=%wide.region_9.10_spmd.clone, body=%wide.region_8.9_spmd.clone.sunk | while | flops 1048580 | bytes 3146033 | solution.py:26
  221.0 1.5 fusion.61
  222.5 1.5 fusion.61
  224.0 1.5 fusion.61
  225.5 1.5 fusion.61
  227.0 1.5 fusion.61
  228.5 1.5 fusion.61
  230.0 1.5 fusion.61
  231.5 2.9 %fusion.14 = f32[16,128,512]{2,1,0:T(8,128)} fusion(f32[16,128,128]{2,1,0:T(8,128)S(1)} %get-tuple-element.235, bf16[512,2048]{1,0:T(8,128)(2,1)S(1)} %copy-done), kind=kOutput, calls=%fused_computation.31 | convolution fusion | flops 268697600 | bytes 7340032 | tf_op jit(solution)/shard_map/nshv,nhkv->nshk/dot_general | solution.py:167
  234.3 0.6 copy-done.6
  234.9 0.9 copy-done.10
  235.8 2.3 fusion.3
  238.1 3.9 %copy.151 = bf16[512,2048]{1,0:T(8,128)(2,1)} copy(bf16[512,2048]{0,1:T(8,128)(2,1)} %bitcast.182) | data formatting | bytes 4194304
  242.0 7.8 %fusion.5 = bf16[1,512,16,128]{1,3,2,0:T(8,128)(2,1)} fusion(f32[16,128,512]{2,1,0:T(8,128)} %fusion.14, bf16[512,16,128]{0,2,1:T(8,128)(2,1)} %bitcast.175, bf16[16,512,512]{2,1,0:T(8,128)(2,1)} %copy-done.5, f32[512,16]{0,1:T(8,128)S(1)} %copy.130), kind=kOutput, calls=%fused_computation.14 | convolution fusion | flops 1076887552 | bytes 16809984 | tf_op jit(solution)/shard_map/nhts,nthd->nshd/dot_general | solution.py:150
  249.8 3.9 %copy.150 = bf16[512,2048]{1,0:T(8,128)(2,1)} copy(bf16[512,2048]{0,1:T(8,128)(2,1)} %bitcast.183) | data formatting | bytes 4194304
  (53 shorter events, 0.4 us)
Async XLA Ops:
  7.2 14.7 %copy-start = (bf16[512,2048]{1,0:T(8,128)(2,1)S(1)}, bf16[512,2048]{1,0:T(8,128)(2,1)}, u32[]{:S(2)}) copy-start(bf16[512,2048]{1,0:T(8,128)(2,1)} %param.12) | copy-start | bytes 6291460
  7.2 103.1 %all-gather.6.cloned.1.call-start = ((), (), s32[]{:S(2)}) async-start(), calls=%async_computation | async-start | bytes 9437184 | tf_op jit(solution)/shard_map/all_gather | solution.py:14
  25.3 188.0 %all-gather.8.cloned.1.call-start = ((), (), s32[]{:S(2)}) async-start(), calls=%async_computation.1 | async-start | bytes 9437184 | tf_op jit(solution)/shard_map/all_gather | solution.py:14
  47.4 7.2 %copy-start.11 = (f32[16,512]{1,0:T(8,128)}, f32[16,512]{1,0:T(8,128)S(1)}, u32[]{:S(2)}) copy-start(f32[16,512]{1,0:T(8,128)S(1)} %bitcast_add_fusion.3) | copy-start | bytes 98308
  54.6 3.2 %copy-start.1 = (bf16[16,512,512]{2,1,0:T(8,128)(2,1)}, bf16[16,512,512]{2,1,0:T(8,128)(2,1)S(1)}, u32[]{:S(2)}) copy-start(bf16[16,512,512]{2,1,0:T(8,128)(2,1)S(1)} %multiply_convert_fusion.1) | copy-start | bytes 25165828
  120.7 5.7 %copy-start.2 = (f32[16,128,128]{2,1,0:T(8,128)}, f32[16,128,128]{2,1,0:T(8,128)S(1)}, u32[]{:S(2)}) copy-start(f32[16,128,128]{2,1,0:T(8,128)S(1)} %get-tuple-element.234) | copy-start | bytes 3145732
  120.7 5.7 %copy-start.4 = (f32[512,2048]{0,1:T(8,128)S(1)}, f32[512,2048]{0,1:T(8,128)}, u32[]{:S(2)}) copy-start(f32[512,2048]{0,1:T(8,128)} %copy.135) | copy-start | bytes 12582916
  126.5 4.3 %copy-start.9 = (bf16[512,2048]{0,1:T(8,128)(2,1)S(1)}, bf16[512,2048]{0,1:T(8,128)(2,1)}, u32[]{:S(2)}) copy-start(bf16[512,2048]{0,1:T(8,128)(2,1)} %copy.158) | copy-start | bytes 6291460
  129.5 1.3 copy-start.7
  132.6 3.9 %copy-start.12 = (f32[16,512]{1,0:T(8,128)S(1)}, f32[16,512]{1,0:T(8,128)}, u32[]{:S(2)}) copy-start(f32[16,512]{1,0:T(8,128)} %copy-done.11) | copy-start | bytes 98308
  143.2 8.1 %copy-start.5 = (bf16[16,512,512]{2,1,0:T(8,128)(2,1)}, bf16[16,512,512]{2,1,0:T(8,128)(2,1)S(1)}, u32[]{:S(2)}) copy-start(bf16[16,512,512]{2,1,0:T(8,128)(2,1)S(1)} %multiply_convert_fusion) | copy-start | bytes 25165828
  143.2 8.1 %copy-start.3 = (f32[16,128,128]{2,1,0:T(8,128)S(1)}, f32[16,128,128]{2,1,0:T(8,128)}, u32[]{:S(2)}) copy-start(f32[16,128,128]{2,1,0:T(8,128)} %copy-done.2) | copy-start | bytes 3145732
  143.3 8.1 %copy-start.8 = (bf16[512,16,128]{0,2,1:T(8,128)(2,1)S(1)}, bf16[512,16,128]{0,2,1:T(8,128)(2,1)}, u32[]{:S(2)}) copy-start(bf16[512,16,128]{0,2,1:T(8,128)(2,1)} %copy-done.7) | copy-start | bytes 6291460
  231.5 3.4 %copy-start.6 = (f32[16,128,512]{2,1,0:T(8,128)S(1)}, f32[16,128,512]{2,1,0:T(8,128)}, u32[]{:S(2)}) copy-start(f32[16,128,512]{2,1,0:T(8,128)} %fusion.39) | copy-start | bytes 12582916
  231.5 4.4 %copy-start.10 = (bf16[512,2048]{1,0:T(8,128)(2,1)S(1)}, bf16[512,2048]{1,0:T(8,128)(2,1)}, u32[]{:S(2)}) copy-start(bf16[512,2048]{1,0:T(8,128)(2,1)} %param.11) | copy-start | bytes 6291460
Sparse Core Ops, SparseCore 0:
  25.4 84.7 all-gather.5
  132.7 80.5 all-gather.7
where the time goes:
time: 262 us; the launch traced here: 261 us
  waiting for transfers between devices  93.8 us (36%)
  matrix products  62.1 us (24%)
  local copies, waits for them, and re-layouts  48.5 us (19%)
  other arithmetic  26.4 us (10%)
  between operations  15.6 us (6%)
  blocking collectives  13.7 us (5%)
    all_gather x2, waiting for transfers between devices, entering(): pieces = jax.tree.map(lambda part: lax.all_gather(part, axis), value)  93.8 us
    unnamed x31, local copies, waits for them, and re-layouts  25.4 us
    select_n x14, other arithmetic, turn(): jnp.where(position < mine, new, old)  20.4 us
    all_gather x1, blocking collectives, entering(): pieces = jax.tree.map(lambda part: lax.all_gather(part, axis), value)  13.7 us
    another operation x13, local copies, waits for them, and re-layouts  9.63 us
    dot_general x1, matrix products, local(): jnp.einsum('nhts,nshd->nthd', attend_gradient, key_block, preferred_eleme...  8.1 us
    dot_general x1, matrix products, local(): jnp.einsum('nhts,nthd->nshd', attend_gradient, query_block, preferred_ele...  7.78 us
    rev x2, local copies, waits for them, and re-layouts, entering(): pieces = jax.tree.map(lambda part: part[::-1], pieces)  7.72 us
  transfers between devices with their start and end apart: 2, of which 2 were waited for; matrix products, arithmetic and copies ran while one was open for 21% of the time, Pallas kernels for 0%

commit v1 on v0

v1 whole, which is shorter than its diff:
```python
import functools

import jax
import jax.numpy as jnp
from jax import lax
from jax.experimental import pallas as pl
from jax.experimental.pallas import tpu as pltpu
from jax.sharding import PartitionSpec as P

C = 128
EPS = 1e-06
NEG = -1e30
GROUPS = 2
F32 = jnp.float32
BF16 = jnp.bfloat16
VMEM_LIMIT = 48 * 1024 * 1024


def dot(a, b):
    return lax.dot_general(a, b, (((1,), (0,)), ((), ())), preferred_element_type=F32)


def dot_t(a, b):
    return lax.dot_general(a, b, (((1,), (1,)), ((), ())), preferred_element_type=F32)


def t_dot(a, b):
    return lax.dot_general(a, b, (((0,), (0,)), ((), ())), preferred_element_type=F32)


def exact_dot(a, b):
    return lax.dot_general(
        a, b, (((1,), (0,)), ((), ())), precision=lax.Precision.HIGHEST, preferred_element_type=F32
    )


def columns(row):
    return jnp.broadcast_to(row, (C, C)).T


def prepare_kernel(chunks, decay_ref, start_ref, run_ref, table_ref, gain_ref, weight_bias_ref, enter_bias_ref, leave_bias_ref):
    heads = decay_ref.shape[0]
    at_row = lax.broadcasted_iota(jnp.int32, (C, C), 0)
    at_lane = lax.broadcasted_iota(jnp.int32, (C, C), 1)
    upper = jnp.where(at_row <= at_lane, 1.0, 0.0).astype(F32)
    ones = jnp.ones((C, C), F32)
    gain = jnp.ones((heads, C), F32)
    for j in range(chunks):
        span = pl.ds(j * C, C)
        decay = decay_ref[:, span]
        run = exact_dot(decay, upper)
        last = exact_dot(decay, ones)
        starts = jnp.broadcast_to(start_ref[:, span].astype(F32), (8, C))
        docs = exact_dot(starts, upper)[:1]
        docs_last = exact_dot(starts, ones)[:1]
        passing = jnp.where(docs_last == 0.0, jnp.exp(last), 0.0)
        gain = gain * passing
        run_ref[:, 0, span] = run
        table_ref[:, j, :] = passing
        table_ref[:, chunks + j, :] = last
        docs_column = columns(docs)
        weight_bias_ref[span, :] = jnp.where((docs_column == docs) & (at_lane <= at_row), 0.0, NEG)
        enter_bias_ref[span, :] = jnp.where(docs_column == 0.0, 0.0, NEG)
        leave_bias_ref[span, :] = jnp.where(docs_column == docs_last, 0.0, NEG)
    gain_ref[...] = gain


def state_kernel(chunks, quarter, core_ref, k_ref, v_ref, run_ref, table_ref, leave_bias_ref, prefix_ref, mine_ref, other_ref):
    p = pl.program_id(0)
    total = None
    for j in range(chunks):
        span = pl.ds(j * C, C)
        run = columns(run_ref[0, :, span])
        leave = jnp.exp(table_ref[0, chunks + j : chunks + j + 1, :] - run + leave_bias_ref[span, :])
        kd = (k_ref[span, :].astype(F32) * leave).astype(BF16)
        update = t_dot(kd, v_ref[span, :])
        total = update if total is None else table_ref[0, j : j + 1, :] * total + update
        if j < chunks - 1:
            prefix_ref[0, j] = total

    @pl.when(p < quarter)
    def _():
        mine_ref[0] = total

    @pl.when(p >= quarter)
    def _():
        other_ref[0] = total


def forward_kernel(
    chunks, quarter, core_ref, q_ref, k_ref, v_ref, og_ref, run_ref, table_ref, weight_bias_ref, enter_bias_ref,
    prefix_ref, keep_ref, back_ref, *rest
):
    normed_ref, grad_ref, suffix_ref, mine_ref, other_ref = rest[-5:]
    p = pl.program_id(0)
    incoming = jnp.where(p < quarter, keep_ref[0], back_ref[0])
    gain = None
    parts = []
    for j in range(chunks):
        span = pl.ds(j * C, C)
        row = run_ref[0, :, span]
        run = columns(row)
        weights = jnp.exp(run - row + weight_bias_ref[span, :])
        enter = jnp.exp(run + enter_bias_ref[span, :])
        q, k, v = q_ref[span, :], k_ref[span, :], v_ref[span, :]
        attend = (dot_t(q, k) * weights).astype(BF16)
        state = incoming if j == 0 else gain * incoming + prefix_ref[0, j - 1]
        passing = table_ref[0, j : j + 1, :]
        gain = passing if gain is None else gain * passing
        out = dot(attend, v) + enter * dot(q, state.astype(BF16))
        factor = lax.rsqrt(jnp.mean(out * out, axis=-1, keepdims=True) + EPS)
        normed = out * factor
        normed_ref[span, :] = normed.astype(BF16)
        og = og_ref[span, :].astype(F32)
        along = jnp.mean(og * out, axis=-1, keepdims=True)
        grad = (factor * og - (factor * factor * factor * along) * out).astype(BF16)
        grad_ref[span, :] = grad
        qd = (q.astype(F32) * enter).astype(BF16)
        parts.append(t_dot(qd, grad))
    total = parts[-1]
    for j in range(chunks - 2, -1, -1):
        suffix_ref[0, j] = total
        total = table_ref[0, j : j + 1, :] * total + parts[j]

    @pl.when(p < quarter)
    def _():
        mine_ref[0] = total

    @pl.when(p >= quarter)
    def _():
        other_ref[0] = total


def backward_kernel(
    chunks, quarter, core_ref, q_ref, k_ref, v_ref, g_ref, run_ref, table_ref, weight_bias_ref, enter_bias_ref,
    leave_bias_ref, prefix_ref, suffix_ref, keep_ref, back_ref, gkeep_ref, gback_ref, *rest
):
    dq_ref, dk_ref, dv_ref = rest[-3:]
    p = pl.program_id(0)
    incoming = jnp.where(p < quarter, keep_ref[0], back_ref[0])
    outgoing = jnp.where(p < quarter, gkeep_ref[0], gback_ref[0])
    states = []
    gain = None
    for j in range(chunks):
        states.append((incoming if j == 0 else gain * incoming + prefix_ref[0, j - 1]).astype(BF16))
        passing = table_ref[0, j : j + 1, :]
        gain = passing if gain is None else gain * passing
    gain = None
    for j in range(chunks - 1, -1, -1):
        span = pl.ds(j * C, C)
        row = run_ref[0, :, span]
        run = columns(row)
        weights = jnp.exp(run - row + weight_bias_ref[span, :])
        enter = jnp.exp(run + enter_bias_ref[span, :])
        leave = jnp.exp(table_ref[0, chunks + j : chunks + j + 1, :] - run + leave_bias_ref[span, :])
        q, k, v, g = q_ref[span, :], k_ref[span, :], v_ref[span, :], g_ref[span, :]
        attend = (dot_t(q, k) * weights).astype(BF16)
        dattend = (dot_t(g, v) * weights).astype(BF16)
        gstate = outgoing if j == chunks - 1 else gain * outgoing + suffix_ref[0, j]
        passing = table_ref[0, j : j + 1, :]
        gain = passing if gain is None else gain * passing
        gstate = gstate.astype(BF16)
        dq = dot(dattend, k) + enter * dot_t(g, states[j])
        dk = t_dot(dattend, q) + leave * dot_t(v, gstate)
        dv = t_dot(attend, g) + leave * dot(k, gstate)
        dq_ref[span, :] = dq.astype(BF16)
        dk_ref[span, :] = dk.astype(BF16)
        dv_ref[span, :] = dv.astype(BF16)


def local(query_in, key_in, value_in, log_decay, doc_start, out_grad):
    length, width = query_in.shape
    heads = log_decay.shape[0]
    dh = width // heads
    chunks = length // C
    groups = GROUPS
    size = heads // groups
    quarter = size // 2
    shards = lax.axis_size("seq")
    core = lax.axis_index("ctx")
    first = core == 0
    core_arg = core.astype(jnp.int32).reshape(1)
    swap = [(0, 1), (1, 0)]
    shape = jax.ShapeDtypeStruct

    run, table, gain, weight_bias, enter_bias, leave_bias = pl.pallas_call(
        functools.partial(prepare_kernel, chunks),
        out_shape=(
            shape((heads, 1, length), F32),
            shape((heads, 2 * chunks, C), F32),
            shape((heads, C), F32),
            shape((length, C), F32),
            shape((length, C), F32),
            shape((length, C), F32),
        ),
        name="prepare",
    )(log_decay, doc_start.reshape(1, length))
    gain_other = lax.ppermute(gain, "ctx", swap)
    gain0 = jnp.where(first, gain, gain_other)
    gain1 = jnp.where(first, gain_other, gain)

    def specs(group):
        def head(p, core_ref):
            return group * size + lax.rem(p + core_ref[0] * quarter, size)

        return dict(
            rows=pl.BlockSpec((length, dh), lambda p, c: (0, head(p, c))),
            run=pl.BlockSpec((1, 1, length), lambda p, c: (head(p, c), 0, 0)),
            table=pl.BlockSpec((1, 2 * chunks, C), lambda p, c: (head(p, c), 0, 0)),
            bias=pl.BlockSpec((length, C), lambda p, c: (0, 0)),
            states=pl.BlockSpec((1, chunks - 1, dh, dh), lambda p, c: (p, 0, 0, 0)),
            mine=pl.BlockSpec((1, dh, dh), lambda p, c: (jnp.minimum(p, quarter - 1), 0, 0)),
            other=pl.BlockSpec((1, dh, dh), lambda p, c: (jnp.maximum(p - quarter, 0), 0, 0)),
            any=pl.BlockSpec(memory_space=pl.ANY),
        )

    states_shape = shape((size, chunks - 1, dh, dh), F32)
    part_shape = shape((quarter, dh, dh), F32)
    rows_shape = shape((length, width), BF16)

    def call(kernel, group, in_names, out_names, out_shapes, args, name, products, reads, aliases=()):
        table = specs(group)
        extra = [a for a in aliases if a is not None]
        return pl.pallas_call(
            functools.partial(kernel, chunks, quarter),
            grid_spec=pltpu.PrefetchScalarGridSpec(
                num_scalar_prefetch=1,
                grid=(size,),
                in_specs=[table[n] for n in in_names] + [table["any"]] * len(extra),
                out_specs=[table[n] for n in out_names],
            ),
            out_shape=out_shapes,
            input_output_aliases={1 + len(in_names) + i: i for i in range(len(extra))},
            compiler_params=pltpu.CompilerParams(
                dimension_semantics=("arbitrary",), vmem_limit_bytes=VMEM_LIMIT
            ),
            cost_estimate=pl.CostEstimate(
                flops=products * size * 2 * length * C * dh,
                bytes_accessed=reads * size * length * dh * 2,
                transcendentals=size * length * C,
            ),
            name=name,
        )(core_arg, *args, *extra)

    def pick(array, group):
        start = group * size + core * quarter
        return lax.dynamic_slice_in_dim(array, start, quarter, 0)[:, None, :]

    def carry(group, mine, other, backward):
        g0, g1 = pick(gain0, group), pick(gain1, group)
        got = lax.ppermute(other, "ctx", swap)
        zero = jnp.where(first, mine, got)
        one = jnp.where(first, got, mine)
        both = g0 * g1
        if backward:
            total = g0 * one + zero
            order = [(k, k - 1) for k in range(shards - 1, 0, -1)]
        else:
            total = g1 * zero + one
            order = [(k, k + 1) for k in range(shards - 1)]
        state = None
        for hop in order:
            sent = total if state is None else both * state + total
            landed = lax.ppermute(sent, "seq", [hop])
            state = landed if state is None else state + landed
        if backward:
            inner = g1 * state + one
            keep, send = jnp.where(first, inner, state), jnp.where(first, state, inner)
        else:
            inner = g0 * state + zero
            keep, send = jnp.where(first, state, inner), jnp.where(first, inner, state)
        return keep, lax.ppermute(send, "ctx", swap)

    prefixes, updates = [], []
    for group in range(groups):
        prefix, mine, other = call(
            state_kernel, group,
            ["rows", "rows", "run", "table", "bias"],
            ["states", "mine", "other"],
            (states_shape, part_shape, part_shape),
            (key_in, value_in, run, table, leave_bias),
            "state", 1, 4,
        )
        prefixes.append(prefix)
        updates.append((mine, other))
    incoming = [carry(group, *updates[group], False) for group in range(groups)]

    normed = grad = None
    suffixes, outgoing = [], []
    for group in range(groups):
        normed, grad_new, suffix, mine, other = call(
            forward_kernel, group,
            ["rows"] * 4 + ["run", "table", "bias", "bias", "states", "mine", "other"],
            ["rows", "rows", "states", "mine", "other"],
            (rows_shape, rows_shape, states_shape, part_shape, part_shape),
            (query_in, key_in, value_in, out_grad, run, table, weight_bias, enter_bias, prefixes[group], *incoming[group]),
            "forward", 4, 8,
            aliases=(normed,),
        )
        grad = grad_new
        suffixes.append((grad, suffix))
        outgoing.append(carry(group, mine, other, True))

    grads = (None, None, None)
    for group in range(groups):
        grad, suffix = suffixes[group]
        grads = call(
            backward_kernel, group,
            ["rows"] * 4 + ["run", "table", "bias", "bias", "bias", "states", "states", "mine", "other", "mine", "other"],
            ["rows", "rows", "rows"],
            (rows_shape, rows_shape, rows_shape),
            (
                query_in, key_in, value_in, grad, run, table, weight_bias, enter_bias, leave_bias,
                prefixes[group], suffix, *incoming[group], *outgoing[group],
            ),
            "backward", 8, 10,
            aliases=grads,
        )
    return (normed, *grads)


def solution(mesh):
    rows = P(("groups", "seq", "ctx"), "tensor")
    return jax.shard_map(
        local,
        mesh=mesh,
        in_specs=(rows, rows, rows, P("tensor", ("groups", "seq", "ctx")), P(("groups", "seq", "ctx")), rows),
        out_specs=(rows, rows, rows, rows),
        check_vma=False,
    )
```

time: 262 us -> 142 us (0.54)
  Pallas kernels: 0 us -> 66.1 us
  matrix products: 62.1 us -> 0 us
  waiting for transfers between devices: 93.8 us -> 48.4 us
  local copies, waits for them, and re-layouts: 48.5 us -> 4.89 us
  other arithmetic: 26.4 us -> 2.81 us
  starting transfers between devices: 0.08 us -> 17.6 us
  between operations: 15.6 us -> 0.97 us
  blocking collectives: 13.7 us -> 0 us
    all_gather x2 -> x0, waiting for transfers between devices: 93.8 us -> none  [entering(): pieces = jax.tree.map(lambda part: lax.all_gather(part, axis), value)]
    pallas_call x0 -> x7, Pallas kernels: none -> 66.1 us  [the longest x6 63.5 us: call(): pl.pallas_call(functools.partial(kernel, chunks, quarter), grid_spec=pltp...]
    dot_general x12 -> x0, matrix products: 62.1 us -> none  [the longest x1 8.1 us: local(): jnp.einsum('nhts,nshd->nthd', attend_gradient, key_block, preferred_eleme...]
    ppermute x0 -> x21, waiting for transfers between devices: none -> 48.4 us  [the longest x12 47.7 us: carry(): landed = lax.ppermute(sent, 'seq', [hop])]
    unnamed x31 -> x24, local copies, waits for them, and re-layouts: 25.4 us -> 4.89 us
    select_n x14 -> x5, other arithmetic: 20.4 us -> 0.28 us  [the longest x2 0.15 us: carry(): jnp.where(first, inner, state)]
    ppermute x0 -> x21, starting transfers between devices: none -> 17.6 us  [the longest x12 14.2 us: carry(): landed = lax.ppermute(sent, 'seq', [hop])]
    all_gather x1 -> x0, blocking collectives: 13.7 us -> none  [entering(): pieces = jax.tree.map(lambda part: lax.all_gather(part, axis), value)]
  transfers between devices with their start and end apart: 2 -> 21, of which waited for: 2 -> 5; matrix products, arithmetic and copies ran while one was open for 21% -> 2% of each run, Pallas kernels for 0% -> 37%
where the time goes in v1:
time: 142 us; the launch traced here: 141 us
  Pallas kernels  66.1 us (47%)
  waiting for transfers between devices  48.4 us (34%)
  starting transfers between devices  17.6 us (12%)
  local copies, waits for them, and re-layouts  4.89 us (3%)
  other arithmetic  2.81 us (2%)
    pallas_call x6, Pallas kernels, call(): pl.pallas_call(functools.partial(kernel, chunks, quarter), grid_spec=pltp...  63.5 us
    ppermute x12, waiting for transfers between devices, carry(): landed = lax.ppermute(sent, 'seq', [hop])  47.7 us
    ppermute x12, starting transfers between devices, carry(): landed = lax.ppermute(sent, 'seq', [hop])  14.2 us
    unnamed x24, local copies, waits for them, and re-layouts  4.89 us
  transfers between devices with their start and end apart: 21, of which 5 were waited for; matrix products, arithmetic and copies ran while one was open for 2% of the time, Pallas kernels for 37%

profile of v1, /device:TPU:0, one launch (start us, length us, event | category | flops | bytes accessed | tf_op | source)
XLA Modules:
  0.0 140.7 jit_solution(1725916857881143406)
XLA Ops:
  0.6 2.5 %prepare.1 = (f32[16,1,512]{2,1,0:T(1,128)}, f32[16,8,128]{2,1,0:T(8,128)}, f32[16,128]{1,0:T(8,128)}, f32[512,128]{1,0:T(8,128)}, f32[512,128]{1,0:T(8,128)}, /*index=5*/f32[512,128]{1,0:T(8,128)}) custom-call(f32[16,512]{1,0:T(8,128)} %decay_ref.1, s32[1,512]{1,0:T(1,128)} %bitcast.2), custom_call_target="tpu_custom_call" | custom-call | tf_op jit(solution)/shard_map/prepare/pallas_call | solution.py:186
  3.2 0.5 collective-permute-start
  3.6 1.6 %copy-done = bf16[512,2048]{1,0:T(8,128)(2,1)S(1)} copy-done((bf16[512,2048]{1,0:T(8,128)(2,1)S(1)}, bf16[512,2048]{1,0:T(8,128)(2,1)}, u32[]{:S(2)}) %copy-start) | copy-done | bytes 2097176
  5.2 0.9 copy-done.3
  6.2 0.8 copy-done.5
  7.0 0.8 copy-done.7
  7.8 6.4 %state.3 = (f32[8,3,128,128]{3,2,1,0:T(8,128)S(1)}, f32[4,128,128]{2,1,0:T(8,128)S(1)}, f32[4,128,128]{2,1,0:T(8,128)}) custom-call(s32[1]{0:T(128)} %bitcast.core_ref, bf16[512,2048]{1,0:T(8,128)(2,1)S(1)} %copy-done, bf16[512,2048]{1,0:T(8,128)(2,1)} %v_ref.11, f32[16,1,512]{2,1,0:T(1,128)S(1)} %copy-done.7, f32[16,8,128]{2,1,0:T(8,128)S(1)} %copy-done.5, ...), custom_call_target="tpu_custom_call" | custom-call | flops 134217728 | bytes 4194304 | tf_op jit(solution)/shard_map/state/pallas_call | solution.py:224
  14.2 0.7 copy-done.9
  14.9 0.1 collective-permute-start.6
  15.0 6.4 %state.2 = (f32[8,3,128,128]{3,2,1,0:T(8,128)S(1)}, f32[4,128,128]{2,1,0:T(8,128)S(1)}, f32[4,128,128]{2,1,0:T(8,128)}) custom-call(s32[1]{0:T(128)} %bitcast.core_ref, bf16[512,2048]{1,0:T(8,128)(2,1)S(1)} %copy-done, bf16[512,2048]{1,0:T(8,128)(2,1)} %v_ref.11, f32[16,1,512]{2,1,0:T(1,128)S(1)} %copy-done.7, f32[16,8,128]{2,1,0:T(8,128)S(1)} %copy-done.5, ...), custom_call_target="tpu_custom_call" | custom-call | flops 134217728 | bytes 4194304 | tf_op jit(solution)/shard_map/state/pallas_call | solution.py:224
  21.4 0.5 collective-permute-start.1
  21.9 0.0 collective-permute-done
  21.9 0.0 collective-permute-done.6
  21.9 1.1 select_add_fusion.2
  23.0 4.5 %collective-permute-start.7 = (f32[4,128,128]{2,1,0:T(8,128)S(1)}, f32[4,128,128]{2,1,0:T(8,128)S(1)}, u32[]{:S(2)}, u32[]{:S(2)}) collective-permute-start(f32[4,128,128]{2,1,0:T(8,128)S(1)} %select_add_fusion.2), channel_id=1, source_target_pairs={{0,4},{1,5},{2,6},{3,7},{16,20},{17,21},{18,22},{19,23}} | collective-permute-start | bytes 786440 | tf_op jit(solution)/shard_map/ppermute | solution.py:264
  27.5 0.0 collective-permute-done.1
  27.5 1.0 select_add_fusion.3
  28.5 1.3 collective-permute-start.2
  29.8 4.3 %collective-permute-done.7 = f32[4,128,128]{2,1,0:T(8,128)S(1)} collective-permute-done((f32[4,128,128]{2,1,0:T(8,128)S(1)}, f32[4,128,128]{2,1,0:T(8,128)S(1)}, u32[]{:S(2)}, u32[]{:S(2)}) %collective-permute-start.7) | collective-permute-done | bytes 262176 | tf_op jit(solution)/shard_map/ppermute | solution.py:264
  34.1 0.8 collective-permute-start.8
  35.0 4.4 %collective-permute-done.2 = f32[4,128,128]{2,1,0:T(8,128)S(1)} collective-permute-done((f32[4,128,128]{2,1,0:T(8,128)S(1)}, f32[4,128,128]{2,1,0:T(8,128)S(1)}, u32[]{:S(2)}, u32[]{:S(2)}) %collective-permute-start.2) | collective-permute-done | bytes 262176 | tf_op jit(solution)/shard_map/ppermute | solution.py:264
  39.4 0.7 collective-permute-start.3
  40.1 0.0 collective-permute-done.8
  40.1 0.0 copy-start.1
  40.1 0.0 copy-start.2
  40.2 0.8 collective-permute-start.9
  41.0 0.1 multiply_add_fusion.10
  41.1 0.7 collective-permute-start.4
  41.7 0.0 collective-permute-done.9
  41.8 0.1 fusion.4
  41.8 0.7 collective-permute-start.10
  42.6 0.0 collective-permute-done.4
  42.6 0.1 fusion.6
  42.6 1.0 collective-permute-start.5
  43.7 0.0 collective-permute-done.10.back_ref
  43.7 14.1 %forward.2 = (bf16[512,2048]{1,0:T(8,128)(2,1)}, bf16[512,2048]{1,0:T(8,128)(2,1)}, f32[8,3,128,128]{3,2,1,0:T(8,128)S(1)}, f32[4,128,128]{2,1,0:T(8,128)S(1)}, f32[4,128,128]{2,1,0:T(8,128)S(1)}) custom-call(s32[1]{0:T(128)} %bitcast.core_ref, bf16[512,2048]{1,0:T(8,128)(2,1)} %q_ref.7, bf16[512,2048]{1,0:T(8,128)(2,1)} %k_ref.11, ...), custom_call_target="tpu_custom_call" | custom-call | flops 536870912 | bytes 8388608 | tf_op jit(solution)/shard_map/forward/pallas_call | solution.py:224
  57.8 0.4 collective-permute-start.16
  58.2 14.0 %forward.3 = (bf16[512,2048]{1,0:T(8,128)(2,1)}, bf16[512,2048]{1,0:T(8,128)(2,1)}, f32[8,3,128,128]{3,2,1,0:T(8,128)S(1)}, f32[4,128,128]{2,1,0:T(8,128)S(1)}, f32[4,128,128]{2,1,0:T(8,128)S(1)}) custom-call(s32[1]{0:T(128)} %bitcast.core_ref, bf16[512,2048]{1,0:T(8,128)(2,1)} %q_ref.7, bf16[512,2048]{1,0:T(8,128)(2,1)} %k_ref.11, ...), custom_call_target="tpu_custom_call", output_to_operand_aliasing={{0}: (12, {})} | custom-call | flops 536870912 | bytes 8388608 | tf_op jit(solution)/shard_map/forward/pallas_call | solution.py:224
  72.3 0.1 collective-permute-start.11
  72.4 0.0 collective-permute-done.16
  72.4 0.7 collective-permute-start.17
  73.1 0.7 collective-permute-done.11
  73.8 0.7 collective-permute-start.12
  74.5 0.0 collective-permute-done.17
  74.6 0.7 collective-permute-start.18
  75.3 0.0 collective-permute-done.12
  75.3 0.7 collective-permute-start.13
  76.0 0.0 collective-permute-done.18
  76.0 0.1 multiply_add_fusion.1
  76.1 0.0 copy-start.4
  76.1 1.4 %collective-permute-start.19 = (f32[4,128,128]{2,1,0:T(8,128)S(1)}, f32[4,128,128]{2,1,0:T(8,128)S(1)}, u32[]{:S(2)}, u32[]{:S(2)}) collective-permute-start(f32[4,128,128]{2,1,0:T(8,128)S(1)} %get-tuple-element.60), channel_id=1, source_target_pairs={{4,0},{5,1},{6,2},{7,3},{20,16},{21,17},{22,18},{23,19}} | collective-permute-start | bytes 786440 | tf_op jit(solution)/shard_map/ppermute | solution.py:264
  77.5 0.0 collective-permute-done.13
  77.5 0.1 multiply_add_fusion.4
  77.6 1.3 collective-permute-start.14
  78.9 33.4 %collective-permute-done.19 = f32[4,128,128]{2,1,0:T(8,128)S(1)} collective-permute-done((f32[4,128,128]{2,1,0:T(8,128)S(1)}, f32[4,128,128]{2,1,0:T(8,128)S(1)}, u32[]{:S(2)}, u32[]{:S(2)}) %collective-permute-start.19) | collective-permute-done | bytes 262176 | tf_op jit(solution)/shard_map/ppermute | solution.py:264
  112.3 0.1 fusion
  112.3 0.1 collective-permute-start.20
  112.4 5.6 %collective-permute-done.14 = f32[4,128,128]{2,1,0:T(8,128)S(1)} collective-permute-done((f32[4,128,128]{2,1,0:T(8,128)S(1)}, f32[4,128,128]{2,1,0:T(8,128)S(1)}, u32[]{:S(2)}, u32[]{:S(2)}) %collective-permute-start.14) | collective-permute-done | bytes 262176 | tf_op jit(solution)/shard_map/ppermute | solution.py:264
  118.1 0.1 fusion.2
  118.1 0.1 collective-permute-start.15
  118.2 0.0 collective-permute-done.20.gback_ref
  118.2 11.3 %backward.2 = (bf16[512,2048]{1,0:T(8,128)(2,1)}, bf16[512,2048]{1,0:T(8,128)(2,1)}, bf16[512,2048]{1,0:T(8,128)(2,1)}) custom-call(s32[1]{0:T(128)} %bitcast.core_ref, bf16[512,2048]{1,0:T(8,128)(2,1)} %q_ref.7, bf16[512,2048]{1,0:T(8,128)(2,1)} %k_ref.11, bf16[512,2048]{1,0:T(8,128)(2,1)} %v_ref.11, bf16[512,2048]{1,0:T(8,128)(2,1)} %get-tuple-element.50.g_ref, ...), custom_call_target="tpu_custom_call" | custom-call | flops 1073741824 | bytes 10485760 | tf_op jit(solution)/shard_map/backward/pallas_call | solution.py:224
  129.5 0.0 collective-permute-done.15.gback_ref
  129.5 11.3 %backward.3 = (bf16[512,2048]{1,0:T(8,128)(2,1)}, bf16[512,2048]{1,0:T(8,128)(2,1)}, bf16[512,2048]{1,0:T(8,128)(2,1)}) custom-call(s32[1]{0:T(128)} %bitcast.core_ref, bf16[512,2048]{1,0:T(8,128)(2,1)} %q_ref.7, bf16[512,2048]{1,0:T(8,128)(2,1)} %k_ref.11, bf16[512,2048]{1,0:T(8,128)(2,1)} %v_ref.11, ...), custom_call_target="tpu_custom_call", output_to_operand_aliasing={{0}: (16, {}), {1}: (17, {}), {2}: (18, {})} | custom-call | flops 1073741824 | bytes 10485760 | tf_op jit(solution)/shard_map/backward/pallas_call | solution.py:224
  (27 shorter events, 0.3 us)
Async XLA Ops:
  3.2 18.7 %collective-permute-start = (f32[16,128]{1,0:T(8,128)}, f32[16,128]{1,0:T(8,128)S(1)}, u32[]{:S(2)}, u32[]{:S(2)}) collective-permute-start(f32[16,128]{1,0:T(8,128)} %get-tuple-element.38), channel_id=1, source_target_pairs={{0,1},{1,0},{2,3},{3,2},{4,5},{5,4},{6,7},{7,6},{8,9},{9,8},{10,11... | collective-permute-start | bytes 24584 | tf_op jit(solution)/shard_map/ppermute | solution.py:198
  3.6 1.6 %copy-start = (bf16[512,2048]{1,0:T(8,128)(2,1)S(1)}, bf16[512,2048]{1,0:T(8,128)(2,1)}, u32[]{:S(2)}) copy-start(bf16[512,2048]{1,0:T(8,128)(2,1)} %k_ref.11) | copy-start | bytes 6291460
  5.2 0.9 copy-start.3
  6.2 0.8 copy-start.5
  7.0 0.8 copy-start.7
  14.2 0.7 copy-start.9
  14.9 7.0 %copy-start.11 = (f32[16,128]{1,0:T(8,128)S(1)}, f32[16,128]{1,0:T(8,128)}, u32[]{:S(2)}) copy-start(f32[16,128]{1,0:T(8,128)} %get-tuple-element.38) | copy-start | bytes 24580
  14.9 7.0 %collective-permute-start.6 = (f32[4,128,128]{2,1,0:T(8,128)}, f32[4,128,128]{2,1,0:T(8,128)}, u32[]{:S(2)}, u32[]{:S(2)}) collective-permute-start(f32[4,128,128]{2,1,0:T(8,128)} %get-tuple-element.43), channel_id=1, source_target_pairs={{0,1},{1,0},{2,3},{3,2},{4,5},{5,4},{6,7},{7,6},{8,9},{9,8},{10,11... | collective-permute-start | bytes 786440 | tf_op jit(solution)/shard_map/ppermute | solution.py:251
  21.4 6.1 %collective-permute-start.1 = (f32[4,128,128]{2,1,0:T(8,128)}, f32[4,128,128]{2,1,0:T(8,128)}, u32[]{:S(2)}, u32[]{:S(2)}) collective-permute-start(f32[4,128,128]{2,1,0:T(8,128)} %get-tuple-element.40), channel_id=1, source_target_pairs={{0,1},{1,0},{2,3},{3,2},{4,5},{5,4},{6,7},{7,6},{8,9},{9,8},{10,11... | collective-permute-start | bytes 786440 | tf_op jit(solution)/shard_map/ppermute | solution.py:251
  23.0 11.1 %collective-permute-start.7 = (f32[4,128,128]{2,1,0:T(8,128)S(1)}, f32[4,128,128]{2,1,0:T(8,128)S(1)}, u32[]{:S(2)}, u32[]{:S(2)}) collective-permute-start(f32[4,128,128]{2,1,0:T(8,128)S(1)} %select_add_fusion.2), channel_id=1, source_target_pairs={{0,4},{1,5},{2,6},{3,7},{16,20},{17,21},{18,22},{19,23}} | collective-permute-start | bytes 786440 | tf_op jit(solution)/shard_map/ppermute | solution.py:264
  28.5 10.8 %collective-permute-start.2 = (f32[4,128,128]{2,1,0:T(8,128)S(1)}, f32[4,128,128]{2,1,0:T(8,128)S(1)}, u32[]{:S(2)}, u32[]{:S(2)}) collective-permute-start(f32[4,128,128]{2,1,0:T(8,128)S(1)} %select_add_fusion.3), channel_id=1, source_target_pairs={{0,4},{1,5},{2,6},{3,7},{16,20},{17,21},{18,22},{19,23}} | collective-permute-start | bytes 786440 | tf_op jit(solution)/shard_map/ppermute | solution.py:264
  34.1 7.6 %copy-start.10 = (f32[4,128,128]{2,1,0:T(8,128)S(1)}, f32[4,128,128]{2,1,0:T(8,128)}, u32[]{:S(2)}) copy-start(f32[4,128,128]{2,1,0:T(8,128)} %copy-done.9) | copy-start | bytes 786436
  34.1 5.9 %collective-permute-start.8 = (f32[4,128,128]{2,1,0:T(8,128)S(1)}, f32[4,128,128]{2,1,0:T(8,128)S(1)}, u32[]{:S(2)}, u32[]{:S(2)}) collective-permute-start(f32[4,128,128]{2,1,0:T(8,128)S(1)} %multiply_add_fusion.8), channel_id=1, source_target_pairs={{4,8},{5,9},{6,10},{7,11},{20,24},{21,25},{22,26},{23,27}} | collective-permute-start | bytes 786440 | tf_op jit(solution)/shard_map/ppermute | solution.py:264
  39.4 1.6 %collective-permute-start.3 = (f32[4,128,128]{2,1,0:T(8,128)S(1)}, f32[4,128,128]{2,1,0:T(8,128)S(1)}, u32[]{:S(2)}, u32[]{:S(2)}) collective-permute-start(f32[4,128,128]{2,1,0:T(8,128)S(1)} %multiply_add_fusion.11), channel_id=1, source_target_pairs={{4,8},{5,9},{6,10},{7,11},{20,24},{21,25},{22,26},{23,27}} | collective-permute-start | bytes 786440 | tf_op jit(solution)/shard_map/ppermute | solution.py:264
  40.1 3.6 %copy-start.1 = (f32[512,128]{1,0:T(8,128)S(1)}, f32[512,128]{1,0:T(8,128)}, u32[]{:S(2)}) copy-start(f32[512,128]{1,0:T(8,128)} %get-tuple-element.34.weight_bias_ref) | copy-start | bytes 786436
  40.1 3.6 %copy-start.2 = (f32[512,128]{1,0:T(8,128)S(1)}, f32[512,128]{1,0:T(8,128)}, u32[]{:S(2)}) copy-start(f32[512,128]{1,0:T(8,128)} %get-tuple-element.35.enter_bias_ref) | copy-start | bytes 786436
  40.1 3.6 %copy-start.6 = (f32[16,8,128]{2,1,0:T(8,128)S(1)}, f32[16,8,128]{2,1,0:T(8,128)}, u32[]{:S(2)}) copy-start(f32[16,8,128]{2,1,0:T(8,128)} %get-tuple-element.33.table_ref) | copy-start | bytes 196612
  40.2 3.6 %copy-start.8 = (f32[16,1,512]{2,1,0:T(1,128)S(1)}, f32[16,1,512]{2,1,0:T(1,128)}, u32[]{:S(2)}) copy-start(f32[16,1,512]{2,1,0:T(1,128)} %get-tuple-element.32.run_ref) | copy-start | bytes 98308
  40.2 1.6 %collective-permute-start.9 = (f32[4,128,128]{2,1,0:T(8,128)S(1)}, f32[4,128,128]{2,1,0:T(8,128)S(1)}, u32[]{:S(2)}, u32[]{:S(2)}) collective-permute-start(f32[4,128,128]{2,1,0:T(8,128)S(1)} %get-tuple-element.64), channel_id=1, source_target_pairs={{8,12},{9,13},{10,14},{11,15},{24,28},{25,29},{26,30},{27,31}} | collective-permute-start | bytes 786440 | tf_op jit(solution)/shard_map/ppermute | solution.py:264
  41.1 1.5 %collective-permute-start.4 = (f32[4,128,128]{2,1,0:T(8,128)S(1)}, f32[4,128,128]{2,1,0:T(8,128)S(1)}, u32[]{:S(2)}, u32[]{:S(2)}) collective-permute-start(f32[4,128,128]{2,1,0:T(8,128)S(1)} %get-tuple-element.69), channel_id=1, source_target_pairs={{8,12},{9,13},{10,14},{11,15},{24,28},{25,29},{26,30},{27,31}} | collective-permute-start | bytes 786440 | tf_op jit(solution)/shard_map/ppermute | solution.py:264
  41.8 1.9 %collective-permute-start.10 = (f32[4,128,128]{2,1,0:T(8,128)S(1)}, f32[4,128,128]{2,1,0:T(8,128)S(1)}, u32[]{:S(2)}, u32[]{:S(2)}) collective-permute-start(f32[4,128,128]{2,1,0:T(8,128)S(1)} %get-tuple-element.78), channel_id=1, source_target_pairs={{0,1},{1,0},{2,3},{3,2},{4,5},{5,4},{6,7},{7,6},{8,9},{9,8},{10,11... | collective-permute-start | bytes 786440 | tf_op jit(solution)/shard_map/ppermute | solution.py:272
  42.6 15.6 %collective-permute-start.5 = (f32[4,128,128]{2,1,0:T(8,128)S(1)}, f32[4,128,128]{2,1,0:T(8,128)S(1)}, u32[]{:S(2)}, u32[]{:S(2)}) collective-permute-start(f32[4,128,128]{2,1,0:T(8,128)S(1)} %get-tuple-element.80), channel_id=1, source_target_pairs={{0,1},{1,0},{2,3},{3,2},{4,5},{5,4},{6,7},{7,6},{8,9},{9,8},{10,11... | collective-permute-start | bytes 786440 | tf_op jit(solution)/shard_map/ppermute | solution.py:272
  57.8 14.5 %collective-permute-start.16 = (f32[4,128,128]{2,1,0:T(8,128)S(1)}, f32[4,128,128]{2,1,0:T(8,128)S(1)}, u32[]{:S(2)}, u32[]{:S(2)}) collective-permute-start(f32[4,128,128]{2,1,0:T(8,128)S(1)} %get-tuple-element.52), channel_id=1, source_target_pairs={{0,1},{1,0},{2,3},{3,2},{4,5},{5,4},{6,7},{7,6},{8,9},{9,8},{10,11... | collective-permute-start | bytes 786440 | tf_op jit(solution)/shard_map/ppermute | solution.py:251
  72.3 1.5 %collective-permute-start.11 = (f32[4,128,128]{2,1,0:T(8,128)S(1)}, f32[4,128,128]{2,1,0:T(8,128)S(1)}, u32[]{:S(2)}, u32[]{:S(2)}) collective-permute-start(f32[4,128,128]{2,1,0:T(8,128)S(1)} %get-tuple-element.48), channel_id=1, source_target_pairs={{0,1},{1,0},{2,3},{3,2},{4,5},{5,4},{6,7},{7,6},{8,9},{9,8},{10,11... | collective-permute-start | bytes 786440 | tf_op jit(solution)/shard_map/ppermute | solution.py:251
  72.4 2.1 %collective-permute-start.17 = (f32[4,128,128]{2,1,0:T(8,128)S(1)}, f32[4,128,128]{2,1,0:T(8,128)S(1)}, u32[]{:S(2)}, u32[]{:S(2)}) collective-permute-start(f32[4,128,128]{2,1,0:T(8,128)S(1)} %select_add_fusion), channel_id=1, source_target_pairs={{12,8},{13,9},{14,10},{15,11},{28,24},{29,25},{30,26},{31,27}} | collective-permute-start | bytes 786440 | tf_op jit(solution)/shard_map/ppermute | solution.py:264
  73.8 1.4 %collective-permute-start.12 = (f32[4,128,128]{2,1,0:T(8,128)S(1)}, f32[4,128,128]{2,1,0:T(8,128)S(1)}, u32[]{:S(2)}, u32[]{:S(2)}) collective-permute-start(f32[4,128,128]{2,1,0:T(8,128)S(1)} %select_add_fusion.1), channel_id=1, source_target_pairs={{12,8},{13,9},{14,10},{15,11},{28,24},{29,25},{30,26},{31,27}} | collective-permute-start | bytes 786440 | tf_op jit(solution)/shard_map/ppermute | solution.py:264
  74.6 1.4 %collective-permute-start.18 = (f32[4,128,128]{2,1,0:T(8,128)S(1)}, f32[4,128,128]{2,1,0:T(8,128)S(1)}, u32[]{:S(2)}, u32[]{:S(2)}) collective-permute-start(f32[4,128,128]{2,1,0:T(8,128)S(1)} %multiply_add_fusion.2), channel_id=1, source_target_pairs={{8,4},{9,5},{10,6},{11,7},{24,20},{25,21},{26,22},{27,23}} | collective-permute-start | bytes 786440 | tf_op jit(solution)/shard_map/ppermute | solution.py:264
  75.3 2.2 %collective-permute-start.13 = (f32[4,128,128]{2,1,0:T(8,128)S(1)}, f32[4,128,128]{2,1,0:T(8,128)S(1)}, u32[]{:S(2)}, u32[]{:S(2)}) collective-permute-start(f32[4,128,128]{2,1,0:T(8,128)S(1)} %multiply_add_fusion.5), channel_id=1, source_target_pairs={{8,4},{9,5},{10,6},{11,7},{24,20},{25,21},{26,22},{27,23}} | collective-permute-start | bytes 786440 | tf_op jit(solution)/shard_map/ppermute | solution.py:264
  76.1 42.1 %copy-start.4 = (f32[512,128]{1,0:T(8,128)S(1)}, f32[512,128]{1,0:T(8,128)}, u32[]{:S(2)}) copy-start(f32[512,128]{1,0:T(8,128)} %get-tuple-element.36.leave_bias_ref) | copy-start | bytes 786436
  76.1 36.2 %collective-permute-start.19 = (f32[4,128,128]{2,1,0:T(8,128)S(1)}, f32[4,128,128]{2,1,0:T(8,128)S(1)}, u32[]{:S(2)}, u32[]{:S(2)}) collective-permute-start(f32[4,128,128]{2,1,0:T(8,128)S(1)} %get-tuple-element.60), channel_id=1, source_target_pairs={{4,0},{5,1},{6,2},{7,3},{20,16},{21,17},{22,18},{23,19}} | collective-permute-start | bytes 786440 | tf_op jit(solution)/shard_map/ppermute | solution.py:264
  77.6 40.5 %collective-permute-start.14 = (f32[4,128,128]{2,1,0:T(8,128)S(1)}, f32[4,128,128]{2,1,0:T(8,128)S(1)}, u32[]{:S(2)}, u32[]{:S(2)}) collective-permute-start(f32[4,128,128]{2,1,0:T(8,128)S(1)} %get-tuple-element.62), channel_id=1, source_target_pairs={{4,0},{5,1},{6,2},{7,3},{20,16},{21,17},{22,18},{23,19}} | collective-permute-start | bytes 786440 | tf_op jit(solution)/shard_map/ppermute | solution.py:264
  112.3 5.9 %collective-permute-start.20 = (f32[4,128,128]{2,1,0:T(8,128)S(1)}, f32[4,128,128]{2,1,0:T(8,128)S(1)}, u32[]{:S(2)}, u32[]{:S(2)}) collective-permute-start(f32[4,128,128]{2,1,0:T(8,128)S(1)} %get-tuple-element.74), channel_id=1, source_target_pairs={{0,1},{1,0},{2,3},{3,2},{4,5},{5,4},{6,7},{7,6},{8,9},{9,8},{10,11... | collective-permute-start | bytes 786440 | tf_op jit(solution)/shard_map/ppermute | solution.py:272
  118.1 11.4 %collective-permute-start.15 = (f32[4,128,128]{2,1,0:T(8,128)S(1)}, f32[4,128,128]{2,1,0:T(8,128)S(1)}, u32[]{:S(2)}, u32[]{:S(2)}) collective-permute-start(f32[4,128,128]{2,1,0:T(8,128)S(1)} %get-tuple-element.76), channel_id=1, source_target_pairs={{0,1},{1,0},{2,3},{3,2},{4,5},{5,4},{6,7},{7,6},{8,9},{9,8},{10,11... | collective-permute-start | bytes 786440 | tf_op jit(solution)/shard_map/ppermute | solution.py:272

commit v2 on v1

--- a/solution.py
+++ b/solution.py
@@ -13,7 +13,7 @@
 GROUPS = 2
 F32 = jnp.float32
 BF16 = jnp.bfloat16
-VMEM_LIMIT = 48 * 1024 * 1024
+VMEM_LIMIT = 32 * 1024 * 1024
 
 
 def dot(a, b):
@@ -67,14 +67,17 @@
 
 def state_kernel(chunks, quarter, core_ref, k_ref, v_ref, run_ref, table_ref, leave_bias_ref, prefix_ref, mine_ref, other_ref):
     p = pl.program_id(0)
+    spans = [pl.ds(j * C, C) for j in range(chunks)]
+    runs = [columns(run_ref[0, :, span]) for span in spans]
+    leaves = [
+        jnp.exp(table_ref[0, chunks + j : chunks + j + 1, :] - runs[j] + leave_bias_ref[spans[j], :])
+        for j in range(chunks)
+    ]
+    kds = [(k_ref[spans[j], :].astype(F32) * leaves[j]).astype(BF16) for j in range(chunks)]
+    updates = [t_dot(kds[j], v_ref[spans[j], :]) for j in range(chunks)]
     total = None
     for j in range(chunks):
-        span = pl.ds(j * C, C)
-        run = columns(run_ref[0, :, span])
-        leave = jnp.exp(table_ref[0, chunks + j : chunks + j + 1, :] - run + leave_bias_ref[span, :])
-        kd = (k_ref[span, :].astype(F32) * leave).astype(BF16)
-        update = t_dot(kd, v_ref[span, :])
-        total = update if total is None else table_ref[0, j : j + 1, :] * total + update
+        total = updates[j] if total is None else table_ref[0, j : j + 1, :] * total + updates[j]
         if j < chunks - 1:
             prefix_ref[0, j] = total
 
@@ -85,6 +88,15 @@
     @pl.when(p >= quarter)
     def _():
         other_ref[0] = total
+
+
+def entering_states(chunks, incoming, table_ref, prefix_ref):
+    states, gain = [], None
+    for j in range(chunks):
+        states.append((incoming if j == 0 else gain * incoming + prefix_ref[0, j - 1]).astype(BF16))
+        passing = table_ref[0, j : j + 1, :]
+        gain = passing if gain is None else gain * passing
+    return states
 
 
 def forward_kernel(
@@ -93,30 +105,33 @@
 ):
     normed_ref, grad_ref, suffix_ref, mine_ref, other_ref = rest[-5:]
     p = pl.program_id(0)
+    each = range(chunks)
+    spans = [pl.ds(j * C, C) for j in each]
     incoming = jnp.where(p < quarter, keep_ref[0], back_ref[0])
-    gain = None
-    parts = []
-    for j in range(chunks):
-        span = pl.ds(j * C, C)
-        row = run_ref[0, :, span]
-        run = columns(row)
-        weights = jnp.exp(run - row + weight_bias_ref[span, :])
-        enter = jnp.exp(run + enter_bias_ref[span, :])
-        q, k, v = q_ref[span, :], k_ref[span, :], v_ref[span, :]
-        attend = (dot_t(q, k) * weights).astype(BF16)
-        state = incoming if j == 0 else gain * incoming + prefix_ref[0, j - 1]
-        passing = table_ref[0, j : j + 1, :]
-        gain = passing if gain is None else gain * passing
-        out = dot(attend, v) + enter * dot(q, state.astype(BF16))
-        factor = lax.rsqrt(jnp.mean(out * out, axis=-1, keepdims=True) + EPS)
-        normed = out * factor
-        normed_ref[span, :] = normed.astype(BF16)
-        og = og_ref[span, :].astype(F32)
-        along = jnp.mean(og * out, axis=-1, keepdims=True)
-        grad = (factor * og - (factor * factor * factor * along) * out).astype(BF16)
-        grad_ref[span, :] = grad
-        qd = (q.astype(F32) * enter).astype(BF16)
-        parts.append(t_dot(qd, grad))
+    states = entering_states(chunks, incoming, table_ref, prefix_ref)
+    q = [q_ref[span, :] for span in spans]
+    scores = [dot_t(q[j], k_ref[spans[j], :]) for j in each]
+    outside = [dot(q[j], states[j]) for j in each]
+    rows = [run_ref[0, :, span] for span in spans]
+    runs = [columns(row) for row in rows]
+    attends = [
+        (scores[j] * jnp.exp(runs[j] - rows[j] + weight_bias_ref[spans[j], :])).astype(BF16) for j in each
+    ]
+    enters = [jnp.exp(runs[j] + enter_bias_ref[spans[j], :]) for j in each]
+    qds = [(q[j].astype(F32) * enters[j]).astype(BF16) for j in each]
+    outs = [dot(attends[j], v_ref[spans[j], :]) + enters[j] * outside[j] for j in each]
+    squares = [jnp.mean(outs[j] * outs[j], axis=-1, keepdims=True) for j in each]
+    ogs = [og_ref[span, :].astype(F32) for span in spans]
+    alongs = [jnp.mean(ogs[j] * outs[j], axis=-1, keepdims=True) for j in each]
+    factors = [lax.rsqrt(square + EPS) for square in squares]
+    grads = []
+    for j in each:
+        normed = outs[j] * factors[j]
+        normed_ref[spans[j], :] = normed.astype(BF16)
+        grad = (factors[j] * (ogs[j] - (factors[j] * alongs[j]) * normed)).astype(BF16)
+        grad_ref[spans[j], :] = grad
+        grads.append(grad)
+    parts = [t_dot(qds[j], grads[j]) for j in each]
     total = parts[-1]
     for j in range(chunks - 2, -1, -1):
         suffix_ref[0, j] = total
@@ -137,35 +152,76 @@
 ):
     dq_ref, dk_ref, dv_ref = rest[-3:]
     p = pl.program_id(0)
+    each = range(chunks)
+    spans = [pl.ds(j * C, C) for j in each]
     incoming = jnp.where(p < quarter, keep_ref[0], back_ref[0])
     outgoing = jnp.where(p < quarter, gkeep_ref[0], gback_ref[0])
-    states = []
-    gain = None
-    for j in range(chunks):
-        states.append((incoming if j == 0 else gain * incoming + prefix_ref[0, j - 1]).astype(BF16))
+    states = entering_states(chunks, incoming, table_ref, prefix_ref)
+    gstates, gain = [None] * chunks, None
+    for j in range(chunks - 1, -1, -1):
+        gstates[j] = (outgoing if j == chunks - 1 else gain * outgoing + suffix_ref[0, j]).astype(BF16)
         passing = table_ref[0, j : j + 1, :]
         gain = passing if gain is None else gain * passing
-    gain = None
-    for j in range(chunks - 1, -1, -1):
-        span = pl.ds(j * C, C)
-        row = run_ref[0, :, span]
-        run = columns(row)
-        weights = jnp.exp(run - row + weight_bias_ref[span, :])
-        enter = jnp.exp(run + enter_bias_ref[span, :])
-        leave = jnp.exp(table_ref[0, chunks + j : chunks + j + 1, :] - run + leave_bias_ref[span, :])
-        q, k, v, g = q_ref[span, :], k_ref[span, :], v_ref[span, :], g_ref[span, :]
-        attend = (dot_t(q, k) * weights).astype(BF16)
-        dattend = (dot_t(g, v) * weights).astype(BF16)
-        gstate = outgoing if j == chunks - 1 else gain * outgoing + suffix_ref[0, j]
-        passing = table_ref[0, j : j + 1, :]
-        gain = passing if gain is None else gain * passing
-        gstate = gstate.astype(BF16)
-        dq = dot(dattend, k) + enter * dot_t(g, states[j])
-        dk = t_dot(dattend, q) + leave * dot_t(v, gstate)
-        dv = t_dot(attend, g) + leave * dot(k, gstate)
-        dq_ref[span, :] = dq.astype(BF16)
-        dk_ref[span, :] = dk.astype(BF16)
-        dv_ref[span, :] = dv.astype(BF16)
+    q, k, v, g = ([ref[span, :] for span in spans] for ref in (q_ref, k_ref, v_ref, g_ref))
+    scores = [dot_t(q[j], k[j]) for j in each]
+    dscores = [dot_t(g[j], v[j]) for j in each]
+    rows = [run_ref[0, :, span] for span in spans]
+    runs = [columns(row) for row in rows]
+    weights = [jnp.exp(runs[j] - rows[j] + weight_bias_ref[spans[j], :]) for j in each]
+    attends = [(scores[j] * weights[j]).astype(BF16) for j in each]
+    dattends = [(dscores[j] * weights[j]).astype(BF16) for j in each]
+    enters = [jnp.exp(runs[j] + enter_bias_ref[spans[j], :]) for j in each]
+    leaves = [
+        jnp.exp(table_ref[0, chunks + j : chunks + j + 1, :] - runs[j] + leave_bias_ref[spans[j], :]) for j in each
+    ]
+    for j in each:
+        dq_ref[spans[j], :] = (dot(dattends[j], k[j]) + enters[j] * dot_t(g[j], states[j])).astype(BF16)
+    for j in each:
+        dk_ref[spans[j], :] = (t_dot(dattends[j], q[j]) + leaves[j] * dot_t(v[j], gstates[j])).astype(BF16)
+    for j in each:
+        dv_ref[spans[j], :] = (t_dot(attends[j], g[j]) + leaves[j] * dot(k[j], gstates[j])).astype(BF16)
+
+
+def block_specs(group, size, quarter, chunks, length, dh):
+    def head(p, core_ref):
+        return group * size + lax.rem(p + core_ref[0] * quarter, size)
+
+    return dict(
+        rows=pl.BlockSpec((length, dh), lambda p, c: (0, head(p, c))),
+        run=pl.BlockSpec((1, 1, length), lambda p, c: (head(p, c), 0, 0)),
+        table=pl.BlockSpec((1, 2 * chunks, C), lambda p, c: (head(p, c), 0, 0)),
+        bias=pl.BlockSpec((length, C), lambda p, c: (0, 0)),
+        states=pl.BlockSpec((1, chunks - 1, dh, dh), lambda p, c: (p, 0, 0, 0)),
+        mine=pl.BlockSpec((1, dh, dh), lambda p, c: (jnp.minimum(p, quarter - 1), 0, 0)),
+        other=pl.BlockSpec((1, dh, dh), lambda p, c: (jnp.maximum(p - quarter, 0), 0, 0)),
+        any=pl.BlockSpec(memory_space=pl.ANY),
+    )
+
+
+def call_heads(dims, core_arg, kernel, group, in_names, out_names, out_shapes, args, name, products, reads, aliases=()):
+    size, quarter, chunks, length, dh = dims
+    table = block_specs(group, *dims)
+    extra = [a for a in aliases if a is not None]
+    return pl.pallas_call(
+        functools.partial(kernel, chunks, quarter),
+        grid_spec=pltpu.PrefetchScalarGridSpec(
+            num_scalar_prefetch=1,
+            grid=(size,),
+            in_specs=[table[n] for n in in_names] + [table["any"]] * len(extra),
+            out_specs=[table[n] for n in out_names],
+        ),
+        out_shape=out_shapes,
+        input_output_aliases={1 + len(in_names) + i: i for i in range(len(extra))},
+        compiler_params=pltpu.CompilerParams(
+            dimension_semantics=("arbitrary",), vmem_limit_bytes=VMEM_LIMIT
+        ),
+        cost_estimate=pl.CostEstimate(
+            flops=products * size * 2 * length * C * dh,
+            bytes_accessed=reads * size * length * dh * 2,
+            transcendentals=size * length * C,
+        ),
+        name=name,
+    )(core_arg, *args, *extra)
 
 
 def local(query_in, key_in, value_in, log_decay, doc_start, out_grad):
@@ -199,48 +255,11 @@
     gain0 = jnp.where(first, gain, gain_other)
     gain1 = jnp.where(first, gain_other, gain)
 
-    def specs(group):
-        def head(p, core_ref):
-            return group * size + lax.rem(p + core_ref[0] * quarter, size)
-
-        return dict(
-            rows=pl.BlockSpec((length, dh), lambda p, c: (0, head(p, c))),
-            run=pl.BlockSpec((1, 1, length), lambda p, c: (head(p, c), 0, 0)),
-            table=pl.BlockSpec((1, 2 * chunks, C), lambda p, c: (head(p, c), 0, 0)),
-            bias=pl.BlockSpec((length, C), lambda p, c: (0, 0)),
-            states=pl.BlockSpec((1, chunks - 1, dh, dh), lambda p, c: (p, 0, 0, 0)),
-            mine=pl.BlockSpec((1, dh, dh), lambda p, c: (jnp.minimum(p, quarter - 1), 0, 0)),
-            other=pl.BlockSpec((1, dh, dh), lambda p, c: (jnp.maximum(p - quarter, 0), 0, 0)),
-            any=pl.BlockSpec(memory_space=pl.ANY),
-        )
-
     states_shape = shape((size, chunks - 1, dh, dh), F32)
     part_shape = shape((quarter, dh, dh), F32)
     rows_shape = shape((length, width), BF16)
 
-    def call(kernel, group, in_names, out_names, out_shapes, args, name, products, reads, aliases=()):
-        table = specs(group)
-        extra = [a for a in aliases if a is not None]
-        return pl.pallas_call(
-            functools.partial(kernel, chunks, quarter),
-            grid_spec=pltpu.PrefetchScalarGridSpec(
-                num_scalar_prefetch=1,
-                grid=(size,),
-                in_specs=[table[n] for n in in_names] + [table["any"]] * len(extra),
-                out_specs=[table[n] for n in out_names],
-            ),
-            out_shape=out_shapes,
-            input_output_aliases={1 + len(in_names) + i: i for i in range(len(extra))},
-            compiler_params=pltpu.CompilerParams(
-                dimension_semantics=("arbitrary",), vmem_limit_bytes=VMEM_LIMIT
-            ),
-            cost_estimate=pl.CostEstimate(
-                flops=products * size * 2 * length * C * dh,
-                bytes_accessed=reads * size * length * dh * 2,
-                transcendentals=size * length * C,
-            ),
-            name=name,
-        )(core_arg, *args, *extra)
+    call = functools.partial(call_heads, (size, quarter, chunks, length, dh), core_arg)
 
     def pick(array, group):
         start = group * size + core * quarter

time: 142 us -> 120 us (0.85)
  Pallas kernels: 66.1 us -> 43.7 us
  local copies, waits for them, and re-layouts: 4.89 us -> 6.48 us
    pallas_call x6, Pallas kernels: 63.5 us -> 41.1 us  [call_heads(): pl.pallas_call(functools.partial(kernel, chunks, quarter), grid_spec=pltp...]
    unnamed x24 -> x32, local copies, waits for them, and re-layouts: 4.89 us -> 6.48 us
  transfers between devices with their start and end apart: 21 -> 21, of which waited for: 5 -> 5; matrix products, arithmetic and copies ran while one was open for 2% -> 3% of each run, Pallas kernels for 37% -> 27%
where the time goes in v2:
time: 120 us
  waiting for transfers between devices  47 us (39%)
  Pallas kernels  43.7 us (36%)
  starting transfers between devices  17.7 us (15%)
  local copies, waits for them, and re-layouts  6.48 us (5%)
  other arithmetic  3.9 us (3%)
    ppermute x12, waiting for transfers between devices, carry(): landed = lax.ppermute(sent, 'seq', [hop])  46.6 us
    pallas_call x6, Pallas kernels, call_heads(): pl.pallas_call(functools.partial(kernel, chunks, quarter), grid_spec=pltp...  41.1 us
    ppermute x12, starting transfers between devices, carry(): landed = lax.ppermute(sent, 'seq', [hop])  14.5 us
    unnamed x32, local copies, waits for them, and re-layouts  6.48 us
    pallas_call x1, Pallas kernels, local(): pl.pallas_call(functools.partial(prepare_kernel, chunks), out_shape=(shap...  2.55 us
  transfers between devices with their start and end apart: 21, of which 5 were waited for; matrix products, arithmetic and copies ran while one was open for 3% of the time, Pallas kernels for 27%

profile of v2, /device:TPU:0, one launch (start us, length us, event | category | flops | bytes accessed | tf_op | source)
XLA Modules:
  0.0 119.8 jit_solution(5868688627740947842)
XLA Ops:
  0.6 2.5 %prepare.1 = (f32[16,1,512]{2,1,0:T(1,128)}, f32[16,8,128]{2,1,0:T(8,128)}, f32[16,128]{1,0:T(8,128)}, f32[512,128]{1,0:T(8,128)}, f32[512,128]{1,0:T(8,128)}, /*index=5*/f32[512,128]{1,0:T(8,128)}) custom-call(f32[16,512]{1,0:T(8,128)} %decay_ref.1, s32[1,512]{1,0:T(1,128)} %bitcast.2), custom_call_target="tpu_custom_call" | custom-call | tf_op jit(solution)/shard_map/prepare/pallas_call | solution.py:242
  3.2 0.5 collective-permute-start
  3.6 1.6 %copy-done = bf16[512,2048]{1,0:T(8,128)(2,1)S(1)} copy-done((bf16[512,2048]{1,0:T(8,128)(2,1)S(1)}, bf16[512,2048]{1,0:T(8,128)(2,1)}, u32[]{:S(2)}) %copy-start) | copy-done | bytes 2097176
  5.2 1.6 %copy-done.2 = bf16[512,2048]{1,0:T(8,128)(2,1)S(1)} copy-done((bf16[512,2048]{1,0:T(8,128)(2,1)S(1)}, bf16[512,2048]{1,0:T(8,128)(2,1)}, u32[]{:S(2)}) %copy-start.2) | copy-done | bytes 2097176
  6.8 0.9 copy-done.8
  7.8 0.8 copy-done.10
  8.6 0.8 copy-done.12
  9.4 4.3 %state.3 = (f32[8,3,128,128]{3,2,1,0:T(8,128)S(1)}, f32[4,128,128]{2,1,0:T(8,128)S(1)}, f32[4,128,128]{2,1,0:T(8,128)}) custom-call(s32[1]{0:T(128)} %bitcast.core_ref, bf16[512,2048]{1,0:T(8,128)(2,1)S(1)} %copy-done, bf16[512,2048]{1,0:T(8,128)(2,1)S(1)} %copy-done.2, f32[16,1,512]{2,1,0:T(1,128)S(1)} %copy-done.12, f32[16,8,128]{2,1,0:T(8,128)S(1)} %copy-done.10, ...), custom_call_target="tpu_custom_call" | custom-call | flops 134217728 | bytes 4194304 | tf_op jit(solution)/shard_map/state/pallas_call | solution.py:205
  13.7 0.7 copy-done.14
  14.4 0.1 collective-permute-start.6
  14.4 4.3 %state.2 = (f32[8,3,128,128]{3,2,1,0:T(8,128)S(1)}, f32[4,128,128]{2,1,0:T(8,128)S(1)}, f32[4,128,128]{2,1,0:T(8,128)}) custom-call(s32[1]{0:T(128)} %bitcast.core_ref, bf16[512,2048]{1,0:T(8,128)(2,1)S(1)} %copy-done, bf16[512,2048]{1,0:T(8,128)(2,1)S(1)} %copy-done.2, f32[16,1,512]{2,1,0:T(1,128)S(1)} %copy-done.12, f32[16,8,128]{2,1,0:T(8,128)S(1)} %copy-done.10, ...), custom_call_target="tpu_custom_call" | custom-call | flops 134217728 | bytes 4194304 | tf_op jit(solution)/shard_map/state/pallas_call | solution.py:205
  18.7 0.5 collective-permute-start.1
  19.2 0.0 collective-permute-done
  19.2 0.0 collective-permute-done.6
  19.3 0.0 copy-start.5
  19.3 1.2 %select_add_fusion.2 = f32[4,128,128]{2,1,0:T(8,128)S(1)} fusion(f32[4,128,128]{2,1,0:T(8,128)} %collective-permute-done.6, f32[4,128,128]{2,1,0:T(8,128)} %copy-done.14, f32[4,128]{1,0:T(4,128)S(1)} %get-tuple-element.67, pred[]{:T(512)S(6)} %eq.3), kind=kLoop, calls=%fused_computation.17 | loop fusion | flops 262144 | bytes 788481 | tf_op jit(solution)/shard_map/add | solution.py:278
  20.5 4.5 %collective-permute-start.7 = (f32[4,128,128]{2,1,0:T(8,128)S(1)}, f32[4,128,128]{2,1,0:T(8,128)S(1)}, u32[]{:S(2)}, u32[]{:S(2)}) collective-permute-start(f32[4,128,128]{2,1,0:T(8,128)S(1)} %select_add_fusion.2), channel_id=1, source_target_pairs={{0,4},{1,5},{2,6},{3,7},{16,20},{17,21},{18,22},{19,23}} | collective-permute-start | bytes 786440 | tf_op jit(solution)/shard_map/ppermute | solution.py:283
  25.0 0.0 collective-permute-done.1
  25.0 1.0 select_add_fusion.3
  26.0 1.3 %collective-permute-start.2 = (f32[4,128,128]{2,1,0:T(8,128)S(1)}, f32[4,128,128]{2,1,0:T(8,128)S(1)}, u32[]{:S(2)}, u32[]{:S(2)}) collective-permute-start(f32[4,128,128]{2,1,0:T(8,128)S(1)} %select_add_fusion.3), channel_id=1, source_target_pairs={{0,4},{1,5},{2,6},{3,7},{16,20},{17,21},{18,22},{19,23}} | collective-permute-start | bytes 786440 | tf_op jit(solution)/shard_map/ppermute | solution.py:283
  27.3 4.3 %collective-permute-done.7 = f32[4,128,128]{2,1,0:T(8,128)S(1)} collective-permute-done((f32[4,128,128]{2,1,0:T(8,128)S(1)}, f32[4,128,128]{2,1,0:T(8,128)S(1)}, u32[]{:S(2)}, u32[]{:S(2)}) %collective-permute-start.7) | collective-permute-done | bytes 262176 | tf_op jit(solution)/shard_map/ppermute | solution.py:283
  31.6 0.8 collective-permute-start.8
  32.5 4.3 %collective-permute-done.2 = f32[4,128,128]{2,1,0:T(8,128)S(1)} collective-permute-done((f32[4,128,128]{2,1,0:T(8,128)S(1)}, f32[4,128,128]{2,1,0:T(8,128)S(1)}, u32[]{:S(2)}, u32[]{:S(2)}) %collective-permute-start.2) | collective-permute-done | bytes 262176 | tf_op jit(solution)/shard_map/ppermute | solution.py:283
  36.8 0.8 collective-permute-start.3
  37.7 0.0 collective-permute-done.8
  37.7 0.0 copy-start.1
  37.8 0.0 copy-start.3
  37.8 0.0 copy-start.6
  37.8 0.8 collective-permute-start.9
  38.6 0.0 collective-permute-done.3
  38.6 0.1 multiply_add_fusion.10
  38.7 0.8 collective-permute-start.4
  39.5 0.0 collective-permute-done.9
  39.5 1.0 fusion.4
  40.5 0.1 collective-permute-start.10
  40.6 0.0 collective-permute-done.4
  40.6 0.1 fusion.6
  40.7 1.5 %collective-permute-start.5 = (f32[4,128,128]{2,1,0:T(8,128)S(1)}, f32[4,128,128]{2,1,0:T(8,128)S(1)}, u32[]{:S(2)}, u32[]{:S(2)}) collective-permute-start(f32[4,128,128]{2,1,0:T(8,128)S(1)} %get-tuple-element.80), channel_id=1, source_target_pairs={{0,1},{1,0},{2,3},{3,2},{4,5},{5,4},{6,7},{7,6},{8,9},{9,8},{10,11... | collective-permute-start | bytes 786440 | tf_op jit(solution)/shard_map/ppermute | solution.py:291
  42.2 0.0 collective-permute-done.10.back_ref
  42.3 8.0 %forward.2 = (bf16[512,2048]{1,0:T(8,128)(2,1)}, bf16[512,2048]{1,0:T(8,128)(2,1)S(1)}, f32[8,3,128,128]{3,2,1,0:T(8,128)S(1)}, f32[4,128,128]{2,1,0:T(8,128)S(1)}, f32[4,128,128]{2,1,0:T(8,128)S(1)}) custom-call(s32[1]{0:T(128)} %bitcast.core_ref, bf16[512,2048]{1,0:T(8,128)(2,1)S(1)} %copy-done.4, bf16[512,2048]{1,0:T(8,128)(2,1)S(1)} %copy-done.1, ...), custom_call_target="tpu_custom_call" | custom-call | flops 536870912 | bytes 8388608 | tf_op jit(solution)/shard_map/forward/pallas_call | solution.py:205
  50.3 0.0 collective-permute-start.16
  50.3 8.0 %forward.3 = (bf16[512,2048]{1,0:T(8,128)(2,1)}, bf16[512,2048]{1,0:T(8,128)(2,1)S(1)}, f32[8,3,128,128]{3,2,1,0:T(8,128)S(1)}, f32[4,128,128]{2,1,0:T(8,128)S(1)}, f32[4,128,128]{2,1,0:T(8,128)S(1)}) custom-call(s32[1]{0:T(128)} %bitcast.core_ref, bf16[512,2048]{1,0:T(8,128)(2,1)S(1)} %copy-done.4, ...), custom_call_target="tpu_custom_call", output_to_operand_aliasing={{0}: (12, {})} | custom-call | flops 536870912 | bytes 8388608 | tf_op jit(solution)/shard_map/forward/pallas_call | solution.py:205
  58.3 0.5 collective-permute-start.11
  58.8 0.0 collective-permute-done.16
  58.9 0.7 collective-permute-start.17
  59.6 0.4 collective-permute-done.11
  60.0 0.7 collective-permute-start.12
  60.8 0.7 collective-permute-start.18
  61.4 0.0 collective-permute-done.12
  61.5 0.7 collective-permute-start.13
  62.2 0.1 multiply_add_fusion.1
  62.3 0.0 copy-start.9
  62.3 1.4 %collective-permute-start.19 = (f32[4,128,128]{2,1,0:T(8,128)S(1)}, f32[4,128,128]{2,1,0:T(8,128)S(1)}, u32[]{:S(2)}, u32[]{:S(2)}) collective-permute-start(f32[4,128,128]{2,1,0:T(8,128)S(1)} %get-tuple-element.60), channel_id=1, source_target_pairs={{4,0},{5,1},{6,2},{7,3},{20,16},{21,17},{22,18},{23,19}} | collective-permute-start | bytes 786440 | tf_op jit(solution)/shard_map/ppermute | solution.py:283
  63.7 0.1 multiply_add_fusion.4
  63.8 1.3 %collective-permute-start.14 = (f32[4,128,128]{2,1,0:T(8,128)S(1)}, f32[4,128,128]{2,1,0:T(8,128)S(1)}, u32[]{:S(2)}, u32[]{:S(2)}) collective-permute-start(f32[4,128,128]{2,1,0:T(8,128)S(1)} %get-tuple-element.62), channel_id=1, source_target_pairs={{4,0},{5,1},{6,2},{7,3},{20,16},{21,17},{22,18},{23,19}} | collective-permute-start | bytes 786440 | tf_op jit(solution)/shard_map/ppermute | solution.py:283
  65.1 32.3 %collective-permute-done.19 = f32[4,128,128]{2,1,0:T(8,128)S(1)} collective-permute-done((f32[4,128,128]{2,1,0:T(8,128)S(1)}, f32[4,128,128]{2,1,0:T(8,128)S(1)}, u32[]{:S(2)}, u32[]{:S(2)}) %collective-permute-start.19) | collective-permute-done | bytes 262176 | tf_op jit(solution)/shard_map/ppermute | solution.py:283
  97.3 0.1 fusion
  97.4 0.1 collective-permute-start.20
  97.5 5.6 %collective-permute-done.14 = f32[4,128,128]{2,1,0:T(8,128)S(1)} collective-permute-done((f32[4,128,128]{2,1,0:T(8,128)S(1)}, f32[4,128,128]{2,1,0:T(8,128)S(1)}, u32[]{:S(2)}, u32[]{:S(2)}) %collective-permute-start.14) | collective-permute-done | bytes 262176 | tf_op jit(solution)/shard_map/ppermute | solution.py:283
  103.2 0.1 fusion.2
  103.2 0.1 collective-permute-start.15
  103.3 0.0 collective-permute-done.20.gback_ref
  103.3 8.3 %backward.2 = (bf16[512,2048]{1,0:T(8,128)(2,1)}, bf16[512,2048]{1,0:T(8,128)(2,1)}, bf16[512,2048]{1,0:T(8,128)(2,1)}) custom-call(s32[1]{0:T(128)} %bitcast.core_ref, bf16[512,2048]{1,0:T(8,128)(2,1)S(1)} %copy-done.4, bf16[512,2048]{1,0:T(8,128)(2,1)S(1)} %copy-done.1, bf16[512,2048]{1,0:T(8,128)(2,1)S(1)} %copy-done.3, ...), custom_call_target="tpu_custom_call" | custom-call | flops 1073741824 | bytes 10485760 | tf_op jit(solution)/shard_map/backward/pallas_call | solution.py:205
  111.6 8.2 %backward.3 = (bf16[512,2048]{1,0:T(8,128)(2,1)}, bf16[512,2048]{1,0:T(8,128)(2,1)}, bf16[512,2048]{1,0:T(8,128)(2,1)}) custom-call(s32[1]{0:T(128)} %bitcast.core_ref, bf16[512,2048]{1,0:T(8,128)(2,1)S(1)} %copy-done.4, bf16[512,2048]{1,0:T(8,128)(2,1)S(1)} %copy-done.1, ...), custom_call_target="tpu_custom_call", output_to_operand_aliasing={{0}: (16, {}), {1}: (17, {}), {2}: (18, {})} | custom-call | flops 1073741824 | bytes 10485760 | tf_op jit(solution)/shard_map/backward/pallas_call | solution.py:205
  (35 shorter events, 0.3 us)
Async XLA Ops:
  3.2 16.0 %collective-permute-start = (f32[16,128]{1,0:T(8,128)}, f32[16,128]{1,0:T(8,128)S(1)}, u32[]{:S(2)}, u32[]{:S(2)}) collective-permute-start(f32[16,128]{1,0:T(8,128)} %get-tuple-element.38), channel_id=1, source_target_pairs={{0,1},{1,0},{2,3},{3,2},{4,5},{5,4},{6,7},{7,6},{8,9},{9,8},{10,11... | collective-permute-start | bytes 24584 | tf_op jit(solution)/shard_map/ppermute | solution.py:254
  3.6 1.6 %copy-start = (bf16[512,2048]{1,0:T(8,128)(2,1)S(1)}, bf16[512,2048]{1,0:T(8,128)(2,1)}, u32[]{:S(2)}) copy-start(bf16[512,2048]{1,0:T(8,128)(2,1)} %k_ref.11) | copy-start | bytes 6291460
  5.2 1.6 %copy-start.2 = (bf16[512,2048]{1,0:T(8,128)(2,1)S(1)}, bf16[512,2048]{1,0:T(8,128)(2,1)}, u32[]{:S(2)}) copy-start(bf16[512,2048]{1,0:T(8,128)(2,1)} %v_ref.11) | copy-start | bytes 6291460
  6.8 0.9 copy-start.8
  7.8 0.8 copy-start.10
  8.6 0.8 copy-start.12
  13.7 0.7 copy-start.14
  14.4 4.9 %copy-start.15 = (f32[16,128]{1,0:T(8,128)S(1)}, f32[16,128]{1,0:T(8,128)}, u32[]{:S(2)}) copy-start(f32[16,128]{1,0:T(8,128)} %get-tuple-element.38) | copy-start | bytes 24580
  14.4 4.9 %collective-permute-start.6 = (f32[4,128,128]{2,1,0:T(8,128)}, f32[4,128,128]{2,1,0:T(8,128)}, u32[]{:S(2)}, u32[]{:S(2)}) collective-permute-start(f32[4,128,128]{2,1,0:T(8,128)} %get-tuple-element.43), channel_id=1, source_target_pairs={{0,1},{1,0},{2,3},{3,2},{4,5},{5,4},{6,7},{7,6},{8,9},{9,8},{10,11... | collective-permute-start | bytes 786440 | tf_op jit(solution)/shard_map/ppermute | solution.py:270
  14.4 27.8 %copy-start.11 = (f32[16,8,128]{2,1,0:T(8,128)S(1)}, f32[16,8,128]{2,1,0:T(8,128)}, u32[]{:S(2)}) copy-start(f32[16,8,128]{2,1,0:T(8,128)} %get-tuple-element.33.table_ref) | copy-start | bytes 196612
  18.7 6.3 %collective-permute-start.1 = (f32[4,128,128]{2,1,0:T(8,128)}, f32[4,128,128]{2,1,0:T(8,128)}, u32[]{:S(2)}, u32[]{:S(2)}) collective-permute-start(f32[4,128,128]{2,1,0:T(8,128)} %get-tuple-element.40), channel_id=1, source_target_pairs={{0,1},{1,0},{2,3},{3,2},{4,5},{5,4},{6,7},{7,6},{8,9},{9,8},{10,11... | collective-permute-start | bytes 786440 | tf_op jit(solution)/shard_map/ppermute | solution.py:270
  19.3 22.9 %copy-start.5 = (bf16[512,2048]{1,0:T(8,128)(2,1)S(1)}, bf16[512,2048]{1,0:T(8,128)(2,1)}, u32[]{:S(2)}) copy-start(bf16[512,2048]{1,0:T(8,128)(2,1)} %og_ref.3) | copy-start | bytes 6291460
  20.5 11.1 %collective-permute-start.7 = (f32[4,128,128]{2,1,0:T(8,128)S(1)}, f32[4,128,128]{2,1,0:T(8,128)S(1)}, u32[]{:S(2)}, u32[]{:S(2)}) collective-permute-start(f32[4,128,128]{2,1,0:T(8,128)S(1)} %select_add_fusion.2), channel_id=1, source_target_pairs={{0,4},{1,5},{2,6},{3,7},{16,20},{17,21},{18,22},{19,23}} | collective-permute-start | bytes 786440 | tf_op jit(solution)/shard_map/ppermute | solution.py:283
  26.0 10.8 %collective-permute-start.2 = (f32[4,128,128]{2,1,0:T(8,128)S(1)}, f32[4,128,128]{2,1,0:T(8,128)S(1)}, u32[]{:S(2)}, u32[]{:S(2)}) collective-permute-start(f32[4,128,128]{2,1,0:T(8,128)S(1)} %select_add_fusion.3), channel_id=1, source_target_pairs={{0,4},{1,5},{2,6},{3,7},{16,20},{17,21},{18,22},{19,23}} | collective-permute-start | bytes 786440 | tf_op jit(solution)/shard_map/ppermute | solution.py:283
  31.6 10.6 %copy-start.7 = (f32[512,128]{1,0:T(8,128)S(1)}, f32[512,128]{1,0:T(8,128)}, u32[]{:S(2)}) copy-start(f32[512,128]{1,0:T(8,128)} %get-tuple-element.35.enter_bias_ref) | copy-start | bytes 786436
  31.6 6.0 %collective-permute-start.8 = (f32[4,128,128]{2,1,0:T(8,128)S(1)}, f32[4,128,128]{2,1,0:T(8,128)S(1)}, u32[]{:S(2)}, u32[]{:S(2)}) collective-permute-start(f32[4,128,128]{2,1,0:T(8,128)S(1)} %multiply_add_fusion.8), channel_id=1, source_target_pairs={{4,8},{5,9},{6,10},{7,11},{20,24},{21,25},{22,26},{23,27}} | collective-permute-start | bytes 786440 | tf_op jit(solution)/shard_map/ppermute | solution.py:283
  36.8 5.4 %copy-start.4 = (bf16[512,2048]{1,0:T(8,128)(2,1)S(1)}, bf16[512,2048]{1,0:T(8,128)(2,1)}, u32[]{:S(2)}) copy-start(bf16[512,2048]{1,0:T(8,128)(2,1)} %q_ref.7) | copy-start | bytes 6291460
  36.8 1.8 %collective-permute-start.3 = (f32[4,128,128]{2,1,0:T(8,128)S(1)}, f32[4,128,128]{2,1,0:T(8,128)S(1)}, u32[]{:S(2)}, u32[]{:S(2)}) collective-permute-start(f32[4,128,128]{2,1,0:T(8,128)S(1)} %multiply_add_fusion.11), channel_id=1, source_target_pairs={{4,8},{5,9},{6,10},{7,11},{20,24},{21,25},{22,26},{23,27}} | collective-permute-start | bytes 786440 | tf_op jit(solution)/shard_map/ppermute | solution.py:283
  37.7 4.5 %copy-start.13 = (f32[16,1,512]{2,1,0:T(1,128)S(1)}, f32[16,1,512]{2,1,0:T(1,128)}, u32[]{:S(2)}) copy-start(f32[16,1,512]{2,1,0:T(1,128)} %get-tuple-element.32.run_ref) | copy-start | bytes 98308
  37.7 4.5 %copy-start.1 = (bf16[512,2048]{1,0:T(8,128)(2,1)S(1)}, bf16[512,2048]{1,0:T(8,128)(2,1)}, u32[]{:S(2)}) copy-start(bf16[512,2048]{1,0:T(8,128)(2,1)} %k_ref.11) | copy-start | bytes 6291460
  37.8 4.5 %copy-start.3 = (bf16[512,2048]{1,0:T(8,128)(2,1)S(1)}, bf16[512,2048]{1,0:T(8,128)(2,1)}, u32[]{:S(2)}) copy-start(bf16[512,2048]{1,0:T(8,128)(2,1)} %v_ref.11) | copy-start | bytes 6291460
  37.8 4.5 %copy-start.6 = (f32[512,128]{1,0:T(8,128)S(1)}, f32[512,128]{1,0:T(8,128)}, u32[]{:S(2)}) copy-start(f32[512,128]{1,0:T(8,128)} %get-tuple-element.34.weight_bias_ref) | copy-start | bytes 786436
  37.8 1.7 %collective-permute-start.9 = (f32[4,128,128]{2,1,0:T(8,128)S(1)}, f32[4,128,128]{2,1,0:T(8,128)S(1)}, u32[]{:S(2)}, u32[]{:S(2)}) collective-permute-start(f32[4,128,128]{2,1,0:T(8,128)S(1)} %get-tuple-element.64), channel_id=1, source_target_pairs={{8,12},{9,13},{10,14},{11,15},{24,28},{25,29},{26,30},{27,31}} | collective-permute-start | bytes 786440 | tf_op jit(solution)/shard_map/ppermute | solution.py:283
  38.7 1.9 %collective-permute-start.4 = (f32[4,128,128]{2,1,0:T(8,128)S(1)}, f32[4,128,128]{2,1,0:T(8,128)S(1)}, u32[]{:S(2)}, u32[]{:S(2)}) collective-permute-start(f32[4,128,128]{2,1,0:T(8,128)S(1)} %get-tuple-element.69), channel_id=1, source_target_pairs={{8,12},{9,13},{10,14},{11,15},{24,28},{25,29},{26,30},{27,31}} | collective-permute-start | bytes 786440 | tf_op jit(solution)/shard_map/ppermute | solution.py:283
  40.5 1.7 %collective-permute-start.10 = (f32[4,128,128]{2,1,0:T(8,128)S(1)}, f32[4,128,128]{2,1,0:T(8,128)S(1)}, u32[]{:S(2)}, u32[]{:S(2)}) collective-permute-start(f32[4,128,128]{2,1,0:T(8,128)S(1)} %get-tuple-element.78), channel_id=1, source_target_pairs={{0,1},{1,0},{2,3},{3,2},{4,5},{5,4},{6,7},{7,6},{8,9},{9,8},{10,11... | collective-permute-start | bytes 786440 | tf_op jit(solution)/shard_map/ppermute | solution.py:291
  40.7 9.7 %collective-permute-start.5 = (f32[4,128,128]{2,1,0:T(8,128)S(1)}, f32[4,128,128]{2,1,0:T(8,128)S(1)}, u32[]{:S(2)}, u32[]{:S(2)}) collective-permute-start(f32[4,128,128]{2,1,0:T(8,128)S(1)} %get-tuple-element.80), channel_id=1, source_target_pairs={{0,1},{1,0},{2,3},{3,2},{4,5},{5,4},{6,7},{7,6},{8,9},{9,8},{10,11... | collective-permute-start | bytes 786440 | tf_op jit(solution)/shard_map/ppermute | solution.py:291
  50.3 8.5 %collective-permute-start.16 = (f32[4,128,128]{2,1,0:T(8,128)S(1)}, f32[4,128,128]{2,1,0:T(8,128)S(1)}, u32[]{:S(2)}, u32[]{:S(2)}) collective-permute-start(f32[4,128,128]{2,1,0:T(8,128)S(1)} %get-tuple-element.52), channel_id=1, source_target_pairs={{0,1},{1,0},{2,3},{3,2},{4,5},{5,4},{6,7},{7,6},{8,9},{9,8},{10,11... | collective-permute-start | bytes 786440 | tf_op jit(solution)/shard_map/ppermute | solution.py:270
  58.3 1.6 %collective-permute-start.11 = (f32[4,128,128]{2,1,0:T(8,128)S(1)}, f32[4,128,128]{2,1,0:T(8,128)S(1)}, u32[]{:S(2)}, u32[]{:S(2)}) collective-permute-start(f32[4,128,128]{2,1,0:T(8,128)S(1)} %get-tuple-element.48), channel_id=1, source_target_pairs={{0,1},{1,0},{2,3},{3,2},{4,5},{5,4},{6,7},{7,6},{8,9},{9,8},{10,11... | collective-permute-start | bytes 786440 | tf_op jit(solution)/shard_map/ppermute | solution.py:270
  58.9 1.8 %collective-permute-start.17 = (f32[4,128,128]{2,1,0:T(8,128)S(1)}, f32[4,128,128]{2,1,0:T(8,128)S(1)}, u32[]{:S(2)}, u32[]{:S(2)}) collective-permute-start(f32[4,128,128]{2,1,0:T(8,128)S(1)} %select_add_fusion), channel_id=1, source_target_pairs={{12,8},{13,9},{14,10},{15,11},{28,24},{29,25},{30,26},{31,27}} | collective-permute-start | bytes 786440 | tf_op jit(solution)/shard_map/ppermute | solution.py:283
  60.0 1.4 %collective-permute-start.12 = (f32[4,128,128]{2,1,0:T(8,128)S(1)}, f32[4,128,128]{2,1,0:T(8,128)S(1)}, u32[]{:S(2)}, u32[]{:S(2)}) collective-permute-start(f32[4,128,128]{2,1,0:T(8,128)S(1)} %select_add_fusion.1), channel_id=1, source_target_pairs={{12,8},{13,9},{14,10},{15,11},{28,24},{29,25},{30,26},{31,27}} | collective-permute-start | bytes 786440 | tf_op jit(solution)/shard_map/ppermute | solution.py:283
  60.8 1.4 %collective-permute-start.18 = (f32[4,128,128]{2,1,0:T(8,128)S(1)}, f32[4,128,128]{2,1,0:T(8,128)S(1)}, u32[]{:S(2)}, u32[]{:S(2)}) collective-permute-start(f32[4,128,128]{2,1,0:T(8,128)S(1)} %multiply_add_fusion.2), channel_id=1, source_target_pairs={{8,4},{9,5},{10,6},{11,7},{24,20},{25,21},{26,22},{27,23}} | collective-permute-start | bytes 786440 | tf_op jit(solution)/shard_map/ppermute | solution.py:283
  61.5 2.2 %collective-permute-start.13 = (f32[4,128,128]{2,1,0:T(8,128)S(1)}, f32[4,128,128]{2,1,0:T(8,128)S(1)}, u32[]{:S(2)}, u32[]{:S(2)}) collective-permute-start(f32[4,128,128]{2,1,0:T(8,128)S(1)} %multiply_add_fusion.5), channel_id=1, source_target_pairs={{8,4},{9,5},{10,6},{11,7},{24,20},{25,21},{26,22},{27,23}} | collective-permute-start | bytes 786440 | tf_op jit(solution)/shard_map/ppermute | solution.py:283
  62.3 41.1 %copy-start.9 = (f32[512,128]{1,0:T(8,128)S(1)}, f32[512,128]{1,0:T(8,128)}, u32[]{:S(2)}) copy-start(f32[512,128]{1,0:T(8,128)} %get-tuple-element.36.leave_bias_ref) | copy-start | bytes 786436
  62.3 35.1 %collective-permute-start.19 = (f32[4,128,128]{2,1,0:T(8,128)S(1)}, f32[4,128,128]{2,1,0:T(8,128)S(1)}, u32[]{:S(2)}, u32[]{:S(2)}) collective-permute-start(f32[4,128,128]{2,1,0:T(8,128)S(1)} %get-tuple-element.60), channel_id=1, source_target_pairs={{4,0},{5,1},{6,2},{7,3},{20,16},{21,17},{22,18},{23,19}} | collective-permute-start | bytes 786440 | tf_op jit(solution)/shard_map/ppermute | solution.py:283
  63.8 39.4 %collective-permute-start.14 = (f32[4,128,128]{2,1,0:T(8,128)S(1)}, f32[4,128,128]{2,1,0:T(8,128)S(1)}, u32[]{:S(2)}, u32[]{:S(2)}) collective-permute-start(f32[4,128,128]{2,1,0:T(8,128)S(1)} %get-tuple-element.62), channel_id=1, source_target_pairs={{4,0},{5,1},{6,2},{7,3},{20,16},{21,17},{22,18},{23,19}} | collective-permute-start | bytes 786440 | tf_op jit(solution)/shard_map/ppermute | solution.py:283
  97.4 5.9 %collective-permute-start.20 = (f32[4,128,128]{2,1,0:T(8,128)S(1)}, f32[4,128,128]{2,1,0:T(8,128)S(1)}, u32[]{:S(2)}, u32[]{:S(2)}) collective-permute-start(f32[4,128,128]{2,1,0:T(8,128)S(1)} %get-tuple-element.74), channel_id=1, source_target_pairs={{0,1},{1,0},{2,3},{3,2},{4,5},{5,4},{6,7},{7,6},{8,9},{9,8},{10,11... | collective-permute-start | bytes 786440 | tf_op jit(solution)/shard_map/ppermute | solution.py:291
  103.2 8.4 %collective-permute-start.15 = (f32[4,128,128]{2,1,0:T(8,128)S(1)}, f32[4,128,128]{2,1,0:T(8,128)S(1)}, u32[]{:S(2)}, u32[]{:S(2)}) collective-permute-start(f32[4,128,128]{2,1,0:T(8,128)S(1)} %get-tuple-element.76), channel_id=1, source_target_pairs={{0,1},{1,0},{2,3},{3,2},{4,5},{5,4},{6,7},{7,6},{8,9},{9,8},{10,11... | collective-permute-start | bytes 786440 | tf_op jit(solution)/shard_map/ppermute | solution.py:291

commit v3 on v2

v3 whole, which is shorter than its diff:
```python
import functools

import jax
import jax.numpy as jnp
from jax import lax
from jax.experimental import pallas as pl
from jax.experimental.pallas import tpu as pltpu
from jax.sharding import PartitionSpec as P

C = 128
EPS = 1e-06
NEG = -1e30
GROUPS = 2
PER_STEP = 2
F32 = jnp.float32
BF16 = jnp.bfloat16
VMEM_LIMIT = 32 * 1024 * 1024
VMEM_ALL = 62 * 1024 * 1024


def dot(a, b):
    return lax.dot_general(a, b, (((1,), (0,)), ((), ())), preferred_element_type=F32)


def dot_t(a, b):
    return lax.dot_general(a, b, (((1,), (1,)), ((), ())), preferred_element_type=F32)


def t_dot(a, b):
    return lax.dot_general(a, b, (((0,), (0,)), ((), ())), preferred_element_type=F32)


def exact_dot(a, b):
    return lax.dot_general(
        a, b, (((1,), (0,)), ((), ())), precision=lax.Precision.HIGHEST, preferred_element_type=F32
    )


def columns(row):
    return jnp.broadcast_to(row, (C, C)).T


def fill_tables(chunks, decay_ref, start_ref, run_ref, table_ref, gain_ref, weight_bias_ref, enter_bias_ref, leave_bias_ref):
    heads = decay_ref.shape[0]
    at_row = lax.broadcasted_iota(jnp.int32, (C, C), 0)
    at_lane = lax.broadcasted_iota(jnp.int32, (C, C), 1)
    upper = jnp.where(at_row <= at_lane, 1.0, 0.0).astype(F32)
    sums = jnp.concatenate([upper, jnp.ones((C, C), F32)], axis=1)
    gain = jnp.ones((heads, C), F32)
    each = range(chunks)
    spans = [pl.ds(j * C, C) for j in each]
    runs = [exact_dot(decay_ref[:, span], sums) for span in spans]
    starts = jnp.concatenate([start_ref[:, span].astype(F32) for span in spans] * (8 // chunks), axis=0)
    docs_all = dot(starts.astype(BF16), sums.astype(BF16))
    for j in each:
        span = spans[j]
        last = runs[j][:, C:]
        docs, docs_last = docs_all[j : j + 1, :C], docs_all[j : j + 1, C:]
        passing = jnp.where(docs_last == 0.0, jnp.exp(last), 0.0)
        gain = gain * passing
        run_ref[:, 0, span] = runs[j][:, :C]
        table_ref[:, j, :] = passing
        table_ref[:, chunks + j, :] = last
        docs_column = columns(docs)
        weight_bias_ref[span, :] = jnp.where((docs_column == docs) & (at_lane <= at_row), 0.0, NEG)
        enter_bias_ref[span, :] = jnp.where(docs_column == 0.0, 0.0, NEG)
        leave_bias_ref[span, :] = jnp.where(docs_column == docs_last, 0.0, NEG)
    gain_ref[...] = gain


def items_of(chunks, per_step):
    return [(i, j, pl.ds(j * C, C), pl.ds(i * C, C)) for i in range(per_step) for j in range(chunks)]


def split_store(dims, mine_ref, other_ref, totals):
    mine = lax.rem(pl.program_id(0), dims.steps) * dims.per_step < dims.quarter

    @pl.when(mine)
    def _():
        for i, total in enumerate(totals):
            mine_ref[i] = total

    @pl.when(jnp.logical_not(mine))
    def _():
        for i, total in enumerate(totals):
            other_ref[i] = total


def split_load(dims, mine_ref, other_ref):
    mine = pl.program_id(0) * dims.per_step < dims.quarter
    return [jnp.where(mine, mine_ref[i], other_ref[i]) for i in range(dims.per_step)]


def state_body(dims, heads_at, k_ref, v_ref, run_ref, table_ref, leave_bias_ref, prefix_ref, mine_ref, other_ref):
    chunks = dims.chunks
    items = items_of(chunks, dims.per_step)
    runs = [columns(run_ref[heads_at + i, :, rows]) for i, j, rows, cols in items]
    leaves = [
        jnp.exp(table_ref[heads_at + i, pl.ds(chunks + j, 1), :] - run + leave_bias_ref[rows, :])
        for run, (i, j, rows, cols) in zip(runs, items)
    ]
    kds = [(k_ref[rows, cols].astype(F32) * leave).astype(BF16) for leave, (i, j, rows, cols) in zip(leaves, items)]
    updates = [t_dot(kd, v_ref[rows, cols]) for kd, (i, j, rows, cols) in zip(kds, items)]
    totals = []
    for i in range(dims.per_step):
        total = None
        for j in range(chunks):
            update = updates[i * chunks + j]
            total = update if total is None else table_ref[heads_at + i, pl.ds(j, 1), :] * total + update
            if j < chunks - 1:
                prefix_ref[i, j] = total
        totals.append(total)
    split_store(dims, mine_ref, other_ref, totals)


def begin_kernel(
    dims, core_ref, decay_ref, start_ref, k_ref, v_ref,
    prefix_ref, mine_ref, other_ref, run_ref, table_ref, gain_ref, weight_bias_ref, enter_bias_ref, leave_bias_ref
):
    @pl.when(pl.program_id(0) == 0)
    def _():
        fill_tables(
            dims.chunks, decay_ref, start_ref, run_ref, table_ref, gain_ref, weight_bias_ref, enter_bias_ref,
            leave_bias_ref,
        )

    heads_at = dims.head(0, pl.program_id(0), core_ref) * dims.per_step
    state_body(dims, heads_at, k_ref, v_ref, run_ref, table_ref, leave_bias_ref, prefix_ref, mine_ref, other_ref)


def entering_states(chunks, i, incoming, table_ref, prefix_ref):
    states, gain = [], None
    for j in range(chunks):
        states.append((incoming if j == 0 else gain * incoming + prefix_ref[i, j - 1]).astype(BF16))
        passing = table_ref[i, j : j + 1, :]
        gain = passing if gain is None else gain * passing
    return states


def leaving_states(chunks, i, outgoing, table_ref, suffix_ref):
    states, gain = [None] * chunks, None
    for j in range(chunks - 1, -1, -1):
        states[j] = (outgoing if j == chunks - 1 else gain * outgoing + suffix_ref[i, j]).astype(BF16)
        passing = table_ref[i, j : j + 1, :]
        gain = passing if gain is None else gain * passing
    return states


def forward_kernel(
    dims, core_ref, q_ref, k_ref, v_ref, og_ref, run_ref, table_ref, weight_bias_ref, enter_bias_ref,
    prefix_ref, keep_ref, back_ref, *rest
):
    normed_ref, grad_ref, suffix_ref, mine_ref, other_ref = rest[-5:]
    chunks = dims.chunks
    items = items_of(chunks, dims.per_step)
    states = []
    for i, incoming in enumerate(split_load(dims, keep_ref, back_ref)):
        states += entering_states(chunks, i, incoming, table_ref, prefix_ref)
    q = [q_ref[rows, cols] for i, j, rows, cols in items]
    scores = [dot_t(a, k_ref[rows, cols]) for a, (i, j, rows, cols) in zip(q, items)]
    outside = [dot(a, b) for a, b in zip(q, states)]
    marks = [run_ref[i, :, rows] for i, j, rows, cols in items]
    runs = [columns(mark) for mark in marks]
    attends = [
        (score * jnp.exp(run - mark + weight_bias_ref[rows, :])).astype(BF16)
        for score, run, mark, (i, j, rows, cols) in zip(scores, runs, marks, items)
    ]
    enters = [jnp.exp(run + enter_bias_ref[rows, :]) for run, (i, j, rows, cols) in zip(runs, items)]
    qds = [(a.astype(F32) * enter).astype(BF16) for a, enter in zip(q, enters)]
    outs = [
        dot(attend, v_ref[rows, cols]) + enter * far
        for attend, enter, far, (i, j, rows, cols) in zip(attends, enters, outside, items)
    ]
    squares = [jnp.mean(out * out, axis=-1, keepdims=True) for out in outs]
    ogs = [og_ref[rows, cols].astype(F32) for i, j, rows, cols in items]
    alongs = [jnp.mean(og * out, axis=-1, keepdims=True) for og, out in zip(ogs, outs)]
    factors = [lax.rsqrt(square + EPS) for square in squares]
    grads = []
    for out, factor, og, along, (i, j, rows, cols) in zip(outs, factors, ogs, alongs, items):
        normed = out * factor
        normed_ref[rows, cols] = normed.astype(BF16)
        grad = (factor * (og - (factor * along) * normed)).astype(BF16)
        grad_ref[rows, cols] = grad
        grads.append(grad)
    parts = [t_dot(qd, grad) for qd, grad in zip(qds, grads)]
    totals = []
    for i in range(dims.per_step):
        total = parts[i * chunks + chunks - 1]
        for j in range(chunks - 2, -1, -1):
            suffix_ref[i, j] = total
            total = table_ref[i, j : j + 1, :] * total + parts[i * chunks + j]
        totals.append(total)
    split_store(dims, mine_ref, other_ref, totals)


def backward_kernel(
    dims, core_ref, q_ref, k_ref, v_ref, g_ref, run_ref, table_ref, weight_bias_ref, enter_bias_ref,
    leave_bias_ref, prefix_ref, suffix_ref, keep_ref, back_ref, gkeep_ref, gback_ref, *rest
):
    dq_ref, dk_ref, dv_ref = rest[-3:]
    chunks = dims.chunks
    items = items_of(chunks, dims.per_step)
    states, gstates = [], []
    for i, incoming in enumerate(split_load(dims, keep_ref, back_ref)):
        states += entering_states(chunks, i, incoming, table_ref, prefix_ref)
    for i, outgoing in enumerate(split_load(dims, gkeep_ref, gback_ref)):
        gstates += leaving_states(chunks, i, outgoing, table_ref, suffix_ref)
    q, k, v, g = ([ref[rows, cols] for i, j, rows, cols in items] for ref in (q_ref, k_ref, v_ref, g_ref))
    n = range(len(items))
    scores = [dot_t(q[x], k[x]) for x in n]
    dscores = [dot_t(g[x], v[x]) for x in n]
    marks = [run_ref[i, :, rows] for i, j, rows, cols in items]
    runs = [columns(mark) for mark in marks]
    weights = [jnp.exp(runs[x] - marks[x] + weight_bias_ref[items[x][2], :]) for x in n]
    attends = [(scores[x] * weights[x]).astype(BF16) for x in n]
    dattends = [(dscores[x] * weights[x]).astype(BF16) for x in n]
    enters = [jnp.exp(runs[x] + enter_bias_ref[items[x][2], :]) for x in n]
    leaves = [
        jnp.exp(table_ref[i, chunks + j : chunks + j + 1, :] - run + leave_bias_ref[rows, :])
        for run, (i, j, rows, cols) in zip(runs, items)
    ]
    for x, (i, j, rows, cols) in enumerate(items):
        dq_ref[rows, cols] = (dot(dattends[x], k[x]) + enters[x] * dot_t(g[x], states[x])).astype(BF16)
    for x, (i, j, rows, cols) in enumerate(items):
        dk_ref[rows, cols] = (t_dot(dattends[x], q[x]) + leaves[x] * dot_t(v[x], gstates[x])).astype(BF16)
    for x, (i, j, rows, cols) in enumerate(items):
        dv_ref[rows, cols] = (t_dot(attends[x], g[x]) + leaves[x] * dot(k[x], gstates[x])).astype(BF16)


def after(value, token):
    return value if token is None else lax.optimization_barrier((value, token))[0]


class Dims:
    def __init__(self, size, per_step, chunks, length, dh, heads):
        self.size, self.per_step, self.chunks = size, per_step, chunks
        self.length, self.dh, self.heads = length, dh, heads
        self.quarter = size // 2
        self.steps = size // per_step

    def head(self, group, p, core_ref):
        return (group + p // self.steps) * self.steps + lax.rem(p + core_ref[0] * (self.steps // 2), self.steps)

    def specs(self, group):
        n, halves = self.per_step, self.steps // 2
        length, dh, chunks = self.length, self.dh, self.chunks
        whole = lambda *shape: pl.BlockSpec(shape, lambda p, c: (0,) * len(shape))
        return dict(
            rows=pl.BlockSpec((length, n * dh), lambda p, c: (0, self.head(group, p, c))),
            run=pl.BlockSpec((n, 1, length), lambda p, c: (self.head(group, p, c), 0, 0)),
            table=pl.BlockSpec((n, 2 * chunks, C), lambda p, c: (self.head(group, p, c), 0, 0)),
            bias=whole(length, C),
            states=pl.BlockSpec((n, chunks - 1, dh, dh), lambda p, c: (p, 0, 0, 0)),
            prefix=pl.BlockSpec((n, chunks - 1, dh, dh), lambda p, c: (p + group * self.steps, 0, 0, 0)),
            mine=pl.BlockSpec((n, dh, dh), lambda p, c: (p // self.steps * halves + jnp.minimum(lax.rem(p, self.steps), halves - 1), 0, 0)),
            other=pl.BlockSpec((n, dh, dh), lambda p, c: (p // self.steps * halves + jnp.maximum(lax.rem(p, self.steps) - halves, 0), 0, 0)),
            decay=whole(self.heads, length),
            start=whole(1, length),
            all_run=whole(self.heads, 1, length),
            all_table=whole(self.heads, 2 * chunks, C),
            all_gain=whole(self.heads, C),
            any=pl.BlockSpec(memory_space=pl.ANY),
        )


def call_heads(dims, core_arg, kernel, group, in_names, out_names, out_shapes, args, name, products, reads, aliases=(), tokens=(), vmem=VMEM_LIMIT, steps=None):
    specs = dims.specs(group)
    extra = [a for a in aliases if a is not None]
    return pl.pallas_call(
        functools.partial(kernel, dims),
        grid_spec=pltpu.PrefetchScalarGridSpec(
            num_scalar_prefetch=1,
            grid=(steps or dims.steps,),
            in_specs=[specs[n] for n in in_names] + [specs["any"]] * (len(extra) + len(tokens)),
            out_specs=[specs[n] for n in out_names],
        ),
        out_shape=out_shapes,
        input_output_aliases={1 + len(in_names) + i: i for i in range(len(extra))},
        compiler_params=pltpu.CompilerParams(
            dimension_semantics=("arbitrary",), vmem_limit_bytes=vmem
        ),
        cost_estimate=pl.CostEstimate(
            flops=products * dims.size * 2 * dims.length * C * dims.dh,
            bytes_accessed=reads * dims.size * dims.length * dims.dh * 2,
            transcendentals=dims.size * dims.length * C,
        ),
        name=name,
    )(core_arg, *args, *extra, *tokens)


def local(query_in, key_in, value_in, log_decay, doc_start, out_grad):
    length, width = query_in.shape
    heads = log_decay.shape[0]
    dh = width // heads
    chunks = length // C
    groups = GROUPS
    size = heads // groups
    quarter = size // 2
    dims = Dims(size, PER_STEP, chunks, length, dh, heads)
    shards = lax.axis_size("seq")
    core = lax.axis_index("ctx")
    first = core == 0
    core_arg = core.astype(jnp.int32).reshape(1)
    swap = [(0, 1), (1, 0)]
    shape = jax.ShapeDtypeStruct
    states_shape = shape((size, chunks - 1, dh, dh), F32)
    part_shape = shape((quarter, dh, dh), F32)
    rows_shape = shape((length, width), BF16)
    bias_shape = shape((length, C), F32)
    call = functools.partial(call_heads, dims, core_arg)

    prefix, mines, others, run, table, gain, weight_bias, enter_bias, leave_bias = call(
        begin_kernel, 0,
        ["decay", "start", "rows", "rows"],
        ["states", "mine", "other", "all_run", "all_table", "all_gain", "bias", "bias", "bias"],
        (
            shape((heads, chunks - 1, dh, dh), F32), shape((heads // 2, dh, dh), F32), shape((heads // 2, dh, dh), F32),
            shape((heads, 1, length), F32), shape((heads, 2 * chunks, C), F32), shape((heads, C), F32),
            bias_shape, bias_shape, bias_shape,
        ),
        (log_decay, doc_start.reshape(1, length), key_in, value_in),
        "begin", 1, 4,
        vmem=VMEM_ALL, steps=groups * dims.steps,
    )
    gain_other = lax.ppermute(gain, "ctx", swap)
    gain0 = jnp.where(first, gain, gain_other)
    gain1 = jnp.where(first, gain_other, gain)

    def pick(array, group):
        start = group * size + core * quarter
        return lax.dynamic_slice_in_dim(array, start, quarter, 0)[:, None, :]

    class Carry:
        def __init__(self, group, mine, other, backward):
            self.backward = backward
            self.g0, self.g1 = pick(gain0, group), pick(gain1, group)
            self.both = self.g0 * self.g1
            self.mine, self.got = mine, lax.ppermute(other, "ctx", swap)
            if backward:
                self.hops = [(k, k - 1) for k in range(shards - 1, 0, -1)]
            else:
                self.hops = [(k, k + 1) for k in range(shards - 1)]
            self.landed = []

        def start(self, token=None):
            got = after(self.got, token)
            self.zero = jnp.where(first, self.mine, got)
            self.one = jnp.where(first, got, self.mine)
            if self.backward:
                self.total = self.g0 * self.one + self.zero
            else:
                self.total = self.g1 * self.zero + self.one

        def hop(self, index, token=None):
            if index == 0:
                self.start(token)
                self.sent = self.total
            else:
                self.settle(token)
                self.sent = self.both * self.state + self.total
            self.landed.append(lax.ppermute(self.sent, "seq", [self.hops[index]]))

        def settle(self, token=None):
            self.landed[-1] = after(self.landed[-1], token)
            self.state = sum(self.landed[1:], self.landed[0])

        def finish(self, token=None):
            self.settle(token)
            state = self.state
            if self.backward:
                inner = self.g1 * state + self.one
                keep, send = jnp.where(first, inner, state), jnp.where(first, state, inner)
            else:
                inner = self.g0 * state + self.zero
                keep, send = jnp.where(first, state, inner), jnp.where(first, inner, state)
            return keep, lax.ppermute(send, "ctx", swap)

    hops = range(shards - 1)
    carries = []
    for group in range(groups):
        part = slice(group * quarter, (group + 1) * quarter)
        carries.append(Carry(group, mines[part], others[part], False))
    token = None
    for index in hops:
        for carry in carries:
            carry.hop(index, token)
            token = carry.sent

    normed = None
    incoming, suffixes, backs = [], [], []
    for group in range(groups):
        incoming.append(carries[group].finish(token))
        normed, grad, suffix, mine, other = call(
            forward_kernel, group,
            ["rows"] * 4 + ["run", "table", "bias", "bias", "prefix", "mine", "other"],
            ["rows", "rows", "states", "mine", "other"],
            (rows_shape, rows_shape, states_shape, part_shape, part_shape),
            (query_in, key_in, value_in, out_grad, run, table, weight_bias, enter_bias, prefix, *incoming[group]),
            "forward", 4, 8,
            aliases=(normed,),
            tokens=[backs[-1].sent] if backs else [],
        )
        token = mine
        suffixes.append((grad, suffix))
        backs.append(Carry(group, mine, other, True))
        if group == 0:
            backs[0].hop(0)
    for index in hops:
        for place, back in enumerate(backs):
            ahead = index + 1 if place == 0 else index
            if ahead in hops:
                back.hop(ahead, token)
                token = back.sent

    grads = (None, None, None)
    for group in range(groups):
        grad, suffix = suffixes[group]
        outgoing = backs[group].finish(token)
        grads = call(
            backward_kernel, group,
            ["rows"] * 4 + ["run", "table", "bias", "bias", "bias", "prefix", "states", "mine", "other", "mine", "other"],
            ["rows", "rows", "rows"],
            (rows_shape, rows_shape, rows_shape),
            (
                query_in, key_in, value_in, grad, run, table, weight_bias, enter_bias, leave_bias,
                prefix, suffix, *incoming[group], *outgoing,
            ),
            "backward", 8, 10,
            aliases=grads,
        )
        token = grads[0]
    return (normed, *grads)


def solution(mesh):
    rows = P(("groups", "seq", "ctx"), "tensor")
    return jax.shard_map(
        local,
        mesh=mesh,
        in_specs=(rows, rows, rows, P("tensor", ("groups", "seq", "ctx")), P(("groups", "seq", "ctx")), rows),
        out_specs=(rows, rows, rows, rows),
        check_vma=False,
    )
```

time: 120 us -> 103 us (0.86)
  Pallas kernels: 43.7 us -> 34.5 us
  waiting for transfers between devices: 47 us -> 43.5 us
  local copies, waits for them, and re-layouts: 6.48 us -> 4.35 us
  other arithmetic: 3.9 us -> 2.58 us
  starting transfers between devices: 17.7 us -> 16.4 us
    pallas_call x7 -> x5, Pallas kernels: 43.7 us -> 34.5 us  [call_heads(): pl.pallas_call(functools.partial(kernel, dims), grid_spec=pltpu.PrefetchS...]
    ppermute x20, waiting for transfers between devices: 47 us -> 43.5 us  [the longest x12 39 us: hop(): self.landed.append(lax.ppermute(self.sent, 'seq', [self.hops[index]]))]
    unnamed x32 -> x24, local copies, waits for them, and re-layouts: 6.48 us -> 3.22 us
    ppermute x20, starting transfers between devices: 17.2 us -> 15.9 us  [the longest x12 14.3 us: hop(): self.landed.append(lax.ppermute(self.sent, 'seq', [self.hops[index]]))]
  transfers between devices with their start and end apart: 21 -> 21, of which waited for: 5 -> 10; matrix products, arithmetic and copies ran while one was open for 3% -> 3% of each run, Pallas kernels for 27% -> 18%
where the time goes in v3:
time: 103 us; the launch traced here: 102 us
  waiting for transfers between devices  43.5 us (42%)
  Pallas kernels  34.5 us (33%)
  starting transfers between devices  16.4 us (16%)
  local copies, waits for them, and re-layouts  4.35 us (4%)
  other arithmetic  2.58 us (3%)
    ppermute x12, waiting for transfers between devices, hop(): self.landed.append(lax.ppermute(self.sent, 'seq', [self.hops[index]]))  39 us
    pallas_call x5, Pallas kernels, call_heads(): pl.pallas_call(functools.partial(kernel, dims), grid_spec=pltpu.PrefetchS...  34.5 us
    ppermute x12, starting transfers between devices, hop(): self.landed.append(lax.ppermute(self.sent, 'seq', [self.hops[index]]))  14.3 us
    unnamed x24, local copies, waits for them, and re-layouts  3.22 us
    ppermute x4, waiting for transfers between devices, finish(): return (keep, lax.ppermute(send, 'ctx', swap))  2.58 us
  transfers between devices with their start and end apart: 21, of which 10 were waited for; matrix products, arithmetic and copies ran while one was open for 3% of the time, Pallas kernels for 18%

profile of v3, /device:TPU:0, one launch (start us, length us, event | category | flops | bytes accessed | tf_op | source)
XLA Modules:
  0.0 102.3 jit_solution(15731963932844565369)
XLA Ops:
  0.6 8.9 %begin.1 = (f32[16,3,128,128]{3,2,1,0:T(8,128)}, f32[8,128,128]{2,1,0:T(8,128)}, f32[8,128,128]{2,1,0:T(8,128)}, f32[16,1,512]{2,1,0:T(1,128)}, f32[16,8,128]{2,...) custom-call(s32[1]{0:T(128)} %bitcast.core_ref, ...), custom_call_target="tpu_custom_call" | custom-call | flops 134217728 | bytes 4194304 | tf_op jit(solution)/shard_map/begin/pallas_call | solution.py:269
  9.6 0.0 copy-start.11
  9.6 0.5 collective-permute-start
  10.1 1.1 %fusion.10 = (f32[4,128,128]{2,1,0:T(8,128)S(1)}, f32[4,128,128]{2,1,0:T(8,128)S(1)}) fusion(f32[8,128,128]{2,1,0:T(8,128)} %get-tuple-element.50), kind=kLoop, calls=%fused_computation.36 | loop fusion | bytes 1048576 | tf_op jit(solution)/shard_map/slice | solution.py:382
  11.2 0.1 collective-permute-start.2
  11.4 0.4 collective-permute-start.1
  11.8 0.0 collective-permute-done
  11.8 0.7 broadcast_select_fusion.2
  12.5 0.3 collective-permute-done.2
  12.8 1.1 %select_add_fusion.3 = f32[4,128,128]{2,1,0:T(8,128)S(1)} fusion(f32[4,128,128]{2,1,0:T(8,128)S(1)} %collective-permute-done.2, f32[8,128,128]{2,1,0:T(8,128)} %get-tuple-element.49, f32[4,128]{1,0:T(4,128)S(1)} %get-tuple-element.95, pred[]{:T(512)S(6)} %eq.3), kind=kLoop, calls=%fused_computation.23 | loop fusion | flops 262144 | bytes 788481 | tf_op jit(solution)/shard_map/add | solution.py:352
  14.0 4.6 %collective-permute-start.4 = (f32[4,128,128]{2,1,0:T(8,128)S(1)}, f32[4,128,128]{2,1,0:T(8,128)S(1)}, u32[]{:S(2)}, u32[]{:S(2)}) collective-permute-start(f32[4,128,128]{2,1,0:T(8,128)S(1)} %select_add_fusion.3), channel_id=1, source_target_pairs={{0,4},{1,5},{2,6},{3,7},{16,20},{17,21},{18,22},{19,23}} | collective-permute-start | bytes 786440 | tf_op jit(solution)/shard_map/ppermute | solution.py:361
  18.6 0.0 collective-permute-done.1
  18.7 1.3 %collective-permute-start.3 = (f32[4,128,128]{2,1,0:T(8,128)S(1)}, f32[4,128,128]{2,1,0:T(8,128)S(1)}, u32[]{:S(2)}, u32[]{:S(2)}) collective-permute-start(f32[4,128,128]{2,1,0:T(8,128)S(1)} %select_add_fusion.2), channel_id=1, source_target_pairs={{0,4},{1,5},{2,6},{3,7},{16,20},{17,21},{18,22},{19,23}} | collective-permute-start | bytes 786440 | tf_op jit(solution)/shard_map/ppermute | solution.py:361
  20.0 5.2 %collective-permute-done.4 = f32[4,128,128]{2,1,0:T(8,128)S(1)} collective-permute-done((f32[4,128,128]{2,1,0:T(8,128)S(1)}, f32[4,128,128]{2,1,0:T(8,128)S(1)}, u32[]{:S(2)}, u32[]{:S(2)}) %collective-permute-start.4) | collective-permute-done | bytes 262176 | tf_op jit(solution)/shard_map/ppermute | solution.py:361
  25.3 0.7 collective-permute-start.6
  26.0 4.3 %collective-permute-done.3 = f32[4,128,128]{2,1,0:T(8,128)S(1)} collective-permute-done((f32[4,128,128]{2,1,0:T(8,128)S(1)}, f32[4,128,128]{2,1,0:T(8,128)S(1)}, u32[]{:S(2)}, u32[]{:S(2)}) %collective-permute-start.3) | collective-permute-done | bytes 262176 | tf_op jit(solution)/shard_map/ppermute | solution.py:361
  30.3 0.0 copy-start
  30.4 0.0 copy-start.1
  30.4 0.8 collective-permute-start.5
  31.2 0.0 collective-permute-done.6
  31.2 0.1 multiply_add_fusion.9
  31.3 0.8 collective-permute-start.8
  32.1 0.0 collective-permute-done.5
  32.1 0.0 collective-permute-done.8
  32.1 0.1 fusion.6
  32.2 0.1 collective-permute-start.9
  32.3 0.7 collective-permute-start.7
  33.0 0.8 collective-permute-done.9.back_ref
  33.9 0.0 copy-start.3
  33.9 1.6 %copy-done.3 = bf16[512,2048]{1,0:T(8,128)(2,1)S(1)} copy-done((bf16[512,2048]{1,0:T(8,128)(2,1)S(1)}, bf16[512,2048]{1,0:T(8,128)(2,1)}, u32[]{:S(2)}) %copy-start.3) | copy-done | bytes 2097176
  35.5 1.6 %copy-done.5 = bf16[512,2048]{1,0:T(8,128)(2,1)S(1)} copy-done((bf16[512,2048]{1,0:T(8,128)(2,1)S(1)}, bf16[512,2048]{1,0:T(8,128)(2,1)}, u32[]{:S(2)}) %copy-start.5) | copy-done | bytes 2097176
  37.1 5.8 %forward.2 = (bf16[512,2048]{1,0:T(8,128)(2,1)}, bf16[512,2048]{1,0:T(8,128)(2,1)S(1)}, f32[8,3,128,128]{3,2,1,0:T(8,128)S(1)}, f32[4,128,128]{2,1,0:T(8,128)S(1)}, f32[4,128,128]{2,1,0:T(8,128)S(1)}) custom-call(s32[1]{0:T(128)} %bitcast.core_ref, bf16[512,2048]{1,0:T(8,128)(2,1)S(1)} %copy-done.3, bf16[512,2048]{1,0:T(8,128)(2,1)S(1)} %copy-done, ...), custom_call_target="tpu_custom_call" | custom-call | flops 536870912 | bytes 8388608 | tf_op jit(solution)/shard_map/forward/pallas_call | solution.py:269
  42.8 0.0 collective-permute-done.7
  42.8 0.1 collective-permute-start.11
  43.0 0.1 fusion.4
  43.0 0.4 collective-permute-start.10
  43.5 0.9 collective-permute-done.11
  44.4 0.7 collective-permute-start.13
  45.1 0.0 collective-permute-done.10.back_ref
  45.1 5.9 %forward.3 = (bf16[512,2048]{1,0:T(8,128)(2,1)}, bf16[512,2048]{1,0:T(8,128)(2,1)S(1)}, f32[8,3,128,128]{3,2,1,0:T(8,128)S(1)}, f32[4,128,128]{2,1,0:T(8,128)S(1)}, f32[4,128,128]{2,1,0:T(8,128)S(1)}) custom-call(s32[1]{0:T(128)} %bitcast.core_ref, bf16[512,2048]{1,0:T(8,128)(2,1)S(1)} %copy-done.3, ...), custom_call_target="tpu_custom_call", output_to_operand_aliasing={{0}: (12, {})} | custom-call | flops 536870912 | bytes 8388608 | tf_op jit(solution)/shard_map/forward/pallas_call | solution.py:269
  51.0 0.2 collective-permute-start.12
  51.1 0.0 collective-permute-done.13
  51.2 0.7 collective-permute-start.15
  51.9 0.7 collective-permute-done.12
  52.6 0.7 collective-permute-start.14
  53.2 0.0 collective-permute-done.15
  53.3 0.1 multiply_add_fusion.4
  53.3 0.0 copy-start.4
  53.3 0.0 collective-permute-done.14
  53.4 0.8 collective-permute-start.16
  54.2 1.3 %collective-permute-start.18 = (f32[4,128,128]{2,1,0:T(8,128)S(1)}, f32[4,128,128]{2,1,0:T(8,128)S(1)}, u32[]{:S(2)}, u32[]{:S(2)}) collective-permute-start(f32[4,128,128]{2,1,0:T(8,128)S(1)} %get-tuple-element.84), channel_id=1, source_target_pairs={{4,0},{5,1},{6,2},{7,3},{20,16},{21,17},{22,18},{23,19}} | collective-permute-start | bytes 786440 | tf_op jit(solution)/shard_map/ppermute | solution.py:361
  55.5 0.0 collective-permute-done.16
  55.6 27.4 %collective-permute-done.18 = f32[4,128,128]{2,1,0:T(8,128)S(1)} collective-permute-done((f32[4,128,128]{2,1,0:T(8,128)S(1)}, f32[4,128,128]{2,1,0:T(8,128)S(1)}, u32[]{:S(2)}, u32[]{:S(2)}) %collective-permute-start.18) | collective-permute-done | bytes 262176 | tf_op jit(solution)/shard_map/ppermute | solution.py:361
  82.9 0.1 fusion.2
  83.0 0.1 collective-permute-start.19
  83.1 1.3 %collective-permute-start.17 = (f32[4,128,128]{2,1,0:T(8,128)S(1)}, f32[4,128,128]{2,1,0:T(8,128)S(1)}, u32[]{:S(2)}, u32[]{:S(2)}) collective-permute-start(f32[4,128,128]{2,1,0:T(8,128)S(1)} %get-tuple-element.82), channel_id=1, source_target_pairs={{4,0},{5,1},{6,2},{7,3},{20,16},{21,17},{22,18},{23,19}} | collective-permute-start | bytes 786440 | tf_op jit(solution)/shard_map/ppermute | solution.py:361
  84.4 0.2 collective-permute-done.19.gback_ref
  84.6 0.0 copy-done.4
  84.6 7.0 %backward.2 = (bf16[512,2048]{1,0:T(8,128)(2,1)}, bf16[512,2048]{1,0:T(8,128)(2,1)}, bf16[512,2048]{1,0:T(8,128)(2,1)}) custom-call(s32[1]{0:T(128)} %bitcast.core_ref, bf16[512,2048]{1,0:T(8,128)(2,1)S(1)} %copy-done.4, bf16[512,2048]{1,0:T(8,128)(2,1)S(1)} %copy-done, bf16[512,2048]{1,0:T(8,128)(2,1)S(1)} %copy-done.1, ...), custom_call_target="tpu_custom_call" | custom-call | flops 1073741824 | bytes 10485760 | tf_op jit(solution)/shard_map/backward/pallas_call | solution.py:269
  91.6 2.1 %collective-permute-done.17 = f32[4,128,128]{2,1,0:T(8,128)S(1)} collective-permute-done((f32[4,128,128]{2,1,0:T(8,128)S(1)}, f32[4,128,128]{2,1,0:T(8,128)S(1)}, u32[]{:S(2)}, u32[]{:S(2)}) %collective-permute-start.17) | collective-permute-done | bytes 262176 | tf_op jit(solution)/shard_map/ppermute | solution.py:361
  93.7 0.1 fusion
  93.8 0.1 collective-permute-start.20
  93.8 1.5 %collective-permute-done.20.gback_ref = f32[4,128,128]{2,1,0:T(8,128)S(1)} collective-permute-done((f32[4,128,128]{2,1,0:T(8,128)S(1)}, f32[4,128,128]{2,1,0:T(8,128)S(1)}, u32[]{:S(2)}, u32[]{:S(2)}) %collective-permute-start.20) | collective-permute-done | bytes 262176 | tf_op jit(solution)/shard_map/ppermute | solution.py:376
  95.4 6.9 %backward.3 = (bf16[512,2048]{1,0:T(8,128)(2,1)}, bf16[512,2048]{1,0:T(8,128)(2,1)}, bf16[512,2048]{1,0:T(8,128)(2,1)}) custom-call(s32[1]{0:T(128)} %bitcast.core_ref, bf16[512,2048]{1,0:T(8,128)(2,1)S(1)} %copy-done.4, bf16[512,2048]{1,0:T(8,128)(2,1)S(1)} %copy-done, ...), custom_call_target="tpu_custom_call", output_to_operand_aliasing={{0}: (16, {}), {1}: (17, {}), {2}: (18, {})} | custom-call | flops 1073741824 | bytes 10485760 | tf_op jit(solution)/shard_map/backward/pallas_call | solution.py:269
  (26 shorter events, 0.4 us)
Async XLA Ops:
  9.6 9.1 %copy-start.11 = (f32[8,128,128]{2,1,0:T(8,128)S(1)}, f32[8,128,128]{2,1,0:T(8,128)}, u32[]{:S(2)}) copy-start(f32[8,128,128]{2,1,0:T(8,128)} %get-tuple-element.49) | copy-start | bytes 1572868
  9.6 2.2 %collective-permute-start = (f32[16,128]{1,0:T(8,128)}, f32[16,128]{1,0:T(8,128)S(1)}, u32[]{:S(2)}, u32[]{:S(2)}) collective-permute-start(f32[16,128]{1,0:T(8,128)} %get-tuple-element.48), channel_id=1, source_target_pairs={{0,1},{1,0},{2,3},{3,2},{4,5},{5,4},{6,7},{7,6},{8,9},{9,8},{10,11... | collective-permute-start | bytes 24584 | tf_op jit(solution)/shard_map/ppermute | solution.py:325
  10.1 23.7 %copy-start.6 = (f32[512,128]{1,0:T(8,128)S(1)}, f32[512,128]{1,0:T(8,128)}, u32[]{:S(2)}) copy-start(f32[512,128]{1,0:T(8,128)} %get-tuple-element.45.weight_bias_ref) | copy-start | bytes 786436
  10.1 23.7 %copy-start.7 = (f32[512,128]{1,0:T(8,128)S(1)}, f32[512,128]{1,0:T(8,128)}, u32[]{:S(2)}) copy-start(f32[512,128]{1,0:T(8,128)} %get-tuple-element.46.enter_bias_ref) | copy-start | bytes 786436
  10.1 23.7 %copy-start.9 = (f32[16,8,128]{2,1,0:T(8,128)S(1)}, f32[16,8,128]{2,1,0:T(8,128)}, u32[]{:S(2)}) copy-start(f32[16,8,128]{2,1,0:T(8,128)} %get-tuple-element.44.table_ref) | copy-start | bytes 196612
  11.2 1.6 %collective-permute-start.2 = (f32[4,128,128]{2,1,0:T(8,128)S(1)}, f32[4,128,128]{2,1,0:T(8,128)S(1)}, u32[]{:S(2)}, u32[]{:S(2)}) collective-permute-start(f32[4,128,128]{2,1,0:T(8,128)S(1)} %get-tuple-element.104), channel_id=1, source_target_pairs={{0,1},{1,0},{2,3},{3,2},{4,5},{5,4},{6,7},{7,6},{8,9},{9,8},{10,11... | collective-permute-start | bytes 786440 | tf_op jit(solution)/shard_map/ppermute | solution.py:338
  11.4 7.3 %collective-permute-start.1 = (f32[4,128,128]{2,1,0:T(8,128)S(1)}, f32[4,128,128]{2,1,0:T(8,128)S(1)}, u32[]{:S(2)}, u32[]{:S(2)}) collective-permute-start(f32[4,128,128]{2,1,0:T(8,128)S(1)} %get-tuple-element.105), channel_id=1, source_target_pairs={{0,1},{1,0},{2,3},{3,2},{4,5},{5,4},{6,7},{7,6},{8,9},{9,8},{10,11... | collective-permute-start | bytes 786440 | tf_op jit(solution)/shard_map/ppermute | solution.py:338
  12.8 21.0 %copy-start.2 = (f32[16,3,128,128]{3,2,1,0:T(8,128)S(1)}, f32[16,3,128,128]{3,2,1,0:T(8,128)}, u32[]{:S(2)}) copy-start(f32[16,3,128,128]{3,2,1,0:T(8,128)} %get-tuple-element.47.prefix_ref) | copy-start | bytes 9437188
  14.0 11.3 %collective-permute-start.4 = (f32[4,128,128]{2,1,0:T(8,128)S(1)}, f32[4,128,128]{2,1,0:T(8,128)S(1)}, u32[]{:S(2)}, u32[]{:S(2)}) collective-permute-start(f32[4,128,128]{2,1,0:T(8,128)S(1)} %select_add_fusion.3), channel_id=1, source_target_pairs={{0,4},{1,5},{2,6},{3,7},{16,20},{17,21},{18,22},{19,23}} | collective-permute-start | bytes 786440 | tf_op jit(solution)/shard_map/ppermute | solution.py:361
  18.7 11.6 %collective-permute-start.3 = (f32[4,128,128]{2,1,0:T(8,128)S(1)}, f32[4,128,128]{2,1,0:T(8,128)S(1)}, u32[]{:S(2)}, u32[]{:S(2)}) collective-permute-start(f32[4,128,128]{2,1,0:T(8,128)S(1)} %select_add_fusion.2), channel_id=1, source_target_pairs={{0,4},{1,5},{2,6},{3,7},{16,20},{17,21},{18,22},{19,23}} | collective-permute-start | bytes 786440 | tf_op jit(solution)/shard_map/ppermute | solution.py:361
  25.3 5.9 %collective-permute-start.6 = (f32[4,128,128]{2,1,0:T(8,128)S(1)}, f32[4,128,128]{2,1,0:T(8,128)S(1)}, u32[]{:S(2)}, u32[]{:S(2)}) collective-permute-start(f32[4,128,128]{2,1,0:T(8,128)S(1)} %multiply_add_fusion.11), channel_id=1, source_target_pairs={{4,8},{5,9},{6,10},{7,11},{20,24},{21,25},{22,26},{23,27}} | collective-permute-start | bytes 786440 | tf_op jit(solution)/shard_map/ppermute | solution.py:361
  30.3 3.5 %copy-start.10 = (f32[16,1,512]{2,1,0:T(1,128)S(1)}, f32[16,1,512]{2,1,0:T(1,128)}, u32[]{:S(2)}) copy-start(f32[16,1,512]{2,1,0:T(1,128)} %get-tuple-element.43.run_ref) | copy-start | bytes 98308
  30.3 3.5 %copy-start = (bf16[512,2048]{1,0:T(8,128)(2,1)S(1)}, bf16[512,2048]{1,0:T(8,128)(2,1)}, u32[]{:S(2)}) copy-start(bf16[512,2048]{1,0:T(8,128)(2,1)} %k_ref.9) | copy-start | bytes 6291460
  30.4 3.5 %copy-start.1 = (bf16[512,2048]{1,0:T(8,128)(2,1)S(1)}, bf16[512,2048]{1,0:T(8,128)(2,1)}, u32[]{:S(2)}) copy-start(bf16[512,2048]{1,0:T(8,128)(2,1)} %v_ref.9) | copy-start | bytes 6291460
  30.4 1.7 %collective-permute-start.5 = (f32[4,128,128]{2,1,0:T(8,128)S(1)}, f32[4,128,128]{2,1,0:T(8,128)S(1)}, u32[]{:S(2)}, u32[]{:S(2)}) collective-permute-start(f32[4,128,128]{2,1,0:T(8,128)S(1)} %multiply_add_fusion.10), channel_id=1, source_target_pairs={{4,8},{5,9},{6,10},{7,11},{20,24},{21,25},{22,26},{23,27}} | collective-permute-start | bytes 786440 | tf_op jit(solution)/shard_map/ppermute | solution.py:361
  31.3 0.9 collective-permute-start.8
  32.2 1.6 %collective-permute-start.9 = (f32[4,128,128]{2,1,0:T(8,128)S(1)}, f32[4,128,128]{2,1,0:T(8,128)S(1)}, u32[]{:S(2)}, u32[]{:S(2)}) collective-permute-start(f32[4,128,128]{2,1,0:T(8,128)S(1)} %get-tuple-element.98), channel_id=1, source_target_pairs={{0,1},{1,0},{2,3},{3,2},{4,5},{5,4},{6,7},{7,6},{8,9},{9,8},{10,11... | collective-permute-start | bytes 786440 | tf_op jit(solution)/shard_map/ppermute | solution.py:376
  32.3 10.5 %collective-permute-start.7 = (f32[4,128,128]{2,1,0:T(8,128)S(1)}, f32[4,128,128]{2,1,0:T(8,128)S(1)}, u32[]{:S(2)}, u32[]{:S(2)}) collective-permute-start(f32[4,128,128]{2,1,0:T(8,128)S(1)} %get-tuple-element.86), channel_id=1, source_target_pairs={{8,12},{9,13},{10,14},{11,15},{24,28},{25,29},{26,30},{27,31}} | collective-permute-start | bytes 786440 | tf_op jit(solution)/shard_map/ppermute | solution.py:361
  33.9 1.6 %copy-start.3 = (bf16[512,2048]{1,0:T(8,128)(2,1)S(1)}, bf16[512,2048]{1,0:T(8,128)(2,1)}, u32[]{:S(2)}) copy-start(bf16[512,2048]{1,0:T(8,128)(2,1)} %q_ref.7) | copy-start | bytes 6291460
  35.5 1.6 %copy-start.5 = (bf16[512,2048]{1,0:T(8,128)(2,1)S(1)}, bf16[512,2048]{1,0:T(8,128)(2,1)}, u32[]{:S(2)}) copy-start(bf16[512,2048]{1,0:T(8,128)(2,1)} %og_ref.3) | copy-start | bytes 6291460
  42.8 1.5 %collective-permute-start.11 = (f32[4,128,128]{2,1,0:T(8,128)S(1)}, f32[4,128,128]{2,1,0:T(8,128)S(1)}, u32[]{:S(2)}, u32[]{:S(2)}) collective-permute-start(f32[4,128,128]{2,1,0:T(8,128)S(1)} %get-tuple-element.60), channel_id=1, source_target_pairs={{0,1},{1,0},{2,3},{3,2},{4,5},{5,4},{6,7},{7,6},{8,9},{9,8},{10,11... | collective-permute-start | bytes 786440 | tf_op jit(solution)/shard_map/ppermute | solution.py:338
  43.0 2.1 %collective-permute-start.10 = (f32[4,128,128]{2,1,0:T(8,128)S(1)}, f32[4,128,128]{2,1,0:T(8,128)S(1)}, u32[]{:S(2)}, u32[]{:S(2)}) collective-permute-start(f32[4,128,128]{2,1,0:T(8,128)S(1)} %get-tuple-element.96), channel_id=1, source_target_pairs={{0,1},{1,0},{2,3},{3,2},{4,5},{5,4},{6,7},{7,6},{8,9},{9,8},{10,11... | collective-permute-start | bytes 786440 | tf_op jit(solution)/shard_map/ppermute | solution.py:376
  44.4 6.7 %collective-permute-start.13 = (f32[4,128,128]{2,1,0:T(8,128)S(1)}, f32[4,128,128]{2,1,0:T(8,128)S(1)}, u32[]{:S(2)}, u32[]{:S(2)}) collective-permute-start(f32[4,128,128]{2,1,0:T(8,128)S(1)} %select_add_fusion.1.rest_1_), channel_id=1, source_target_pairs={{12,8},{13,9},{14,10},{15,11},{28,24},{29,25},{30,26},{31,27}} | collective-permute-start | bytes 786440 | tf_op jit(solution)/shard_map/ppermute | solution.py:361
  51.0 1.5 %collective-permute-start.12 = (f32[4,128,128]{2,1,0:T(8,128)S(1)}, f32[4,128,128]{2,1,0:T(8,128)S(1)}, u32[]{:S(2)}, u32[]{:S(2)}) collective-permute-start(f32[4,128,128]{2,1,0:T(8,128)S(1)} %get-tuple-element.65), channel_id=1, source_target_pairs={{0,1},{1,0},{2,3},{3,2},{4,5},{5,4},{6,7},{7,6},{8,9},{9,8},{10,11... | collective-permute-start | bytes 786440 | tf_op jit(solution)/shard_map/ppermute | solution.py:338
  51.2 2.1 %collective-permute-start.15 = (f32[4,128,128]{2,1,0:T(8,128)S(1)}, f32[4,128,128]{2,1,0:T(8,128)S(1)}, u32[]{:S(2)}, u32[]{:S(2)}) collective-permute-start(f32[4,128,128]{2,1,0:T(8,128)S(1)} %multiply_add_fusion.5), channel_id=1, source_target_pairs={{8,4},{9,5},{10,6},{11,7},{24,20},{25,21},{26,22},{27,23}} | collective-permute-start | bytes 786440 | tf_op jit(solution)/shard_map/ppermute | solution.py:361
  52.6 0.8 collective-permute-start.14
  53.3 31.3 %copy-start.4 = (bf16[512,2048]{1,0:T(8,128)(2,1)S(1)}, bf16[512,2048]{1,0:T(8,128)(2,1)}, u32[]{:S(2)}) copy-start(bf16[512,2048]{1,0:T(8,128)(2,1)} %q_ref.7) | copy-start | bytes 6291460
  53.3 31.3 %copy-start.8 = (f32[512,128]{1,0:T(8,128)S(1)}, f32[512,128]{1,0:T(8,128)}, u32[]{:S(2)}) copy-start(f32[512,128]{1,0:T(8,128)} %get-tuple-element.63.leave_bias_ref) | copy-start | bytes 786436
  53.4 2.1 %collective-permute-start.16 = (f32[4,128,128]{2,1,0:T(8,128)S(1)}, f32[4,128,128]{2,1,0:T(8,128)S(1)}, u32[]{:S(2)}, u32[]{:S(2)}) collective-permute-start(f32[4,128,128]{2,1,0:T(8,128)S(1)} %multiply_add_fusion.3), channel_id=1, source_target_pairs={{8,4},{9,5},{10,6},{11,7},{24,20},{25,21},{26,22},{27,23}} | collective-permute-start | bytes 786440 | tf_op jit(solution)/shard_map/ppermute | solution.py:361
  54.2 28.7 %collective-permute-start.18 = (f32[4,128,128]{2,1,0:T(8,128)S(1)}, f32[4,128,128]{2,1,0:T(8,128)S(1)}, u32[]{:S(2)}, u32[]{:S(2)}) collective-permute-start(f32[4,128,128]{2,1,0:T(8,128)S(1)} %get-tuple-element.84), channel_id=1, source_target_pairs={{4,0},{5,1},{6,2},{7,3},{20,16},{21,17},{22,18},{23,19}} | collective-permute-start | bytes 786440 | tf_op jit(solution)/shard_map/ppermute | solution.py:361
  83.0 1.6 %collective-permute-start.19 = (f32[4,128,128]{2,1,0:T(8,128)S(1)}, f32[4,128,128]{2,1,0:T(8,128)S(1)}, u32[]{:S(2)}, u32[]{:S(2)}) collective-permute-start(f32[4,128,128]{2,1,0:T(8,128)S(1)} %get-tuple-element.102), channel_id=1, source_target_pairs={{0,1},{1,0},{2,3},{3,2},{4,5},{5,4},{6,7},{7,6},{8,9},{9,8},{10,11... | collective-permute-start | bytes 786440 | tf_op jit(solution)/shard_map/ppermute | solution.py:376
  83.1 10.6 %collective-permute-start.17 = (f32[4,128,128]{2,1,0:T(8,128)S(1)}, f32[4,128,128]{2,1,0:T(8,128)S(1)}, u32[]{:S(2)}, u32[]{:S(2)}) collective-permute-start(f32[4,128,128]{2,1,0:T(8,128)S(1)} %get-tuple-element.82), channel_id=1, source_target_pairs={{4,0},{5,1},{6,2},{7,3},{20,16},{21,17},{22,18},{23,19}} | collective-permute-start | bytes 786440 | tf_op jit(solution)/shard_map/ppermute | solution.py:361
  93.8 1.6 %collective-permute-start.20 = (f32[4,128,128]{2,1,0:T(8,128)S(1)}, f32[4,128,128]{2,1,0:T(8,128)S(1)}, u32[]{:S(2)}, u32[]{:S(2)}) collective-permute-start(f32[4,128,128]{2,1,0:T(8,128)S(1)} %get-tuple-element.100), channel_id=1, source_target_pairs={{0,1},{1,0},{2,3},{3,2},{4,5},{5,4},{6,7},{7,6},{8,9},{9,8},{10,11... | collective-permute-start | bytes 786440 | tf_op jit(solution)/shard_map/ppermute | solution.py:376

commit v4 on v3

--- a/solution.py
+++ b/solution.py
@@ -14,8 +14,7 @@
 PER_STEP = 2
 F32 = jnp.float32
 BF16 = jnp.bfloat16
-VMEM_LIMIT = 32 * 1024 * 1024
-VMEM_ALL = 62 * 1024 * 1024
+VMEM_LIMIT = 20 * 1024 * 1024
 
 
 def dot(a, b):
@@ -73,7 +72,7 @@
 
 
 def split_store(dims, mine_ref, other_ref, totals):
-    mine = lax.rem(pl.program_id(0), dims.steps) * dims.per_step < dims.quarter
+    mine = pl.program_id(0) * dims.per_step < dims.quarter
 
     @pl.when(mine)
     def _():
@@ -91,41 +90,77 @@
     return [jnp.where(mine, mine_ref[i], other_ref[i]) for i in range(dims.per_step)]
 
 
-def state_body(dims, heads_at, k_ref, v_ref, run_ref, table_ref, leave_bias_ref, prefix_ref, mine_ref, other_ref):
+def leaving_decay(chunks, head, j, run, rows, table_ref, leave_bias_ref):
+    return jnp.exp(table_ref[head, pl.ds(chunks + j, 1), :] - run + leave_bias_ref[rows, :])
+
+
+def begin_kernel(dims, core_ref, own, *rest):
+    updates_refs = rest[:-6]
+    run_ref, table_ref, gain_ref, weight_bias_ref, enter_bias_ref, leave_bias_ref = rest[-6:]
     chunks = dims.chunks
+    p = pl.program_id(0)
+
+    @pl.when(p == 0)
+    def _():
+        fill_tables(
+            chunks, *own.plain, run_ref, table_ref, gain_ref, weight_bias_ref, enter_bias_ref, leave_bias_ref
+        )
+
+    k_ref, v_ref = own()[2:]
+    first = dims.head(0, p, core_ref) * dims.per_step
     items = items_of(chunks, dims.per_step)
-    runs = [columns(run_ref[heads_at + i, :, rows]) for i, j, rows, cols in items]
+    runs = [columns(run_ref[first + i, :, rows]) for i, j, rows, cols in items]
     leaves = [
-        jnp.exp(table_ref[heads_at + i, pl.ds(chunks + j, 1), :] - run + leave_bias_ref[rows, :])
+        leaving_decay(chunks, first + i, j, run, rows, table_ref, leave_bias_ref)
         for run, (i, j, rows, cols) in zip(runs, items)
     ]
     kds = [(k_ref[rows, cols].astype(F32) * leave).astype(BF16) for leave, (i, j, rows, cols) in zip(leaves, items)]
     updates = [t_dot(kd, v_ref[rows, cols]) for kd, (i, j, rows, cols) in zip(kds, items)]
     totals = []
     for i in range(dims.per_step):
+        total = updates[i * chunks]
+        for j in range(1, chunks):
+            total = table_ref[first + i, pl.ds(j, 1), :] * total + updates[i * chunks + j]
+        totals.append(total)
+    for at, ref in enumerate(updates_refs):
+
+        @pl.when(p // (dims.steps // 2) == at)
+        def _():
+            for i, total in enumerate(totals):
+                ref[i] = total
+
+
+def inside_kernel(dims, core_ref, own, *rest):
+    q_ref, k_ref, v_ref, run_ref, table_ref, weight_bias_ref, enter_bias_ref, leave_bias_ref = own()
+    prefix_ref, inside_ref, qd_ref, kd_ref, vd_ref, attend_ref = rest[-6:]
+    chunks = dims.chunks
+    items = items_of(chunks, dims.per_step)
+    q, k, v = ([ref[rows, cols] for i, j, rows, cols in items] for ref in (q_ref, k_ref, v_ref))
+    scores = [dot_t(a, b) for a, b in zip(q, k)]
+    marks = [run_ref[i, :, rows] for i, j, rows, cols in items]
+    runs = [columns(mark) for mark in marks]
+    leaves = [
+        leaving_decay(chunks, i, j, run, rows, table_ref, leave_bias_ref)
+        for run, (i, j, rows, cols) in zip(runs, items)
+    ]
+    kds = [(a.astype(F32) * leave).astype(BF16) for a, leave in zip(k, leaves)]
+    attends = [
+        (score * jnp.exp(run - mark + weight_bias_ref[rows, :])).astype(BF16)
+        for score, run, mark, (i, j, rows, cols) in zip(scores, runs, marks, items)
+    ]
+    updates = [t_dot(kd, b) for kd, b in zip(kds, v)]
+    for x, (i, j, rows, cols) in enumerate(items):
+        inside_ref[i, rows, :] = dot(attends[x], v[x])
+        attend_ref[i, rows, :] = attends[x].T
+        kd_ref[i, rows, :] = kds[x]
+        vd_ref[i, rows, :] = (v[x].astype(F32) * leaves[x]).astype(BF16)
+        qd_ref[i, rows, :] = (q[x].astype(F32) * jnp.exp(runs[x] + enter_bias_ref[rows, :])).astype(BF16)
+    for i in range(dims.per_step):
         total = None
-        for j in range(chunks):
+        for j in range(chunks - 1):
             update = updates[i * chunks + j]
-            total = update if total is None else table_ref[heads_at + i, pl.ds(j, 1), :] * total + update
-            if j < chunks - 1:
-                prefix_ref[i, j] = total
-        totals.append(total)
-    split_store(dims, mine_ref, other_ref, totals)
-
-
-def begin_kernel(
-    dims, core_ref, decay_ref, start_ref, k_ref, v_ref,
-    prefix_ref, mine_ref, other_ref, run_ref, table_ref, gain_ref, weight_bias_ref, enter_bias_ref, leave_bias_ref
-):
-    @pl.when(pl.program_id(0) == 0)
-    def _():
-        fill_tables(
-            dims.chunks, decay_ref, start_ref, run_ref, table_ref, gain_ref, weight_bias_ref, enter_bias_ref,
-            leave_bias_ref,
-        )
-
-    heads_at = dims.head(0, pl.program_id(0), core_ref) * dims.per_step
-    state_body(dims, heads_at, k_ref, v_ref, run_ref, table_ref, leave_bias_ref, prefix_ref, mine_ref, other_ref)
+            total = update if total is None else table_ref[i, j : j + 1, :] * total + update
+            prefix_ref[i, j] = total
 
 
 def entering_states(chunks, i, incoming, table_ref, prefix_ref):
@@ -146,30 +181,16 @@
     return states
 
 
-def forward_kernel(
-    dims, core_ref, q_ref, k_ref, v_ref, og_ref, run_ref, table_ref, weight_bias_ref, enter_bias_ref,
-    prefix_ref, keep_ref, back_ref, *rest
-):
+def forward_kernel(dims, core_ref, own, *rest):
+    inside_ref, qd_ref, og_ref, table_ref, prefix_ref, keep_ref, back_ref = own()
     normed_ref, grad_ref, suffix_ref, mine_ref, other_ref = rest[-5:]
     chunks = dims.chunks
     items = items_of(chunks, dims.per_step)
     states = []
     for i, incoming in enumerate(split_load(dims, keep_ref, back_ref)):
         states += entering_states(chunks, i, incoming, table_ref, prefix_ref)
-    q = [q_ref[rows, cols] for i, j, rows, cols in items]
-    scores = [dot_t(a, k_ref[rows, cols]) for a, (i, j, rows, cols) in zip(q, items)]
-    outside = [dot(a, b) for a, b in zip(q, states)]
-    marks = [run_ref[i, :, rows] for i, j, rows, cols in items]
-    runs = [columns(mark) for mark in marks]
-    attends = [
-        (score * jnp.exp(run - mark + weight_bias_ref[rows, :])).astype(BF16)
-        for score, run, mark, (i, j, rows, cols) in zip(scores, runs, marks, items)
-    ]
-    enters = [jnp.exp(run + enter_bias_ref[rows, :]) for run, (i, j, rows, cols) in zip(runs, items)]
-    qds = [(a.astype(F32) * enter).astype(BF16) for a, enter in zip(q, enters)]
     outs = [
-        dot(attend, v_ref[rows, cols]) + enter * far
-        for attend, enter, far, (i, j, rows, cols) in zip(attends, enters, outside, items)
+        inside_ref[i, rows, :] + dot(qd_ref[i, rows, :], state) for state, (i, j, rows, cols) in zip(states, items)
     ]
     squares = [jnp.mean(out * out, axis=-1, keepdims=True) for out in outs]
     ogs = [og_ref[rows, cols].astype(F32) for i, j, rows, cols in items]
@@ -180,9 +201,9 @@
         normed = out * factor
         normed_ref[rows, cols] = normed.astype(BF16)
         grad = (factor * (og - (factor * along) * normed)).astype(BF16)
-        grad_ref[rows, cols] = grad
+        grad_ref[i, rows, :] = grad
         grads.append(grad)
-    parts = [t_dot(qd, grad) for qd, grad in zip(qds, grads)]
+    parts = [t_dot(qd_ref[i, rows, :], grad) for grad, (i, j, rows, cols) in zip(grads, items)]
     totals = []
     for i in range(dims.per_step):
         total = parts[i * chunks + chunks - 1]
@@ -193,38 +214,46 @@
     split_store(dims, mine_ref, other_ref, totals)
 
 
-def backward_kernel(
-    dims, core_ref, q_ref, k_ref, v_ref, g_ref, run_ref, table_ref, weight_bias_ref, enter_bias_ref,
-    leave_bias_ref, prefix_ref, suffix_ref, keep_ref, back_ref, gkeep_ref, gback_ref, *rest
-):
-    dq_ref, dk_ref, dv_ref = rest[-3:]
+def query_kernel(dims, core_ref, own, *rest):
+    (
+        k_ref, v_ref, grad_ref, run_ref, table_ref, weight_bias_ref, enter_bias_ref, prefix_ref, keep_ref, back_ref
+    ) = own()
+    dq_ref, dattend_ref = rest[-2:]
     chunks = dims.chunks
     items = items_of(chunks, dims.per_step)
-    states, gstates = [], []
+    states = []
     for i, incoming in enumerate(split_load(dims, keep_ref, back_ref)):
         states += entering_states(chunks, i, incoming, table_ref, prefix_ref)
-    for i, outgoing in enumerate(split_load(dims, gkeep_ref, gback_ref)):
-        gstates += leaving_states(chunks, i, outgoing, table_ref, suffix_ref)
-    q, k, v, g = ([ref[rows, cols] for i, j, rows, cols in items] for ref in (q_ref, k_ref, v_ref, g_ref))
-    n = range(len(items))
-    scores = [dot_t(q[x], k[x]) for x in n]
-    dscores = [dot_t(g[x], v[x]) for x in n]
+    grads = [grad_ref[i, rows, :] for i, j, rows, cols in items]
+    scores = [dot_t(grad, v_ref[rows, cols]) for grad, (i, j, rows, cols) in zip(grads, items)]
     marks = [run_ref[i, :, rows] for i, j, rows, cols in items]
     runs = [columns(mark) for mark in marks]
-    weights = [jnp.exp(runs[x] - marks[x] + weight_bias_ref[items[x][2], :]) for x in n]
-    attends = [(scores[x] * weights[x]).astype(BF16) for x in n]
-    dattends = [(dscores[x] * weights[x]).astype(BF16) for x in n]
-    enters = [jnp.exp(runs[x] + enter_bias_ref[items[x][2], :]) for x in n]
-    leaves = [
-        jnp.exp(table_ref[i, chunks + j : chunks + j + 1, :] - run + leave_bias_ref[rows, :])
-        for run, (i, j, rows, cols) in zip(runs, items)
+    dattends = [
+        (score * jnp.exp(run - mark + weight_bias_ref[rows, :])).astype(BF16)
+        for score, run, mark, (i, j, rows, cols) in zip(scores, runs, marks, items)
     ]
+    enters = [jnp.exp(run + enter_bias_ref[rows, :]) for run, (i, j, rows, cols) in zip(runs, items)]
     for x, (i, j, rows, cols) in enumerate(items):
-        dq_ref[rows, cols] = (dot(dattends[x], k[x]) + enters[x] * dot_t(g[x], states[x])).astype(BF16)
-    for x, (i, j, rows, cols) in enumerate(items):
-        dk_ref[rows, cols] = (t_dot(dattends[x], q[x]) + leaves[x] * dot_t(v[x], gstates[x])).astype(BF16)
-    for x, (i, j, rows, cols) in enumerate(items):
-        dv_ref[rows, cols] = (t_dot(attends[x], g[x]) + leaves[x] * dot(k[x], gstates[x])).astype(BF16)
+        dattend_ref[i, rows, :] = dattends[x].T
+        dq = dot(dattends[x], k_ref[rows, cols]) + enters[x] * dot_t(grads[x], states[x])
+        dq_ref[rows, cols] = dq.astype(BF16)
+
+
+def backward_kernel(dims, core_ref, own, *rest):
+    (
+        q_ref, grad_ref, attend_ref, dattend_ref, kd_ref, vd_ref, table_ref, suffix_ref, gkeep_ref, gback_ref
+    ) = own()
+    dk_ref, dv_ref = rest[-2:]
+    chunks = dims.chunks
+    items = items_of(chunks, dims.per_step)
+    states = []
+    for i, outgoing in enumerate(split_load(dims, gkeep_ref, gback_ref)):
+        states += leaving_states(chunks, i, outgoing, table_ref, suffix_ref)
+    for state, (i, j, rows, cols) in zip(states, items):
+        dk = dot(dattend_ref[i, rows, :], q_ref[rows, cols]) + dot_t(vd_ref[i, rows, :], state)
+        dk_ref[rows, cols] = dk.astype(BF16)
+        dv = dot(attend_ref[i, rows, :], grad_ref[i, rows, :]) + dot(kd_ref[i, rows, :], state)
+        dv_ref[rows, cols] = dv.astype(BF16)
 
 
 def after(value, token):
@@ -251,9 +280,13 @@
             table=pl.BlockSpec((n, 2 * chunks, C), lambda p, c: (self.head(group, p, c), 0, 0)),
             bias=whole(length, C),
             states=pl.BlockSpec((n, chunks - 1, dh, dh), lambda p, c: (p, 0, 0, 0)),
-            prefix=pl.BlockSpec((n, chunks - 1, dh, dh), lambda p, c: (p + group * self.steps, 0, 0, 0)),
-            mine=pl.BlockSpec((n, dh, dh), lambda p, c: (p // self.steps * halves + jnp.minimum(lax.rem(p, self.steps), halves - 1), 0, 0)),
-            other=pl.BlockSpec((n, dh, dh), lambda p, c: (p // self.steps * halves + jnp.maximum(lax.rem(p, self.steps) - halves, 0), 0, 0)),
+            headed=pl.BlockSpec((n, length, dh), lambda p, c: (p, 0, 0)),
+            update=[
+                pl.BlockSpec((n, dh, dh), lambda p, c, at=at: (jnp.clip(p - at * halves, 0, halves - 1), 0, 0))
+                for at in range(2 * self.heads // self.size)
+            ],
+            mine=pl.BlockSpec((n, dh, dh), lambda p, c: (jnp.minimum(p, halves - 1), 0, 0)),
+            other=pl.BlockSpec((n, dh, dh), lambda p, c: (jnp.maximum(p - halves, 0), 0, 0)),
             decay=whole(self.heads, length),
             start=whole(1, length),
             all_run=whole(self.heads, 1, length),
@@ -263,21 +296,56 @@
         )
 
 
-def call_heads(dims, core_arg, kernel, group, in_names, out_names, out_shapes, args, name, products, reads, aliases=(), tokens=(), vmem=VMEM_LIMIT, steps=None):
+def with_rows(kernel, dims, group, which, inputs, core_ref, *refs):
+    count = len(which)
+    slots, sems = refs[len(refs) - 2 * count : len(refs) - count], refs[len(refs) - count :]
+    refs = list(refs[: len(refs) - 2 * count])
+    p = pl.program_id(0)
+    width = dims.per_step * dims.dh
+
+    def copy(x, step):
+        start = pl.multiple_of(dims.head(group, step, core_ref) * width, width)
+        return pltpu.make_async_copy(refs[which[x]].at[:, pl.ds(start, width)], slots[x].at[step], sems[x].at[step])
+
+    @pl.when(p == 0)
+    def _():
+        for step in range(slots[0].shape[0]):
+            for x in range(count):
+                copy(x, step).start()
+
+    def own():
+        for x in range(count):
+            copy(x, p).wait()
+        return [slots[which.index(y)].at[p] if y in which else refs[y] for y in range(inputs)]
+
+    own.plain = [refs[y] for y in range(inputs) if y not in which]
+    kernel(dims, core_ref, own, *refs[inputs:])
+
+
+def call_heads(
+    dims, core_arg, kernel, group, in_names, out_names, out_shapes, args, name, products, reads, aliases=(), tokens=(),
+    steps=None, stay=(),
+):
     specs = dims.specs(group)
+    steps = steps or dims.steps
     extra = [a for a in aliases if a is not None]
+    which = [x for x, n in enumerate(in_names) if n == "rows"]
+    args = [pltpu.with_memory_space_constraint(a, pltpu.HBM) if n in stay else a for n, a in zip(in_names, args)]
+    in_specs = [pl.BlockSpec(memory_space=pltpu.HBM) if n == "rows" else specs[n] for n in in_names]
     return pl.pallas_call(
-        functools.partial(kernel, dims),
+        functools.partial(with_rows, kernel, dims, group, which, len(in_names)),
         grid_spec=pltpu.PrefetchScalarGridSpec(
             num_scalar_prefetch=1,
-            grid=(steps or dims.steps,),
-            in_specs=[specs[n] for n in in_names] + [specs["any"]] * (len(extra) + len(tokens)),
-            out_specs=[specs[n] for n in out_names],
+            grid=(steps,),
+            in_specs=in_specs + [specs["any"]] * (len(extra) + len(tokens)),
+            out_specs=[s for n in out_names for s in (specs[n] if n == "update" else [specs[n]])],
+            scratch_shapes=[pltpu.VMEM((steps, dims.length, dims.per_step * dims.dh), BF16) for _ in which]
+            + [pltpu.SemaphoreType.DMA((steps,)) for _ in which],
         ),
         out_shape=out_shapes,
         input_output_aliases={1 + len(in_names) + i: i for i in range(len(extra))},
         compiler_params=pltpu.CompilerParams(
-            dimension_semantics=("arbitrary",), vmem_limit_bytes=vmem
+            dimension_semantics=("arbitrary",), vmem_limit_bytes=VMEM_LIMIT
         ),
         cost_estimate=pl.CostEstimate(
             flops=products * dims.size * 2 * dims.length * C * dims.dh,
@@ -309,18 +377,20 @@
     bias_shape = shape((length, C), F32)
     call = functools.partial(call_heads, dims, core_arg)
 
-    prefix, mines, others, run, table, gain, weight_bias, enter_bias, leave_bias = call(
+    headed = lambda kind: shape((size, length, dh), kind)
+    *updates, run, table, gain, weight_bias, enter_bias, leave_bias = call(
         begin_kernel, 0,
         ["decay", "start", "rows", "rows"],
-        ["states", "mine", "other", "all_run", "all_table", "all_gain", "bias", "bias", "bias"],
+        ["update", "all_run", "all_table", "all_gain", "bias", "bias", "bias"],
         (
-            shape((heads, chunks - 1, dh, dh), F32), shape((heads // 2, dh, dh), F32), shape((heads // 2, dh, dh), F32),
+            *[part_shape] * (2 * groups),
             shape((heads, 1, length), F32), shape((heads, 2 * chunks, C), F32), shape((heads, C), F32),
             bias_shape, bias_shape, bias_shape,
         ),
         (log_decay, doc_start.reshape(1, length), key_in, value_in),
         "begin", 1, 4,
-        vmem=VMEM_ALL, steps=groups * dims.steps,
+        steps=groups * dims.steps,
+        stay=("rows", "decay", "start"),
     )
     gain_other = lax.ppermute(gain, "ctx", swap)
     gain0 = jnp.where(first, gain, gain_other)
@@ -375,61 +445,94 @@
                 keep, send = jnp.where(first, state, inner), jnp.where(first, inner, state)
             return keep, lax.ppermute(send, "ctx", swap)
 
+    def inside_of(group, token):
+        return call(
+            inside_kernel, group,
+            ["rows"] * 3 + ["run", "table", "bias", "bias", "bias"],
+            ["states"] + ["headed"] * 5,
+            (states_shape, headed(F32), headed(BF16), headed(BF16), headed(BF16), headed(BF16)),
+            (query_in, key_in, value_in, run, table, weight_bias, enter_bias, leave_bias),
+            "inside", 4, 10,
+            stay=("rows",),
+            tokens=[token],
+        )
+
     hops = range(shards - 1)
-    carries = []
-    for group in range(groups):
-        part = slice(group * quarter, (group + 1) * quarter)
-        carries.append(Carry(group, mines[part], others[part], False))
+    carries = [Carry(group, updates[2 * group], updates[2 * group + 1], False) for group in range(groups)]
+    insides = []
     token = None
     for index in hops:
         for carry in carries:
             carry.hop(index, token)
             token = carry.sent
+        while index == min(1, shards - 2) and len(insides) < groups:
+            insides.append(inside_of(len(insides), token))
+            token = insides[-1][0]
 
     normed = None
-    incoming, suffixes, backs = [], [], []
+    incoming, middles, backs = [], [], []
     for group in range(groups):
         incoming.append(carries[group].finish(token))
+        prefix, inside, qd = insides[group][:3]
         normed, grad, suffix, mine, other = call(
             forward_kernel, group,
-            ["rows"] * 4 + ["run", "table", "bias", "bias", "prefix", "mine", "other"],
-            ["rows", "rows", "states", "mine", "other"],
-            (rows_shape, rows_shape, states_shape, part_shape, part_shape),
-            (query_in, key_in, value_in, out_grad, run, table, weight_bias, enter_bias, prefix, *incoming[group]),
-            "forward", 4, 8,
+            ["headed", "headed", "rows", "table", "states", "mine", "other"],
+            ["rows", "headed", "states", "mine", "other"],
+            (rows_shape, headed(BF16), states_shape, part_shape, part_shape),
+            (inside, qd, out_grad, table, prefix, *incoming[group]),
+            "forward", 2, 8,
             aliases=(normed,),
             tokens=[backs[-1].sent] if backs else [],
         )
         token = mine
-        suffixes.append((grad, suffix))
+        middles.append((grad, suffix))
         backs.append(Carry(group, mine, other, True))
         if group == 0:
             backs[0].hop(0)
+
+    query_gradient = None
+    dattends = []
+
+    def query_of(group, token):
+        return call(
+            query_kernel, group,
+            ["rows", "rows", "headed", "run", "table", "bias", "bias", "states", "mine", "other"],
+            ["rows", "headed"],
+            (rows_shape, headed(BF16)),
+            (
+                key_in, value_in, middles[group][0], run, table, weight_bias, enter_bias, insides[group][0],
+                *incoming[group],
+            ),
+            "query", 3, 8,
+            aliases=(query_gradient,),
+            tokens=[token],
+        )
+
     for index in hops:
         for place, back in enumerate(backs):
             ahead = index + 1 if place == 0 else index
             if ahead in hops:
                 back.hop(ahead, token)
                 token = back.sent
-
-    grads = (None, None, None)
+        while index == min(1, shards - 2) and len(dattends) < groups:
+            query_gradient, dattend = query_of(len(dattends), token)
+            dattends.append(dattend)
+            token = dattend
+    grads = (None, None)
     for group in range(groups):
-        grad, suffix = suffixes[group]
-        outgoing = backs[group].finish(token)
+        grad, suffix = middles[group]
+        kd, vd, attend = insides[group][3:]
         grads = call(
             backward_kernel, group,
-            ["rows"] * 4 + ["run", "table", "bias", "bias", "bias", "prefix", "states", "mine", "other", "mine", "other"],
-            ["rows", "rows", "rows"],
-            (rows_shape, rows_shape, rows_shape),
-            (
-                query_in, key_in, value_in, grad, run, table, weight_bias, enter_bias, leave_bias,
-                prefix, suffix, *incoming[group], *outgoing,
-            ),
-            "backward", 8, 10,
+            ["rows"] + ["headed"] * 5 + ["table", "states", "mine", "other"],
+            ["rows", "rows"],
+            (rows_shape, rows_shape),
+            (query_in, grad, attend, dattends[group], kd, vd, table, suffix, *backs[group].finish(token)),
+            "backward", 4, 10,
             aliases=grads,
         )
         token = grads[0]
-    return (normed, *grads)
+    return (normed, query_gradient, *grads)
 
 
 def solution(mesh):

time: 103 us -> 91.7 us (0.89)
  waiting for transfers between devices: 43.5 us -> 36.9 us
  local copies, waits for them, and re-layouts: 4.35 us -> 0.03 us
  other arithmetic: 2.58 us -> 0.87 us
  Pallas kernels: 34.5 us -> 36.2 us
    ppermute x12, waiting for transfers between devices: 39 us -> 31.5 us  [hop(): self.landed.append(lax.ppermute(self.sent, 'seq', [self.hops[index]]))]
    unnamed x24 -> x8, local copies, waits for them, and re-layouts: 3.22 us -> 0.03 us
    pallas_call x5 -> x9, Pallas kernels: 34.5 us -> 36.2 us  [call_heads(): pl.pallas_call(functools.partial(with_rows, kernel, dims, group, which, l...]
    slice x1 -> x0, local copies, waits for them, and re-layouts: 1.13 us -> none  [local(): carries.append(Carry(group, mines[part], others[part], False))]
    add x2, other arithmetic: 1.18 us -> 0.08 us  [start(): self.total = self.g1 * self.zero + self.one]
  transfers between devices with their start and end apart: 21 -> 21, of which waited for: 10 -> 11; matrix products, arithmetic and copies ran while one was open for 3% -> 1% of each run, Pallas kernels for 18% -> 29%
where the time goes in v4:
time: 91.7 us; the launch traced here: 91.3 us
  waiting for transfers between devices  36.9 us (40%)
  Pallas kernels  36.2 us (39%)
  starting transfers between devices  16.3 us (18%)
  between operations  1 us (1%)
    pallas_call x9, Pallas kernels, call_heads(): pl.pallas_call(functools.partial(with_rows, kernel, dims, group, which, l...  36.2 us
    ppermute x12, waiting for transfers between devices, hop(): self.landed.append(lax.ppermute(self.sent, 'seq', [self.hops[index]]))  31.5 us
    ppermute x12, starting transfers between devices, hop(): self.landed.append(lax.ppermute(self.sent, 'seq', [self.hops[index]]))  14.2 us
    ppermute x4, waiting for transfers between devices, finish(): return (keep, lax.ppermute(send, 'ctx', swap))  2.58 us
    ppermute x4, waiting for transfers between devices, __init__(): self.mine, self.got = (mine, lax.ppermute(other, 'ctx', swap))  2.49 us
  transfers between devices with their start and end apart: 21, of which 11 were waited for; matrix products, arithmetic and copies ran while one was open for 1% of the time, Pallas kernels for 29%

profile of v4, /device:TPU:0, one launch (start us, length us, event | category | flops | bytes accessed | tf_op | source)
XLA Modules:
  0.0 91.3 jit_solution(554650309539935731)
XLA Ops:
  0.6 6.0 %begin.1 = (f32[4,128,128]{2,1,0:T(8,128)S(1)}, f32[4,128,128]{2,1,0:T(8,128)S(1)}, f32[4,128,128]{2,1,0:T(8,128)S(1)}, f32[4,128,128]{2,1,0:T(8,128)S(1)}, f32[...) custom-call(s32[1]{0:T(128)} %bitcast.core_ref, ...), custom_call_target="tpu_custom_call" | custom-call | flops 134217728 | bytes 4194304 | tf_op jit(solution)/shard_map/begin/pallas_call | solution.py:335
  6.6 0.5 collective-permute-start
  7.1 0.1 collective-permute-start.1
  7.2 0.4 collective-permute-start.2
  7.6 0.3 collective-permute-done
  8.0 1.1 %collective-permute-done.2 = f32[4,128,128]{2,1,0:T(8,128)S(1)} collective-permute-done((f32[4,128,128]{2,1,0:T(8,128)S(1)}, f32[4,128,128]{2,1,0:T(8,128)S(1)}, u32[]{:S(2)}, u32[]{:S(2)}) %collective-permute-start.2) | collective-permute-done | bytes 262176 | tf_op jit(solution)/shard_map/ppermute | solution.py:408
  9.1 4.6 %collective-permute-start.4 = (f32[4,128,128]{2,1,0:T(8,128)S(1)}, f32[4,128,128]{2,1,0:T(8,128)S(1)}, u32[]{:S(2)}, u32[]{:S(2)}) collective-permute-start(f32[4,128,128]{2,1,0:T(8,128)S(1)} %select_add_fusion.3), channel_id=1, source_target_pairs={{0,4},{1,5},{2,6},{3,7},{16,20},{17,21},{18,22},{19,23}} | collective-permute-start | bytes 786440 | tf_op jit(solution)/shard_map/ppermute | solution.py:431
  13.7 0.0 collective-permute-done.1
  13.8 1.3 %collective-permute-start.3 = (f32[4,128,128]{2,1,0:T(8,128)S(1)}, f32[4,128,128]{2,1,0:T(8,128)S(1)}, u32[]{:S(2)}, u32[]{:S(2)}) collective-permute-start(f32[4,128,128]{2,1,0:T(8,128)S(1)} %select_add_fusion.2), channel_id=1, source_target_pairs={{0,4},{1,5},{2,6},{3,7},{16,20},{17,21},{18,22},{19,23}} | collective-permute-start | bytes 786440 | tf_op jit(solution)/shard_map/ppermute | solution.py:431
  15.1 5.2 %collective-permute-done.4 = f32[4,128,128]{2,1,0:T(8,128)S(1)} collective-permute-done((f32[4,128,128]{2,1,0:T(8,128)S(1)}, f32[4,128,128]{2,1,0:T(8,128)S(1)}, u32[]{:S(2)}, u32[]{:S(2)}) %collective-permute-start.4) | collective-permute-done | bytes 262176 | tf_op jit(solution)/shard_map/ppermute | solution.py:431
  20.4 0.7 collective-permute-start.6
  21.0 4.3 %collective-permute-done.3 = f32[4,128,128]{2,1,0:T(8,128)S(1)} collective-permute-done((f32[4,128,128]{2,1,0:T(8,128)S(1)}, f32[4,128,128]{2,1,0:T(8,128)S(1)}, u32[]{:S(2)}, u32[]{:S(2)}) %collective-permute-start.3) | collective-permute-done | bytes 262176 | tf_op jit(solution)/shard_map/ppermute | solution.py:431
  25.4 0.7 collective-permute-start.5
  26.1 3.9 %inside.2 = (f32[8,3,128,128]{3,2,1,0:T(8,128)S(1)}, f32[8,512,128]{2,1,0:T(8,128)S(1)}, bf16[8,512,128]{2,1,0:T(8,128)(2,1)S(1)}, bf16[8,512,128]{2,1,0:T(8,128...) custom-call(s32[1]{0:T(128)} %bitcast.core_ref, bf16[512,2048]{1,0:T(8,128)(2,1)} %refs_0_.13, ...), custom_call_target="tpu_custom_call" | custom-call | flops 536870912 | bytes 10485760 | tf_op jit(solution)/shard_map/inside/pallas_call | solution.py:335
  30.0 3.9 %inside.3 = (f32[8,3,128,128]{3,2,1,0:T(8,128)S(1)}, f32[8,512,128]{2,1,0:T(8,128)S(1)}, bf16[8,512,128]{2,1,0:T(8,128)(2,1)S(1)}, bf16[8,512,128]{2,1,0:T(8,128...) custom-call(s32[1]{0:T(128)} %bitcast.core_ref, bf16[512,2048]{1,0:T(8,128)(2,1)} %refs_0_.13, ...), custom_call_target="tpu_custom_call" | custom-call | flops 536870912 | bytes 10485760 | tf_op jit(solution)/shard_map/inside/pallas_call | solution.py:335
  33.9 0.0 collective-permute-done.6
  33.9 0.0 copy-start.3
  33.9 0.1 multiply_add_fusion.9
  34.0 0.8 collective-permute-start.8
  34.8 0.0 collective-permute-done.5
  34.8 0.1 multiply_add_fusion.8
  34.9 0.0 collective-permute-done.8
  34.9 0.1 fusion.6
  35.0 0.1 collective-permute-start.9
  35.0 0.7 collective-permute-start.7
  35.7 0.8 collective-permute-done.9.refs_6_.refs_9_
  36.6 0.0 copy-done.3
  36.6 4.0 %forward.2 = (bf16[512,2048]{1,0:T(8,128)(2,1)}, bf16[8,512,128]{2,1,0:T(8,128)(2,1)S(1)}, f32[8,3,128,128]{3,2,1,0:T(8,128)S(1)}, f32[4,128,128]{2,1,0:T(8,128)S(1)}, f32[4,128,128]{2,1,0:T(8,128)S(1)}) custom-call(s32[1]{0:T(128)} %bitcast.core_ref, f32[8,512,128]{2,1,0:T(8,128)S(1)} %get-tuple-element.77.refs_0_, ...), custom_call_target="tpu_custom_call" | custom-call | flops 268435456 | bytes 8388608 | tf_op jit(solution)/shard_map/forward/pallas_call | solution.py:335
  40.6 0.0 collective-permute-done.7
  40.6 0.2 collective-permute-start.11
  40.8 0.1 fusion.4
  40.9 0.4 collective-permute-start.10
  41.3 0.9 collective-permute-done.11
  42.3 0.7 collective-permute-start.13
  42.9 0.0 collective-permute-done.10.refs_6_.refs_9_
  43.0 0.0 copy-start.1
  43.0 4.1 %forward.3 = (bf16[512,2048]{1,0:T(8,128)(2,1)}, bf16[8,512,128]{2,1,0:T(8,128)(2,1)S(1)}, f32[8,3,128,128]{3,2,1,0:T(8,128)S(1)}, f32[4,128,128]{2,1,0:T(8,128)S(1)}, f32[4,128,128]{2,1,0:T(8,128)S(1)}) custom-call(s32[1]{0:T(128)} %bitcast.core_ref, f32[8,512,128]{2,1,0:T(8,128)S(1)} %get-tuple-element.72.refs_0_, ...), custom_call_target="tpu_custom_call", output_to_operand_aliasing={{0}: (8, {})} | custom-call | flops 268435456 | bytes 8388608 | tf_op jit(solution)/shard_map/forward/pallas_call | solution.py:335
  47.1 0.0 copy-start
  47.1 0.2 collective-permute-start.12
  47.3 0.0 collective-permute-done.13
  47.4 0.8 collective-permute-start.15
  48.2 0.5 collective-permute-done.12
  48.8 0.7 collective-permute-start.14
  49.5 0.0 collective-permute-done.15
  49.5 0.1 multiply_add_fusion.4
  49.5 0.0 collective-permute-done.14
  49.6 0.7 collective-permute-start.16
  50.3 1.3 %collective-permute-start.18 = (f32[4,128,128]{2,1,0:T(8,128)S(1)}, f32[4,128,128]{2,1,0:T(8,128)S(1)}, u32[]{:S(2)}, u32[]{:S(2)}) collective-permute-start(f32[4,128,128]{2,1,0:T(8,128)S(1)} %get-tuple-element.114), channel_id=1, source_target_pairs={{4,0},{5,1},{6,2},{7,3},{20,16},{21,17},{22,18},{23,19}} | collective-permute-start | bytes 786440 | tf_op jit(solution)/shard_map/ppermute | solution.py:431
  51.6 3.7 %query.2 = (bf16[512,2048]{1,0:T(8,128)(2,1)}, bf16[8,512,128]{2,1,0:T(8,128)(2,1)S(1)}) custom-call(s32[1]{0:T(128)} %bitcast.core_ref, bf16[512,2048]{1,0:T(8,128)(2,1)S(1)} %copy-done, bf16[512,2048]{1,0:T(8,128)(2,1)S(1)} %copy-done.1, bf16[8,512,128]{2,1,0:T(8,128)(2,1)S(1)} %get-tuple-element.86.refs_2_.refs_1_, ...), custom_call_target="tpu_custom_call" | custom-call | flops 402653184 | bytes 8388608 | tf_op jit(solution)/shard_map/query/pallas_call | solution.py:335
  55.3 3.7 %query.3 = (bf16[512,2048]{1,0:T(8,128)(2,1)}, bf16[8,512,128]{2,1,0:T(8,128)(2,1)S(1)}) custom-call(s32[1]{0:T(128)} %bitcast.core_ref, bf16[512,2048]{1,0:T(8,128)(2,1)S(1)} %copy-done, bf16[512,2048]{1,0:T(8,128)(2,1)S(1)} %copy-done.1, bf16[8,512,128]{2,1,0:T(8,128)(2,1)S(1)} %get-tuple-element.85.refs_2_.refs_1_, ...), custom_call_target="tpu_custom_call", output_to_operand_aliasing={{0}: (11, {})} | custom-call | flops 402653184 | bytes 8388608 | tf_op jit(solution)/shard_map/query/pallas_call | solution.py:335
  59.0 0.0 copy-start.2
  59.0 0.0 collective-permute-done.16
  59.0 0.1 multiply_add_fusion.2
  59.1 16.3 %collective-permute-done.18 = f32[4,128,128]{2,1,0:T(8,128)S(1)} collective-permute-done((f32[4,128,128]{2,1,0:T(8,128)S(1)}, f32[4,128,128]{2,1,0:T(8,128)S(1)}, u32[]{:S(2)}, u32[]{:S(2)}) %collective-permute-start.18) | collective-permute-done | bytes 262176 | tf_op jit(solution)/shard_map/ppermute | solution.py:431
  75.4 0.1 fusion.2
  75.5 0.1 collective-permute-start.19
  75.6 1.3 %collective-permute-start.17 = (f32[4,128,128]{2,1,0:T(8,128)S(1)}, f32[4,128,128]{2,1,0:T(8,128)S(1)}, u32[]{:S(2)}, u32[]{:S(2)}) collective-permute-start(f32[4,128,128]{2,1,0:T(8,128)S(1)} %get-tuple-element.112), channel_id=1, source_target_pairs={{4,0},{5,1},{6,2},{7,3},{20,16},{21,17},{22,18},{23,19}} | collective-permute-start | bytes 786440 | tf_op jit(solution)/shard_map/ppermute | solution.py:431
  76.9 0.2 collective-permute-done.19.refs_9_
  77.1 3.5 %backward.2 = (bf16[512,2048]{1,0:T(8,128)(2,1)}, bf16[512,2048]{1,0:T(8,128)(2,1)}) custom-call(s32[1]{0:T(128)} %bitcast.core_ref, bf16[512,2048]{1,0:T(8,128)(2,1)S(1)} %copy-done.2, bf16[8,512,128]{2,1,0:T(8,128)(2,1)S(1)} %get-tuple-element.86.refs_2_.refs_1_, bf16[8,512,128]{2,1,0:T(8,128)(2,1)S(1)} %get-tuple-element.102.refs_2_, ...), custom_call_target="tpu_custom_call" | custom-call | flops 536870912 | bytes 10485760 | tf_op jit(solution)/shard_map/backward/pallas_call | solution.py:335
  80.6 5.6 %collective-permute-done.17 = f32[4,128,128]{2,1,0:T(8,128)S(1)} collective-permute-done((f32[4,128,128]{2,1,0:T(8,128)S(1)}, f32[4,128,128]{2,1,0:T(8,128)S(1)}, u32[]{:S(2)}, u32[]{:S(2)}) %collective-permute-start.17) | collective-permute-done | bytes 262176 | tf_op jit(solution)/shard_map/ppermute | solution.py:431
  86.2 0.1 fusion
  86.2 0.1 collective-permute-start.20
  86.3 1.5 %collective-permute-done.20.refs_9_ = f32[4,128,128]{2,1,0:T(8,128)S(1)} collective-permute-done((f32[4,128,128]{2,1,0:T(8,128)S(1)}, f32[4,128,128]{2,1,0:T(8,128)S(1)}, u32[]{:S(2)}, u32[]{:S(2)}) %collective-permute-start.20) | collective-permute-done | bytes 262176 | tf_op jit(solution)/shard_map/ppermute | solution.py:446
  87.8 3.5 %backward.3 = (bf16[512,2048]{1,0:T(8,128)(2,1)}, bf16[512,2048]{1,0:T(8,128)(2,1)}) custom-call(s32[1]{0:T(128)} %bitcast.core_ref, bf16[512,2048]{1,0:T(8,128)(2,1)S(1)} %copy-done.2, bf16[8,512,128]{2,1,0:T(8,128)(2,1)S(1)} %get-tuple-element.85.refs_2_.refs_1_, ...), custom_call_target="tpu_custom_call", output_to_operand_aliasing={{0}: (11, {}), {1}: (12, {})} | custom-call | flops 536870912 | bytes 10485760 | tf_op jit(solution)/shard_map/backward/pallas_call | solution.py:335
  (13 shorter events, 0.3 us)
Async XLA Ops:
  6.6 1.4 %collective-permute-start = (f32[16,128]{1,0:T(8,128)S(1)}, f32[16,128]{1,0:T(8,128)S(1)}, u32[]{:S(2)}, u32[]{:S(2)}) collective-permute-start(f32[16,128]{1,0:T(8,128)S(1)} %get-tuple-element.63), channel_id=1, source_target_pairs={{0,1},{1,0},{2,3},{3,2},{4,5},{5,4},{6,7},{7,6},{8,9},{9,8},{10,11... | collective-permute-start | bytes 24584 | tf_op jit(solution)/shard_map/ppermute | solution.py:395
  7.1 6.6 %collective-permute-start.1 = (f32[4,128,128]{2,1,0:T(8,128)S(1)}, f32[4,128,128]{2,1,0:T(8,128)S(1)}, u32[]{:S(2)}, u32[]{:S(2)}) collective-permute-start(f32[4,128,128]{2,1,0:T(8,128)S(1)} %get-tuple-element.65), channel_id=1, source_target_pairs={{0,1},{1,0},{2,3},{3,2},{4,5},{5,4},{6,7},{7,6},{8,9},{9,8},{10,11... | collective-permute-start | bytes 786440 | tf_op jit(solution)/shard_map/ppermute | solution.py:408
  7.2 1.8 %collective-permute-start.2 = (f32[4,128,128]{2,1,0:T(8,128)S(1)}, f32[4,128,128]{2,1,0:T(8,128)S(1)}, u32[]{:S(2)}, u32[]{:S(2)}) collective-permute-start(f32[4,128,128]{2,1,0:T(8,128)S(1)} %get-tuple-element.67), channel_id=1, source_target_pairs={{0,1},{1,0},{2,3},{3,2},{4,5},{5,4},{6,7},{7,6},{8,9},{9,8},{10,11... | collective-permute-start | bytes 786440 | tf_op jit(solution)/shard_map/ppermute | solution.py:408
  9.1 11.2 %collective-permute-start.4 = (f32[4,128,128]{2,1,0:T(8,128)S(1)}, f32[4,128,128]{2,1,0:T(8,128)S(1)}, u32[]{:S(2)}, u32[]{:S(2)}) collective-permute-start(f32[4,128,128]{2,1,0:T(8,128)S(1)} %select_add_fusion.3), channel_id=1, source_target_pairs={{0,4},{1,5},{2,6},{3,7},{16,20},{17,21},{18,22},{19,23}} | collective-permute-start | bytes 786440 | tf_op jit(solution)/shard_map/ppermute | solution.py:431
  13.8 11.6 %collective-permute-start.3 = (f32[4,128,128]{2,1,0:T(8,128)S(1)}, f32[4,128,128]{2,1,0:T(8,128)S(1)}, u32[]{:S(2)}, u32[]{:S(2)}) collective-permute-start(f32[4,128,128]{2,1,0:T(8,128)S(1)} %select_add_fusion.2), channel_id=1, source_target_pairs={{0,4},{1,5},{2,6},{3,7},{16,20},{17,21},{18,22},{19,23}} | collective-permute-start | bytes 786440 | tf_op jit(solution)/shard_map/ppermute | solution.py:431
  20.4 13.5 %collective-permute-start.6 = (f32[4,128,128]{2,1,0:T(8,128)S(1)}, f32[4,128,128]{2,1,0:T(8,128)S(1)}, u32[]{:S(2)}, u32[]{:S(2)}) collective-permute-start(f32[4,128,128]{2,1,0:T(8,128)S(1)} %multiply_add_fusion.11), channel_id=1, source_target_pairs={{4,8},{5,9},{6,10},{7,11},{20,24},{21,25},{22,26},{23,27}} | collective-permute-start | bytes 786440 | tf_op jit(solution)/shard_map/ppermute | solution.py:431
  25.4 9.4 %collective-permute-start.5 = (f32[4,128,128]{2,1,0:T(8,128)S(1)}, f32[4,128,128]{2,1,0:T(8,128)S(1)}, u32[]{:S(2)}, u32[]{:S(2)}) collective-permute-start(f32[4,128,128]{2,1,0:T(8,128)S(1)} %multiply_add_fusion.10.refs_8_), channel_id=1, source_target_pairs={{4,8},{5,9},{6,10},{7,11},{20,24},{21,25},{22,26},{23,27}} | collective-permute-start | bytes 786440 | tf_op jit(solution)/shard_map/ppermute | solution.py:431
  33.9 2.7 %copy-start.3 = (bf16[512,2048]{1,0:T(8,128)(2,1)S(1)}, bf16[512,2048]{1,0:T(8,128)(2,1)}, u32[]{:S(2)}) copy-start(bf16[512,2048]{1,0:T(8,128)(2,1)} %refs_2_.9) | copy-start | bytes 6291460
  34.0 0.9 collective-permute-start.8
  35.0 1.6 %collective-permute-start.9 = (f32[4,128,128]{2,1,0:T(8,128)S(1)}, f32[4,128,128]{2,1,0:T(8,128)S(1)}, u32[]{:S(2)}, u32[]{:S(2)}) collective-permute-start(f32[4,128,128]{2,1,0:T(8,128)S(1)} %get-tuple-element.132), channel_id=1, source_target_pairs={{0,1},{1,0},{2,3},{3,2},{4,5},{5,4},{6,7},{7,6},{8,9},{9,8},{10,11... | collective-permute-start | bytes 786440 | tf_op jit(solution)/shard_map/ppermute | solution.py:446
  35.0 5.6 %collective-permute-start.7 = (f32[4,128,128]{2,1,0:T(8,128)S(1)}, f32[4,128,128]{2,1,0:T(8,128)S(1)}, u32[]{:S(2)}, u32[]{:S(2)}) collective-permute-start(f32[4,128,128]{2,1,0:T(8,128)S(1)} %get-tuple-element.116), channel_id=1, source_target_pairs={{8,12},{9,13},{10,14},{11,15},{24,28},{25,29},{26,30},{27,31}} | collective-permute-start | bytes 786440 | tf_op jit(solution)/shard_map/ppermute | solution.py:431
  40.6 1.6 %collective-permute-start.11 = (f32[4,128,128]{2,1,0:T(8,128)S(1)}, f32[4,128,128]{2,1,0:T(8,128)S(1)}, u32[]{:S(2)}, u32[]{:S(2)}) collective-permute-start(f32[4,128,128]{2,1,0:T(8,128)S(1)} %get-tuple-element.83), channel_id=1, source_target_pairs={{0,1},{1,0},{2,3},{3,2},{4,5},{5,4},{6,7},{7,6},{8,9},{9,8},{10,11... | collective-permute-start | bytes 786440 | tf_op jit(solution)/shard_map/ppermute | solution.py:408
  40.9 2.1 %collective-permute-start.10 = (f32[4,128,128]{2,1,0:T(8,128)S(1)}, f32[4,128,128]{2,1,0:T(8,128)S(1)}, u32[]{:S(2)}, u32[]{:S(2)}) collective-permute-start(f32[4,128,128]{2,1,0:T(8,128)S(1)} %get-tuple-element.130), channel_id=1, source_target_pairs={{0,1},{1,0},{2,3},{3,2},{4,5},{5,4},{6,7},{7,6},{8,9},{9,8},{10,11... | collective-permute-start | bytes 786440 | tf_op jit(solution)/shard_map/ppermute | solution.py:446
  42.3 5.1 %collective-permute-start.13 = (f32[4,128,128]{2,1,0:T(8,128)S(1)}, f32[4,128,128]{2,1,0:T(8,128)S(1)}, u32[]{:S(2)}, u32[]{:S(2)}) collective-permute-start(f32[4,128,128]{2,1,0:T(8,128)S(1)} %select_add_fusion.1.refs_8_), channel_id=1, source_target_pairs={{12,8},{13,9},{14,10},{15,11},{28,24},{29,25},{30,26},{31,27}} | collective-permute-start | bytes 786440 | tf_op jit(solution)/shard_map/ppermute | solution.py:431
  43.0 8.6 %copy-start.1 = (bf16[512,2048]{1,0:T(8,128)(2,1)S(1)}, bf16[512,2048]{1,0:T(8,128)(2,1)}, u32[]{:S(2)}) copy-start(bf16[512,2048]{1,0:T(8,128)(2,1)} %refs_1_.7) | copy-start | bytes 6291460
  47.1 4.5 %copy-start = (bf16[512,2048]{1,0:T(8,128)(2,1)S(1)}, bf16[512,2048]{1,0:T(8,128)(2,1)}, u32[]{:S(2)}) copy-start(bf16[512,2048]{1,0:T(8,128)(2,1)} %refs_0_.11) | copy-start | bytes 6291460
  47.1 1.6 %collective-permute-start.12 = (f32[4,128,128]{2,1,0:T(8,128)S(1)}, f32[4,128,128]{2,1,0:T(8,128)S(1)}, u32[]{:S(2)}, u32[]{:S(2)}) collective-permute-start(f32[4,128,128]{2,1,0:T(8,128)S(1)} %get-tuple-element.87), channel_id=1, source_target_pairs={{0,1},{1,0},{2,3},{3,2},{4,5},{5,4},{6,7},{7,6},{8,9},{9,8},{10,11... | collective-permute-start | bytes 786440 | tf_op jit(solution)/shard_map/ppermute | solution.py:408
  47.4 2.1 %collective-permute-start.15 = (f32[4,128,128]{2,1,0:T(8,128)S(1)}, f32[4,128,128]{2,1,0:T(8,128)S(1)}, u32[]{:S(2)}, u32[]{:S(2)}) collective-permute-start(f32[4,128,128]{2,1,0:T(8,128)S(1)} %multiply_add_fusion.5), channel_id=1, source_target_pairs={{8,4},{9,5},{10,6},{11,7},{24,20},{25,21},{26,22},{27,23}} | collective-permute-start | bytes 786440 | tf_op jit(solution)/shard_map/ppermute | solution.py:431
  48.8 0.8 collective-permute-start.14
  49.6 9.4 %collective-permute-start.16 = (f32[4,128,128]{2,1,0:T(8,128)S(1)}, f32[4,128,128]{2,1,0:T(8,128)S(1)}, u32[]{:S(2)}, u32[]{:S(2)}) collective-permute-start(f32[4,128,128]{2,1,0:T(8,128)S(1)} %multiply_add_fusion.3.refs_10_), channel_id=1, source_target_pairs={{8,4},{9,5},{10,6},{11,7},{24,20},{25,21},{26,22},{27,23}} | collective-permute-start | bytes 786440 | tf_op jit(solution)/shard_map/ppermute | solution.py:431
  50.3 25.1 %collective-permute-start.18 = (f32[4,128,128]{2,1,0:T(8,128)S(1)}, f32[4,128,128]{2,1,0:T(8,128)S(1)}, u32[]{:S(2)}, u32[]{:S(2)}) collective-permute-start(f32[4,128,128]{2,1,0:T(8,128)S(1)} %get-tuple-element.114), channel_id=1, source_target_pairs={{4,0},{5,1},{6,2},{7,3},{20,16},{21,17},{22,18},{23,19}} | collective-permute-start | bytes 786440 | tf_op jit(solution)/shard_map/ppermute | solution.py:431
  59.0 18.1 %copy-start.2 = (bf16[512,2048]{1,0:T(8,128)(2,1)S(1)}, bf16[512,2048]{1,0:T(8,128)(2,1)}, u32[]{:S(2)}) copy-start(bf16[512,2048]{1,0:T(8,128)(2,1)} %refs_0_.13) | copy-start | bytes 6291460
  75.5 1.6 %collective-permute-start.19 = (f32[4,128,128]{2,1,0:T(8,128)S(1)}, f32[4,128,128]{2,1,0:T(8,128)S(1)}, u32[]{:S(2)}, u32[]{:S(2)}) collective-permute-start(f32[4,128,128]{2,1,0:T(8,128)S(1)} %get-tuple-element.128), channel_id=1, source_target_pairs={{0,1},{1,0},{2,3},{3,2},{4,5},{5,4},{6,7},{7,6},{8,9},{9,8},{10,11... | collective-permute-start | bytes 786440 | tf_op jit(solution)/shard_map/ppermute | solution.py:446
  75.6 10.6 %collective-permute-start.17 = (f32[4,128,128]{2,1,0:T(8,128)S(1)}, f32[4,128,128]{2,1,0:T(8,128)S(1)}, u32[]{:S(2)}, u32[]{:S(2)}) collective-permute-start(f32[4,128,128]{2,1,0:T(8,128)S(1)} %get-tuple-element.112), channel_id=1, source_target_pairs={{4,0},{5,1},{6,2},{7,3},{20,16},{21,17},{22,18},{23,19}} | collective-permute-start | bytes 786440 | tf_op jit(solution)/shard_map/ppermute | solution.py:431
  86.2 1.6 %collective-permute-start.20 = (f32[4,128,128]{2,1,0:T(8,128)S(1)}, f32[4,128,128]{2,1,0:T(8,128)S(1)}, u32[]{:S(2)}, u32[]{:S(2)}) collective-permute-start(f32[4,128,128]{2,1,0:T(8,128)S(1)} %get-tuple-element.126), channel_id=1, source_target_pairs={{0,1},{1,0},{2,3},{3,2},{4,5},{5,4},{6,7},{7,6},{8,9},{9,8},{10,11... | collective-permute-start | bytes 786440 | tf_op jit(solution)/shard_map/ppermute | solution.py:446

commit v5 on v4

--- a/solution.py
+++ b/solution.py
@@ -95,13 +95,14 @@
 
 
 def begin_kernel(dims, core_ref, own, *rest):
-    updates_refs = rest[:-6]
+    updates_refs, place_ref = rest[:-7], rest[-7]
     run_ref, table_ref, gain_ref, weight_bias_ref, enter_bias_ref, leave_bias_ref = rest[-6:]
     chunks = dims.chunks
     p = pl.program_id(0)
 
     @pl.when(p == 0)
     def _():
+        place_ref[...] = jnp.where(lax.broadcasted_iota(jnp.int32, place_ref.shape, 0) == core_ref[1], 1.0, 0.0)
         fill_tables(
             chunks, *own.plain, run_ref, table_ref, gain_ref, weight_bias_ref, enter_bias_ref, leave_bias_ref
         )
@@ -261,11 +262,12 @@
 
 
 class Dims:
-    def __init__(self, size, per_step, chunks, length, dh, heads):
+    def __init__(self, size, per_step, chunks, length, dh, heads, shards):
         self.size, self.per_step, self.chunks = size, per_step, chunks
         self.length, self.dh, self.heads = length, dh, heads
         self.quarter = size // 2
         self.steps = size // per_step
+        self.places = -(-shards // 8) * 8
 
     def head(self, group, p, core_ref):
         return (group + p // self.steps) * self.steps + lax.rem(p + core_ref[0] * (self.steps // 2), self.steps)
@@ -292,6 +294,7 @@
             all_run=whole(self.heads, 1, length),
             all_table=whole(self.heads, 2 * chunks, C),
             all_gain=whole(self.heads, C),
+            place=whole(self.places, C),
             any=pl.BlockSpec(memory_space=pl.ANY),
         )
 
@@ -364,11 +367,11 @@
     groups = GROUPS
     size = heads // groups
     quarter = size // 2
-    dims = Dims(size, PER_STEP, chunks, length, dh, heads)
     shards = lax.axis_size("seq")
+    dims = Dims(size, PER_STEP, chunks, length, dh, heads, shards)
     core = lax.axis_index("ctx")
     first = core == 0
-    core_arg = core.astype(jnp.int32).reshape(1)
+    core_arg = jnp.stack([core, lax.axis_index("seq")]).astype(jnp.int32)
     swap = [(0, 1), (1, 0)]
     shape = jax.ShapeDtypeStruct
     states_shape = shape((size, chunks - 1, dh, dh), F32)
@@ -378,12 +381,13 @@
     call = functools.partial(call_heads, dims, core_arg)
 
     headed = lambda kind: shape((size, length, dh), kind)
-    *updates, run, table, gain, weight_bias, enter_bias, leave_bias = call(
+    *updates, places, run, table, gain, weight_bias, enter_bias, leave_bias = call(
         begin_kernel, 0,
         ["decay", "start", "rows", "rows"],
-        ["update", "all_run", "all_table", "all_gain", "bias", "bias", "bias"],
+        ["update", "place", "all_run", "all_table", "all_gain", "bias", "bias", "bias"],
         (
             *[part_shape] * (2 * groups),
+            shape((dims.places, C), F32),
             shape((heads, 1, length), F32), shape((heads, 2 * chunks, C), F32), shape((heads, C), F32),
             bias_shape, bias_shape, bias_shape,
         ),
@@ -406,11 +410,6 @@
             self.g0, self.g1 = pick(gain0, group), pick(gain1, group)
             self.both = self.g0 * self.g1
             self.mine, self.got = mine, lax.ppermute(other, "ctx", swap)
-            if backward:
-                self.hops = [(k, k - 1) for k in range(shards - 1, 0, -1)]
-            else:
-                self.hops = [(k, k + 1) for k in range(shards - 1)]
-            self.landed = []
 
         def start(self, token=None):
             got = after(self.got, token)
@@ -421,22 +420,7 @@
             else:
                 self.total = self.g1 * self.zero + self.one
 
-        def hop(self, index, token=None):
-            if index == 0:
-                self.start(token)
-                self.sent = self.total
-            else:
-                self.settle(token)
-                self.sent = self.both * self.state + self.total
-            self.landed.append(lax.ppermute(self.sent, "seq", [self.hops[index]]))
-
-        def settle(self, token=None):
-            self.landed[-1] = after(self.landed[-1], token)
-            self.state = sum(self.landed[1:], self.landed[0])
-
-        def finish(self, token=None):
-            self.settle(token)
-            state = self.state
+        def finish(self, state):
             if self.backward:
                 inner = self.g1 * state + self.one
                 keep, send = jnp.where(first, inner, state), jnp.where(first, state, inner)
@@ -444,6 +428,41 @@
                 inner = self.g0 * state + self.zero
                 keep, send = jnp.where(first, state, inner), jnp.where(first, inner, state)
             return keep, lax.ppermute(send, "ctx", swap)
+
+    class Line:
+        def __init__(self, backward):
+            self.at = (lambda i: shards - 1 - i) if backward else (lambda i: i)
+            self.landed = []
+
+        def step(self, carries, token=None):
+            s = len(self.landed)
+            sent = None
+            for group, carry in enumerate(carries):
+                if s - shards + 1 < group <= s:
+                    if group == s:
+                        carry.start(token)
+                        new = carry.total
+                    else:
+                        new = carry.both * self.last(token) + carry.total
+                        token = new
+                    sent = new if sent is None else jnp.where(self.here(s - group), new, sent)
+            pairs = [(self.at(i), self.at(i + 1)) for i in range(shards - 1) if 0 <= s - i < groups]
+            self.landed.append(lax.ppermute(sent, "seq", pairs))
+            return sent
+
+        def last(self, token=None):
+            self.landed[-1] = after(self.landed[-1], token)
+            return self.landed[-1]
+
+        def state(self, group, token=None):
+            self.last(token)
+            state = self.landed[group + shards - 2]
+            for i in range(1, shards - 1):
+                state = jnp.where(self.here(i), self.landed[group + i - 1], state)
+            return jnp.where(self.here(0), 0.0, state)
+
+        def here(self, i):
+            return places[None, self.at(i) : self.at(i) + 1, :] != 0.0
 
     def inside_of(group, token):
         return call(
@@ -457,22 +476,27 @@
             tokens=[token],
         )
 
-    hops = range(shards - 1)
     carries = [Carry(group, updates[2 * group], updates[2 * group + 1], False) for group in range(groups)]
+    line = Line(False)
     insides = []
     token = None
-    for index in hops:
-        for carry in carries:
-            carry.hop(index, token)
-            token = carry.sent
-        while index == min(1, shards - 2) and len(insides) < groups:
+    for index in range(shards - 1):
+        token = line.step(carries, token)
+        if len(insides) < groups:
             insides.append(inside_of(len(insides), token))
             token = insides[-1][0]
+    while len(insides) < groups:
+        insides.append(inside_of(len(insides), token))
+        token = insides[-1][0]
 
     normed = None
     incoming, middles, backs = [], [], []
+    back_line = Line(True)
     for group in range(groups):
-        incoming.append(carries[group].finish(token))
+        state = line.state(group, token)
+        if group < groups - 1:
+            line.step(carries)
+        incoming.append(carries[group].finish(state))
         prefix, inside, qd = insides[group][:3]
         normed, grad, suffix, mine, other = call(
             forward_kernel, group,
@@ -482,13 +506,13 @@
             (inside, qd, out_grad, table, prefix, *incoming[group]),
             "forward", 2, 8,
             aliases=(normed,),
-            tokens=[backs[-1].sent] if backs else [],
+            tokens=[sent] if backs else [],
         )
         token = mine
         middles.append((grad, suffix))
         backs.append(Carry(group, mine, other, True))
-        if group == 0:
-            backs[0].hop(0)
+        if group < groups - 1:
+            sent = back_line.step(backs, token if group else None)
 
     query_gradient = None
     dattends = []
@@ -508,18 +532,19 @@
             tokens=[token],
         )
 
-    for index in hops:
-        for place, back in enumerate(backs):
-            ahead = index + 1 if place == 0 else index
-            if ahead in hops:
-                back.hop(ahead, token)
-                token = back.sent
-        while index == min(1, shards - 2) and len(dattends) < groups:
+    while len(back_line.landed) < shards - 1 or len(dattends) < groups:
+        if len(back_line.landed) < shards - 1:
+            token = back_line.step(backs, token)
+        if len(dattends) < groups:
             query_gradient, dattend = query_of(len(dattends), token)
             dattends.append(dattend)
             token = dattend
+
     grads = (None, None)
     for group in range(groups):
+        state = back_line.state(group, token)
+        if group < groups - 1:
+            back_line.step(backs)
         grad, suffix = middles[group]
         kd, vd, attend = insides[group][3:]
         grads = call(
@@ -527,7 +552,7 @@
             ["rows"] + ["headed"] * 5 + ["table", "states", "mine", "other"],
             ["rows", "rows"],
             (rows_shape, rows_shape),
-            (query_in, grad, attend, dattends[group], kd, vd, table, suffix, *backs[group].finish(token)),
+            (query_in, grad, attend, dattends[group], kd, vd, table, suffix, *backs[group].finish(state)),
             "backward", 4, 10,
             aliases=grads,
         )

time: 91.7 us -> 95 us (1.036)
  Pallas kernels: 36.2 us -> 41.3 us
  waiting for transfers between devices: 36.9 us -> 34.6 us
    pallas_call x9, Pallas kernels: 36.2 us -> 41.3 us  [call_heads(): pl.pallas_call(functools.partial(with_rows, kernel, dims, group, which, l...]
    ppermute x12 -> x8, waiting for transfers between devices: 31.5 us -> 28.5 us  [step(): self.landed.append(lax.ppermute(sent, 'seq', pairs))]
    ppermute x12 -> x8, starting transfers between devices: 14.2 us -> 14.5 us  [step(): self.landed.append(lax.ppermute(sent, 'seq', pairs))]
  transfers between devices with their start and end apart: 21 -> 17, of which waited for: 11 -> 11; matrix products, arithmetic and copies ran while one was open for 1% -> 0% of each run, Pallas kernels for 29% -> 32%
where the time goes in v5:
time: 95 us; the launch traced here: 94.6 us
  Pallas kernels  41.3 us (43%)
  waiting for transfers between devices  34.6 us (36%)
  starting transfers between devices  16.6 us (17%)
  other arithmetic  1.2 us (1%)
  between operations  0.96 us (1%)
    pallas_call x9, Pallas kernels, call_heads(): pl.pallas_call(functools.partial(with_rows, kernel, dims, group, which, l...  41.3 us
    ppermute x8, waiting for transfers between devices, step(): self.landed.append(lax.ppermute(sent, 'seq', pairs))  28.5 us
    ppermute x8, starting transfers between devices, step(): self.landed.append(lax.ppermute(sent, 'seq', pairs))  14.5 us
    ppermute x4, waiting for transfers between devices, __init__(): self.mine, self.got = (mine, lax.ppermute(other, 'ctx', swap))  3.28 us
    ppermute x4, waiting for transfers between devices, finish(): return (keep, lax.ppermute(send, 'ctx', swap))  2.43 us
  transfers between devices with their start and end apart: 17, of which 11 were waited for; matrix products, arithmetic and copies ran while one was open for 0% of the time, Pallas kernels for 32%

profile of v5, /device:TPU:0, one launch (start us, length us, event | category | flops | bytes accessed | tf_op | source)
XLA Modules:
  0.0 94.6 jit_solution(9186512278965931172)
XLA Ops:
  0.6 0.1 pad_add_fusion.core_ref
  0.7 6.5 %begin.1 = (f32[4,128,128]{2,1,0:T(8,128)S(1)}, f32[4,128,128]{2,1,0:T(8,128)S(1)}, f32[4,128,128]{2,1,0:T(8,128)S(1)}, f32[4,128,128]{2,1,0:T(8,128)S(1)}, f32[...) custom-call(s32[2]{0:T(128)S(1)} %pad_add_fusion.core_ref, ...), custom_call_target="tpu_custom_call" | custom-call | flops 134217728 | bytes 4194304 | tf_op jit(solution)/shard_map/begin/pallas_call | solution.py:338
  7.2 0.5 collective-permute-start
  7.7 0.1 collective-permute-start.1
  7.8 0.4 collective-permute-start.2
  8.2 0.3 collective-permute-done
  8.6 1.1 %collective-permute-done.2 = f32[4,128,128]{2,1,0:T(8,128)S(1)} collective-permute-done((f32[4,128,128]{2,1,0:T(8,128)S(1)}, f32[4,128,128]{2,1,0:T(8,128)S(1)}, u32[]{:S(2)}, u32[]{:S(2)}) %collective-permute-start.2) | collective-permute-done | bytes 262176 | tf_op jit(solution)/shard_map/ppermute | solution.py:412
  9.7 4.6 %collective-permute-start.3 = (f32[4,128,128]{2,1,0:T(8,128)S(1)}, f32[4,128,128]{2,1,0:T(8,128)S(1)}, u32[]{:S(2)}, u32[]{:S(2)}) collective-permute-start(f32[4,128,128]{2,1,0:T(8,128)S(1)} %select_add_fusion.3.refs_8_), channel_id=1, source_target_pairs={{0,4},{1,5},{2,6},{3,7},{16,20},{17,21},{18,22},{19,23}} | collective-permute-start | bytes 786440 | tf_op jit(solution)/shard_map/ppermute | solution.py:450
  14.3 4.4 %inside.2 = (f32[8,3,128,128]{3,2,1,0:T(8,128)S(1)}, f32[8,512,128]{2,1,0:T(8,128)S(1)}, bf16[8,512,128]{2,1,0:T(8,128)(2,1)S(1)}, bf16[8,512,128]{2,1,0:T(8,128...) custom-call(s32[2]{0:T(128)S(1)} %pad_add_fusion.core_ref, bf16[512,2048]{1,0:T(8,128)(2,1)} %refs_0_.13, ...), custom_call_target="tpu_custom_call" | custom-call | flops 536870912 | bytes 10485760 | tf_op jit(solution)/shard_map/inside/pallas_call | solution.py:338
  18.8 1.6 %collective-permute-done.3 = f32[4,128,128]{2,1,0:T(8,128)S(1)} collective-permute-done((f32[4,128,128]{2,1,0:T(8,128)S(1)}, f32[4,128,128]{2,1,0:T(8,128)S(1)}, u32[]{:S(2)}, u32[]{:S(2)}) %collective-permute-start.3) | collective-permute-done | bytes 262176 | tf_op jit(solution)/shard_map/ppermute | solution.py:450
  20.4 0.0 collective-permute-done.1
  20.4 0.1 broadcast_select_fusion.5
  20.5 4.4 %collective-permute-start.4 = (f32[4,128,128]{2,1,0:T(8,128)S(1)}, f32[4,128,128]{2,1,0:T(8,128)S(1)}, u32[]{:S(2)}, u32[]{:S(2)}) collective-permute-start(f32[4,128,128]{2,1,0:T(8,128)S(1)} %get-tuple-element.123.refs_8_), channel_id=1, source_target_pairs={{0,4},{4,8},{1,5},{5,9},{2,6},{6,10},{3,7},{7,11},{16,20},{20,24},... | collective-permute-start | bytes 786440 | tf_op jit(solution)/shard_map/ppermute | solution.py:450
  24.9 4.4 %inside.3 = (f32[8,3,128,128]{3,2,1,0:T(8,128)S(1)}, f32[8,512,128]{2,1,0:T(8,128)S(1)}, bf16[8,512,128]{2,1,0:T(8,128)(2,1)S(1)}, bf16[8,512,128]{2,1,0:T(8,128...) custom-call(s32[2]{0:T(128)S(1)} %pad_add_fusion.core_ref, bf16[512,2048]{1,0:T(8,128)(2,1)} %refs_0_.13, ...), custom_call_target="tpu_custom_call" | custom-call | flops 536870912 | bytes 10485760 | tf_op jit(solution)/shard_map/inside/pallas_call | solution.py:338
  29.3 0.8 collective-permute-done.4
  30.2 0.0 copy-start.3
  30.2 0.1 add_select_fusion.1
  30.2 0.8 collective-permute-start.5
  31.1 0.0 collective-permute-done.5
  31.1 0.1 fusion.6
  31.2 0.1 collective-permute-start.7
  31.3 0.7 collective-permute-start.6
  32.0 0.8 collective-permute-done.7.refs_6_.refs_9_
  32.8 0.0 copy-done.3
  32.8 4.7 %forward.2 = (bf16[512,2048]{1,0:T(8,128)(2,1)}, bf16[8,512,128]{2,1,0:T(8,128)(2,1)S(1)}, f32[8,3,128,128]{3,2,1,0:T(8,128)S(1)}, f32[4,128,128]{2,1,0:T(8,128)S(1)}, f32[4,128,128]{2,1,0:T(8,128)S(1)}) custom-call(s32[2]{0:T(128)S(1)} %pad_add_fusion.core_ref, f32[8,512,128]{2,1,0:T(8,128)S(1)} %get-tuple-element.77.refs_0_, ...), custom_call_target="tpu_custom_call" | custom-call | flops 268435456 | bytes 8388608 | tf_op jit(solution)/shard_map/forward/pallas_call | solution.py:338
  37.5 0.0 collective-permute-done.6
  37.5 0.2 collective-permute-start.9
  37.7 0.1 fusion.4
  37.8 0.4 collective-permute-start.8
  38.2 0.9 collective-permute-done.9
  39.1 0.7 collective-permute-start.11
  39.8 0.1 fusion.5.refs_5_.refs_8_
  39.9 0.0 collective-permute-done.8.refs_6_.refs_9_
  39.9 0.0 copy-start.1
  39.9 4.7 %forward.3 = (bf16[512,2048]{1,0:T(8,128)(2,1)}, bf16[8,512,128]{2,1,0:T(8,128)(2,1)S(1)}, f32[8,3,128,128]{3,2,1,0:T(8,128)S(1)}, f32[4,128,128]{2,1,0:T(8,128)S(1)}, f32[4,128,128]{2,1,0:T(8,128)S(1)}) custom-call(s32[2]{0:T(128)S(1)} %pad_add_fusion.core_ref, f32[8,512,128]{2,1,0:T(8,128)S(1)} %get-tuple-element.71.refs_0_, ...), custom_call_target="tpu_custom_call", output_to_operand_aliasing={{0}: (8, {})} | custom-call | flops 268435456 | bytes 8388608 | tf_op jit(solution)/shard_map/forward/pallas_call | solution.py:338
  44.6 0.0 copy-start
  44.6 0.2 collective-permute-start.10
  44.8 0.0 collective-permute-done.11
  44.9 1.4 %collective-permute-done.10 = f32[4,128,128]{2,1,0:T(8,128)S(1)} collective-permute-done((f32[4,128,128]{2,1,0:T(8,128)S(1)}, f32[4,128,128]{2,1,0:T(8,128)S(1)}, u32[]{:S(2)}, u32[]{:S(2)}) %collective-permute-start.10) | collective-permute-done | bytes 262176 | tf_op jit(solution)/shard_map/ppermute | solution.py:412
  46.2 0.1 broadcast_select_fusion
  46.3 0.7 collective-permute-start.12
  47.0 0.0 copy-done.1
  47.0 0.0 copy-done
  47.0 4.2 %query.2 = (bf16[512,2048]{1,0:T(8,128)(2,1)}, bf16[8,512,128]{2,1,0:T(8,128)(2,1)S(1)}) custom-call(s32[2]{0:T(128)S(1)} %pad_add_fusion.core_ref, bf16[512,2048]{1,0:T(8,128)(2,1)S(1)} %copy-done, bf16[512,2048]{1,0:T(8,128)(2,1)S(1)} %copy-done.1, bf16[8,512,128]{2,1,0:T(8,128)(2,1)S(1)} %get-tuple-element.85.refs_2_.refs_1_, ...), custom_call_target="tpu_custom_call" | custom-call | flops 402653184 | bytes 8388608 | tf_op jit(solution)/shard_map/query/pallas_call | solution.py:338
  51.2 0.0 collective-permute-done.12
  51.3 0.1 add_select_fusion.refs_11_
  51.3 1.3 %collective-permute-start.13 = (f32[4,128,128]{2,1,0:T(8,128)S(1)}, f32[4,128,128]{2,1,0:T(8,128)S(1)}, u32[]{:S(2)}, u32[]{:S(2)}) collective-permute-start(f32[4,128,128]{2,1,0:T(8,128)S(1)} %add_select_fusion.refs_11_), channel_id=1, source_target_pairs={{8,4},{4,0},{9,5},{5,1},{10,6},{6,2},{11,7},{7,3},{24,20},{20,16},... | collective-permute-start | bytes 786440 | tf_op jit(solution)/shard_map/ppermute | solution.py:450
  52.6 4.2 %query.3 = (bf16[512,2048]{1,0:T(8,128)(2,1)}, bf16[8,512,128]{2,1,0:T(8,128)(2,1)S(1)}) custom-call(s32[2]{0:T(128)S(1)} %pad_add_fusion.core_ref, bf16[512,2048]{1,0:T(8,128)(2,1)S(1)} %copy-done, bf16[512,2048]{1,0:T(8,128)(2,1)S(1)} %copy-done.1, bf16[8,512,128]{2,1,0:T(8,128)(2,1)S(1)} %get-tuple-element.84.refs_2_.refs_1_, ...), custom_call_target="tpu_custom_call", output_to_operand_aliasing={{0}: (11, {})} | custom-call | flops 402653184 | bytes 8388608 | tf_op jit(solution)/shard_map/query/pallas_call | solution.py:338
  56.9 0.0 copy-start.2
  56.9 21.1 %collective-permute-done.13 = f32[4,128,128]{2,1,0:T(8,128)S(1)} collective-permute-done((f32[4,128,128]{2,1,0:T(8,128)S(1)}, f32[4,128,128]{2,1,0:T(8,128)S(1)}, u32[]{:S(2)}, u32[]{:S(2)}) %collective-permute-start.13) | collective-permute-done | bytes 262176 | tf_op jit(solution)/shard_map/ppermute | solution.py:450
  78.0 0.1 fusion.2
  78.1 0.1 collective-permute-start.15
  78.2 1.3 %collective-permute-start.14 = (f32[4,128,128]{2,1,0:T(8,128)S(1)}, f32[4,128,128]{2,1,0:T(8,128)S(1)}, u32[]{:S(2)}, u32[]{:S(2)}) collective-permute-start(f32[4,128,128]{2,1,0:T(8,128)S(1)} %get-tuple-element.128), channel_id=1, source_target_pairs={{4,0},{5,1},{6,2},{7,3},{20,16},{21,17},{22,18},{23,19}} | collective-permute-start | bytes 786440 | tf_op jit(solution)/shard_map/ppermute | solution.py:450
  79.5 0.1 fusion.3.refs_8_
  79.6 0.2 collective-permute-done.15.refs_9_
  79.7 0.0 copy-done.2
  79.8 4.1 %backward.2 = (bf16[512,2048]{1,0:T(8,128)(2,1)}, bf16[512,2048]{1,0:T(8,128)(2,1)}) custom-call(s32[2]{0:T(128)S(1)} %pad_add_fusion.core_ref, bf16[512,2048]{1,0:T(8,128)(2,1)S(1)} %copy-done.2, bf16[8,512,128]{2,1,0:T(8,128)(2,1)S(1)} %get-tuple-element.85.refs_2_.refs_1_, bf16[8,512,128]{2,1,0:T(8,128)(2,1)S(1)} %get-tuple-element.101.refs_2_, ...), custom_call_target="tpu_custom_call" | custom-call | flops 536870912 | bytes 10485760 | tf_op jit(solution)/shard_map/backward/pallas_call | solution.py:338
  83.9 4.9 %collective-permute-done.14 = f32[4,128,128]{2,1,0:T(8,128)S(1)} collective-permute-done((f32[4,128,128]{2,1,0:T(8,128)S(1)}, f32[4,128,128]{2,1,0:T(8,128)S(1)}, u32[]{:S(2)}, u32[]{:S(2)}) %collective-permute-start.14) | collective-permute-done | bytes 262176 | tf_op jit(solution)/shard_map/ppermute | solution.py:450
  88.8 0.1 fusion
  88.9 0.1 collective-permute-start.16
  89.1 1.5 %collective-permute-done.16.refs_9_ = f32[4,128,128]{2,1,0:T(8,128)S(1)} collective-permute-done((f32[4,128,128]{2,1,0:T(8,128)S(1)}, f32[4,128,128]{2,1,0:T(8,128)S(1)}, u32[]{:S(2)}, u32[]{:S(2)}) %collective-permute-start.16) | collective-permute-done | bytes 262176 | tf_op jit(solution)/shard_map/ppermute | solution.py:430
  90.5 4.1 %backward.3 = (bf16[512,2048]{1,0:T(8,128)(2,1)}, bf16[512,2048]{1,0:T(8,128)(2,1)}) custom-call(s32[2]{0:T(128)S(1)} %pad_add_fusion.core_ref, bf16[512,2048]{1,0:T(8,128)(2,1)S(1)} %copy-done.2, bf16[8,512,128]{2,1,0:T(8,128)(2,1)S(1)} %get-tuple-element.84.refs_2_.refs_1_, ...), custom_call_target="tpu_custom_call", output_to_operand_aliasing={{0}: (11, {}), {1}: (12, {})} | custom-call | flops 536870912 | bytes 10485760 | tf_op jit(solution)/shard_map/backward/pallas_call | solution.py:338
  (11 shorter events, 0.3 us)
Async XLA Ops:
  7.2 1.4 %collective-permute-start = (f32[16,128]{1,0:T(8,128)S(1)}, f32[16,128]{1,0:T(8,128)S(1)}, u32[]{:S(2)}, u32[]{:S(2)}) collective-permute-start(f32[16,128]{1,0:T(8,128)S(1)} %get-tuple-element.63), channel_id=1, source_target_pairs={{0,1},{1,0},{2,3},{3,2},{4,5},{5,4},{6,7},{7,6},{8,9},{9,8},{10,11... | collective-permute-start | bytes 24584 | tf_op jit(solution)/shard_map/ppermute | solution.py:399
  7.7 12.7 %collective-permute-start.1 = (f32[4,128,128]{2,1,0:T(8,128)S(1)}, f32[4,128,128]{2,1,0:T(8,128)S(1)}, u32[]{:S(2)}, u32[]{:S(2)}) collective-permute-start(f32[4,128,128]{2,1,0:T(8,128)S(1)} %get-tuple-element.65), channel_id=1, source_target_pairs={{0,1},{1,0},{2,3},{3,2},{4,5},{5,4},{6,7},{7,6},{8,9},{9,8},{10,11... | collective-permute-start | bytes 786440 | tf_op jit(solution)/shard_map/ppermute | solution.py:412
  7.8 1.8 %collective-permute-start.2 = (f32[4,128,128]{2,1,0:T(8,128)S(1)}, f32[4,128,128]{2,1,0:T(8,128)S(1)}, u32[]{:S(2)}, u32[]{:S(2)}) collective-permute-start(f32[4,128,128]{2,1,0:T(8,128)S(1)} %get-tuple-element.67), channel_id=1, source_target_pairs={{0,1},{1,0},{2,3},{3,2},{4,5},{5,4},{6,7},{7,6},{8,9},{9,8},{10,11... | collective-permute-start | bytes 786440 | tf_op jit(solution)/shard_map/ppermute | solution.py:412
  9.7 10.7 %collective-permute-start.3 = (f32[4,128,128]{2,1,0:T(8,128)S(1)}, f32[4,128,128]{2,1,0:T(8,128)S(1)}, u32[]{:S(2)}, u32[]{:S(2)}) collective-permute-start(f32[4,128,128]{2,1,0:T(8,128)S(1)} %select_add_fusion.3.refs_8_), channel_id=1, source_target_pairs={{0,4},{1,5},{2,6},{3,7},{16,20},{17,21},{18,22},{19,23}} | collective-permute-start | bytes 786440 | tf_op jit(solution)/shard_map/ppermute | solution.py:450
  20.5 9.7 %collective-permute-start.4 = (f32[4,128,128]{2,1,0:T(8,128)S(1)}, f32[4,128,128]{2,1,0:T(8,128)S(1)}, u32[]{:S(2)}, u32[]{:S(2)}) collective-permute-start(f32[4,128,128]{2,1,0:T(8,128)S(1)} %get-tuple-element.123.refs_8_), channel_id=1, source_target_pairs={{0,4},{4,8},{1,5},{5,9},{2,6},{6,10},{3,7},{7,11},{16,20},{20,24},... | collective-permute-start | bytes 786440 | tf_op jit(solution)/shard_map/ppermute | solution.py:450
  30.2 2.6 %copy-start.3 = (bf16[512,2048]{1,0:T(8,128)(2,1)S(1)}, bf16[512,2048]{1,0:T(8,128)(2,1)}, u32[]{:S(2)}) copy-start(bf16[512,2048]{1,0:T(8,128)(2,1)} %refs_2_.9) | copy-start | bytes 6291460
  30.2 0.8 collective-permute-start.5
  31.2 1.6 %collective-permute-start.7 = (f32[4,128,128]{2,1,0:T(8,128)S(1)}, f32[4,128,128]{2,1,0:T(8,128)S(1)}, u32[]{:S(2)}, u32[]{:S(2)}) collective-permute-start(f32[4,128,128]{2,1,0:T(8,128)S(1)} %get-tuple-element.118), channel_id=1, source_target_pairs={{0,1},{1,0},{2,3},{3,2},{4,5},{5,4},{6,7},{7,6},{8,9},{9,8},{10,11... | collective-permute-start | bytes 786440 | tf_op jit(solution)/shard_map/ppermute | solution.py:430
  31.3 6.2 %collective-permute-start.6 = (f32[4,128,128]{2,1,0:T(8,128)S(1)}, f32[4,128,128]{2,1,0:T(8,128)S(1)}, u32[]{:S(2)}, u32[]{:S(2)}) collective-permute-start(f32[4,128,128]{2,1,0:T(8,128)S(1)} %get-tuple-element.129), channel_id=1, source_target_pairs={{8,12},{9,13},{10,14},{11,15},{24,28},{25,29},{26,30},{27,31}} | collective-permute-start | bytes 786440 | tf_op jit(solution)/shard_map/ppermute | solution.py:450
  37.5 1.6 %collective-permute-start.9 = (f32[4,128,128]{2,1,0:T(8,128)S(1)}, f32[4,128,128]{2,1,0:T(8,128)S(1)}, u32[]{:S(2)}, u32[]{:S(2)}) collective-permute-start(f32[4,128,128]{2,1,0:T(8,128)S(1)} %get-tuple-element.82), channel_id=1, source_target_pairs={{0,1},{1,0},{2,3},{3,2},{4,5},{5,4},{6,7},{7,6},{8,9},{9,8},{10,11... | collective-permute-start | bytes 786440 | tf_op jit(solution)/shard_map/ppermute | solution.py:412
  37.8 2.1 %collective-permute-start.8 = (f32[4,128,128]{2,1,0:T(8,128)S(1)}, f32[4,128,128]{2,1,0:T(8,128)S(1)}, u32[]{:S(2)}, u32[]{:S(2)}) collective-permute-start(f32[4,128,128]{2,1,0:T(8,128)S(1)} %get-tuple-element.116), channel_id=1, source_target_pairs={{0,1},{1,0},{2,3},{3,2},{4,5},{5,4},{6,7},{7,6},{8,9},{9,8},{10,11... | collective-permute-start | bytes 786440 | tf_op jit(solution)/shard_map/ppermute | solution.py:430
  39.1 5.7 %collective-permute-start.11 = (f32[4,128,128]{2,1,0:T(8,128)S(1)}, f32[4,128,128]{2,1,0:T(8,128)S(1)}, u32[]{:S(2)}, u32[]{:S(2)}) collective-permute-start(f32[4,128,128]{2,1,0:T(8,128)S(1)} %select_add_fusion.1.refs_8_), channel_id=1, source_target_pairs={{12,8},{13,9},{14,10},{15,11},{28,24},{29,25},{30,26},{31,27}} | collective-permute-start | bytes 786440 | tf_op jit(solution)/shard_map/ppermute | solution.py:450
  39.9 7.1 %copy-start.1 = (bf16[512,2048]{1,0:T(8,128)(2,1)S(1)}, bf16[512,2048]{1,0:T(8,128)(2,1)}, u32[]{:S(2)}) copy-start(bf16[512,2048]{1,0:T(8,128)(2,1)} %refs_1_.7) | copy-start | bytes 6291460
  44.6 2.4 %copy-start = (bf16[512,2048]{1,0:T(8,128)(2,1)S(1)}, bf16[512,2048]{1,0:T(8,128)(2,1)}, u32[]{:S(2)}) copy-start(bf16[512,2048]{1,0:T(8,128)(2,1)} %refs_0_.11) | copy-start | bytes 6291460
  44.6 1.6 %collective-permute-start.10 = (f32[4,128,128]{2,1,0:T(8,128)S(1)}, f32[4,128,128]{2,1,0:T(8,128)S(1)}, u32[]{:S(2)}, u32[]{:S(2)}) collective-permute-start(f32[4,128,128]{2,1,0:T(8,128)S(1)} %get-tuple-element.86), channel_id=1, source_target_pairs={{0,1},{1,0},{2,3},{3,2},{4,5},{5,4},{6,7},{7,6},{8,9},{9,8},{10,11... | collective-permute-start | bytes 786440 | tf_op jit(solution)/shard_map/ppermute | solution.py:412
  46.3 4.9 %collective-permute-start.12 = (f32[4,128,128]{2,1,0:T(8,128)S(1)}, f32[4,128,128]{2,1,0:T(8,128)S(1)}, u32[]{:S(2)}, u32[]{:S(2)}) collective-permute-start(f32[4,128,128]{2,1,0:T(8,128)S(1)} %get-tuple-element.114.refs_10_), channel_id=1, source_target_pairs={{12,8},{8,4},{13,9},{9,5},{14,10},{10,6},{15,11},{11,7},{28,24},{2... | collective-permute-start | bytes 786440 | tf_op jit(solution)/shard_map/ppermute | solution.py:450
  51.3 26.7 %collective-permute-start.13 = (f32[4,128,128]{2,1,0:T(8,128)S(1)}, f32[4,128,128]{2,1,0:T(8,128)S(1)}, u32[]{:S(2)}, u32[]{:S(2)}) collective-permute-start(f32[4,128,128]{2,1,0:T(8,128)S(1)} %add_select_fusion.refs_11_), channel_id=1, source_target_pairs={{8,4},{4,0},{9,5},{5,1},{10,6},{6,2},{11,7},{7,3},{24,20},{20,16},... | collective-permute-start | bytes 786440 | tf_op jit(solution)/shard_map/ppermute | solution.py:450
  56.9 22.9 %copy-start.2 = (bf16[512,2048]{1,0:T(8,128)(2,1)S(1)}, bf16[512,2048]{1,0:T(8,128)(2,1)}, u32[]{:S(2)}) copy-start(bf16[512,2048]{1,0:T(8,128)(2,1)} %refs_0_.13) | copy-start | bytes 6291460
  78.1 1.6 %collective-permute-start.15 = (f32[4,128,128]{2,1,0:T(8,128)S(1)}, f32[4,128,128]{2,1,0:T(8,128)S(1)}, u32[]{:S(2)}, u32[]{:S(2)}) collective-permute-start(f32[4,128,128]{2,1,0:T(8,128)S(1)} %get-tuple-element.112), channel_id=1, source_target_pairs={{0,1},{1,0},{2,3},{3,2},{4,5},{5,4},{6,7},{7,6},{8,9},{9,8},{10,11... | collective-permute-start | bytes 786440 | tf_op jit(solution)/shard_map/ppermute | solution.py:430
  78.2 10.6 %collective-permute-start.14 = (f32[4,128,128]{2,1,0:T(8,128)S(1)}, f32[4,128,128]{2,1,0:T(8,128)S(1)}, u32[]{:S(2)}, u32[]{:S(2)}) collective-permute-start(f32[4,128,128]{2,1,0:T(8,128)S(1)} %get-tuple-element.128), channel_id=1, source_target_pairs={{4,0},{5,1},{6,2},{7,3},{20,16},{21,17},{22,18},{23,19}} | collective-permute-start | bytes 786440 | tf_op jit(solution)/shard_map/ppermute | solution.py:450
  88.9 1.6 %collective-permute-start.16 = (f32[4,128,128]{2,1,0:T(8,128)S(1)}, f32[4,128,128]{2,1,0:T(8,128)S(1)}, u32[]{:S(2)}, u32[]{:S(2)}) collective-permute-start(f32[4,128,128]{2,1,0:T(8,128)S(1)} %get-tuple-element.110), channel_id=1, source_target_pairs={{0,1},{1,0},{2,3},{3,2},{4,5},{5,4},{6,7},{7,6},{8,9},{9,8},{10,11... | collective-permute-start | bytes 786440 | tf_op jit(solution)/shard_map/ppermute | solution.py:430

commit v6 on v4

--- a/solution.py
+++ b/solution.py
@@ -11,7 +11,7 @@
 EPS = 1e-06
 NEG = -1e30
 GROUPS = 2
-PER_STEP = 2
+PER_STEP = 4
 F32 = jnp.float32
 BF16 = jnp.bfloat16
 VMEM_LIMIT = 20 * 1024 * 1024
@@ -364,7 +364,7 @@
     groups = GROUPS
     size = heads // groups
     quarter = size // 2
-    dims = Dims(size, PER_STEP, chunks, length, dh, heads)
+    dims = Dims(size, min(PER_STEP, quarter), chunks, length, dh, heads)
     shards = lax.axis_size("seq")
     core = lax.axis_index("ctx")
     first = core == 0

time: 91.7 us -> 90.4 us (0.986)
  Pallas kernels: 36.2 us -> 32.5 us
  waiting for transfers between devices: 36.9 us -> 39.3 us
    pallas_call x9, Pallas kernels: 36.2 us -> 32.5 us  [call_heads(): pl.pallas_call(functools.partial(with_rows, kernel, dims, group, which, l...]
    ppermute x12, waiting for transfers between devices: 31.5 us -> 33.9 us  [hop(): self.landed.append(lax.ppermute(self.sent, 'seq', [self.hops[index]]))]
  transfers between devices with their start and end apart: 21 -> 21, of which waited for: 11 -> 11; matrix products, arithmetic and copies ran while one was open for 1% -> 1% of each run, Pallas kernels for 29% -> 27%
where the time goes in v6:
time: 90.4 us; the launch traced here: 90 us
  waiting for transfers between devices  39.3 us (43%)
  Pallas kernels  32.5 us (36%)
  starting transfers between devices  16.3 us (18%)
  between operations  1 us (1%)
    ppermute x12, waiting for transfers between devices, hop(): self.landed.append(lax.ppermute(self.sent, 'seq', [self.hops[index]]))  33.9 us
    pallas_call x9, Pallas kernels, call_heads(): pl.pallas_call(functools.partial(with_rows, kernel, dims, group, which, l...  32.5 us
    ppermute x12, starting transfers between devices, hop(): self.landed.append(lax.ppermute(self.sent, 'seq', [self.hops[index]]))  14.2 us
    ppermute x4, waiting for transfers between devices, finish(): return (keep, lax.ppermute(send, 'ctx', swap))  2.58 us
    ppermute x4, waiting for transfers between devices, __init__(): self.mine, self.got = (mine, lax.ppermute(other, 'ctx', swap))  2.49 us
  transfers between devices with their start and end apart: 21, of which 11 were waited for; matrix products, arithmetic and copies ran while one was open for 1% of the time, Pallas kernels for 27%

profile of v6, /device:TPU:0, one launch (start us, length us, event | category | flops | bytes accessed | tf_op | source)
XLA Modules:
  0.0 90.0 jit_solution(4599571476941861369)
XLA Ops:
  0.6 5.1 %begin.1 = (f32[4,128,128]{2,1,0:T(8,128)S(1)}, f32[4,128,128]{2,1,0:T(8,128)S(1)}, f32[4,128,128]{2,1,0:T(8,128)S(1)}, f32[4,128,128]{2,1,0:T(8,128)S(1)}, f32[...) custom-call(s32[1]{0:T(128)} %bitcast.core_ref, ...), custom_call_target="tpu_custom_call" | custom-call | flops 134217728 | bytes 4194304 | tf_op jit(solution)/shard_map/begin/pallas_call | solution.py:335
  5.7 0.5 collective-permute-start
  6.2 0.1 collective-permute-start.1
  6.3 0.4 collective-permute-start.2
  6.7 0.3 collective-permute-done
  7.1 1.1 %collective-permute-done.2 = f32[4,128,128]{2,1,0:T(8,128)S(1)} collective-permute-done((f32[4,128,128]{2,1,0:T(8,128)S(1)}, f32[4,128,128]{2,1,0:T(8,128)S(1)}, u32[]{:S(2)}, u32[]{:S(2)}) %collective-permute-start.2) | collective-permute-done | bytes 262176 | tf_op jit(solution)/shard_map/ppermute | solution.py:408
  8.2 4.6 %collective-permute-start.4 = (f32[4,128,128]{2,1,0:T(8,128)S(1)}, f32[4,128,128]{2,1,0:T(8,128)S(1)}, u32[]{:S(2)}, u32[]{:S(2)}) collective-permute-start(f32[4,128,128]{2,1,0:T(8,128)S(1)} %select_add_fusion.3), channel_id=1, source_target_pairs={{0,4},{1,5},{2,6},{3,7},{16,20},{17,21},{18,22},{19,23}} | collective-permute-start | bytes 786440 | tf_op jit(solution)/shard_map/ppermute | solution.py:431
  12.8 0.0 collective-permute-done.1
  12.9 1.3 %collective-permute-start.3 = (f32[4,128,128]{2,1,0:T(8,128)S(1)}, f32[4,128,128]{2,1,0:T(8,128)S(1)}, u32[]{:S(2)}, u32[]{:S(2)}) collective-permute-start(f32[4,128,128]{2,1,0:T(8,128)S(1)} %select_add_fusion.2), channel_id=1, source_target_pairs={{0,4},{1,5},{2,6},{3,7},{16,20},{17,21},{18,22},{19,23}} | collective-permute-start | bytes 786440 | tf_op jit(solution)/shard_map/ppermute | solution.py:431
  14.2 5.2 %collective-permute-done.4 = f32[4,128,128]{2,1,0:T(8,128)S(1)} collective-permute-done((f32[4,128,128]{2,1,0:T(8,128)S(1)}, f32[4,128,128]{2,1,0:T(8,128)S(1)}, u32[]{:S(2)}, u32[]{:S(2)}) %collective-permute-start.4) | collective-permute-done | bytes 262176 | tf_op jit(solution)/shard_map/ppermute | solution.py:431
  19.5 0.7 collective-permute-start.6
  20.2 4.3 %collective-permute-done.3 = f32[4,128,128]{2,1,0:T(8,128)S(1)} collective-permute-done((f32[4,128,128]{2,1,0:T(8,128)S(1)}, f32[4,128,128]{2,1,0:T(8,128)S(1)}, u32[]{:S(2)}, u32[]{:S(2)}) %collective-permute-start.3) | collective-permute-done | bytes 262176 | tf_op jit(solution)/shard_map/ppermute | solution.py:431
  24.5 0.7 collective-permute-start.5
  25.2 3.9 %inside.2 = (f32[8,3,128,128]{3,2,1,0:T(8,128)S(1)}, f32[8,512,128]{2,1,0:T(8,128)S(1)}, bf16[8,512,128]{2,1,0:T(8,128)(2,1)S(1)}, bf16[8,512,128]{2,1,0:T(8,128...) custom-call(s32[1]{0:T(128)} %bitcast.core_ref, bf16[512,2048]{1,0:T(8,128)(2,1)} %refs_0_.13, ...), custom_call_target="tpu_custom_call" | custom-call | flops 536870912 | bytes 10485760 | tf_op jit(solution)/shard_map/inside/pallas_call | solution.py:335
  29.1 3.9 %inside.3 = (f32[8,3,128,128]{3,2,1,0:T(8,128)S(1)}, f32[8,512,128]{2,1,0:T(8,128)S(1)}, bf16[8,512,128]{2,1,0:T(8,128)(2,1)S(1)}, bf16[8,512,128]{2,1,0:T(8,128...) custom-call(s32[1]{0:T(128)} %bitcast.core_ref, bf16[512,2048]{1,0:T(8,128)(2,1)} %refs_0_.13, ...), custom_call_target="tpu_custom_call" | custom-call | flops 536870912 | bytes 10485760 | tf_op jit(solution)/shard_map/inside/pallas_call | solution.py:335
  33.1 0.0 collective-permute-done.6
  33.1 0.0 copy-start.3
  33.1 0.1 multiply_add_fusion.9
  33.2 0.8 collective-permute-start.8
  34.0 0.0 collective-permute-done.5
  34.0 0.1 multiply_add_fusion.8
  34.0 0.0 collective-permute-done.8
  34.1 0.1 fusion.6
  34.1 0.1 collective-permute-start.9
  34.2 0.7 collective-permute-start.7
  34.9 0.8 collective-permute-done.9.refs_6_.refs_9_
  35.7 0.0 copy-done.3
  35.8 3.3 %forward.2 = (bf16[512,2048]{1,0:T(8,128)(2,1)}, bf16[8,512,128]{2,1,0:T(8,128)(2,1)S(1)}, f32[8,3,128,128]{3,2,1,0:T(8,128)S(1)}, f32[4,128,128]{2,1,0:T(8,128)S(1)}, f32[4,128,128]{2,1,0:T(8,128)S(1)}) custom-call(s32[1]{0:T(128)} %bitcast.core_ref, f32[8,512,128]{2,1,0:T(8,128)S(1)} %get-tuple-element.77.refs_0_, ...), custom_call_target="tpu_custom_call" | custom-call | flops 268435456 | bytes 8388608 | tf_op jit(solution)/shard_map/forward/pallas_call | solution.py:335
  39.0 0.0 collective-permute-done.7
  39.1 0.2 collective-permute-start.11
  39.3 0.1 fusion.4
  39.3 0.4 collective-permute-start.10
  39.8 0.9 collective-permute-done.11
  40.7 0.7 collective-permute-start.13
  41.4 0.0 collective-permute-done.10.refs_6_.refs_9_
  41.4 0.0 copy-start.1
  41.4 3.4 %forward.3 = (bf16[512,2048]{1,0:T(8,128)(2,1)}, bf16[8,512,128]{2,1,0:T(8,128)(2,1)S(1)}, f32[8,3,128,128]{3,2,1,0:T(8,128)S(1)}, f32[4,128,128]{2,1,0:T(8,128)S(1)}, f32[4,128,128]{2,1,0:T(8,128)S(1)}) custom-call(s32[1]{0:T(128)} %bitcast.core_ref, f32[8,512,128]{2,1,0:T(8,128)S(1)} %get-tuple-element.72.refs_0_, ...), custom_call_target="tpu_custom_call", output_to_operand_aliasing={{0}: (8, {})} | custom-call | flops 268435456 | bytes 8388608 | tf_op jit(solution)/shard_map/forward/pallas_call | solution.py:335
  44.8 0.0 copy-start
  44.8 0.2 collective-permute-start.12
  45.0 0.0 collective-permute-done.13
  45.1 0.8 collective-permute-start.15
  45.9 0.5 collective-permute-done.12
  46.5 0.7 collective-permute-start.14
  47.2 0.0 collective-permute-done.15
  47.2 0.1 multiply_add_fusion.4
  47.2 0.0 collective-permute-done.14
  47.3 0.7 collective-permute-start.16
  48.0 1.3 %collective-permute-start.18 = (f32[4,128,128]{2,1,0:T(8,128)S(1)}, f32[4,128,128]{2,1,0:T(8,128)S(1)}, u32[]{:S(2)}, u32[]{:S(2)}) collective-permute-start(f32[4,128,128]{2,1,0:T(8,128)S(1)} %get-tuple-element.114), channel_id=1, source_target_pairs={{4,0},{5,1},{6,2},{7,3},{20,16},{21,17},{22,18},{23,19}} | collective-permute-start | bytes 786440 | tf_op jit(solution)/shard_map/ppermute | solution.py:431
  49.3 3.4 %query.2 = (bf16[512,2048]{1,0:T(8,128)(2,1)}, bf16[8,512,128]{2,1,0:T(8,128)(2,1)S(1)}) custom-call(s32[1]{0:T(128)} %bitcast.core_ref, bf16[512,2048]{1,0:T(8,128)(2,1)S(1)} %copy-done, bf16[512,2048]{1,0:T(8,128)(2,1)S(1)} %copy-done.1, bf16[8,512,128]{2,1,0:T(8,128)(2,1)S(1)} %get-tuple-element.86.refs_2_.refs_1_, ...), custom_call_target="tpu_custom_call" | custom-call | flops 402653184 | bytes 8388608 | tf_op jit(solution)/shard_map/query/pallas_call | solution.py:335
  52.7 3.4 %query.3 = (bf16[512,2048]{1,0:T(8,128)(2,1)}, bf16[8,512,128]{2,1,0:T(8,128)(2,1)S(1)}) custom-call(s32[1]{0:T(128)} %bitcast.core_ref, bf16[512,2048]{1,0:T(8,128)(2,1)S(1)} %copy-done, bf16[512,2048]{1,0:T(8,128)(2,1)S(1)} %copy-done.1, bf16[8,512,128]{2,1,0:T(8,128)(2,1)S(1)} %get-tuple-element.85.refs_2_.refs_1_, ...), custom_call_target="tpu_custom_call", output_to_operand_aliasing={{0}: (11, {})} | custom-call | flops 402653184 | bytes 8388608 | tf_op jit(solution)/shard_map/query/pallas_call | solution.py:335
  56.1 0.0 copy-start.2
  56.1 0.0 collective-permute-done.16
  56.1 0.1 multiply_add_fusion.2
  56.2 18.3 %collective-permute-done.18 = f32[4,128,128]{2,1,0:T(8,128)S(1)} collective-permute-done((f32[4,128,128]{2,1,0:T(8,128)S(1)}, f32[4,128,128]{2,1,0:T(8,128)S(1)}, u32[]{:S(2)}, u32[]{:S(2)}) %collective-permute-start.18) | collective-permute-done | bytes 262176 | tf_op jit(solution)/shard_map/ppermute | solution.py:431
  74.5 0.1 fusion.2
  74.6 0.1 collective-permute-start.19
  74.7 1.3 %collective-permute-start.17 = (f32[4,128,128]{2,1,0:T(8,128)S(1)}, f32[4,128,128]{2,1,0:T(8,128)S(1)}, u32[]{:S(2)}, u32[]{:S(2)}) collective-permute-start(f32[4,128,128]{2,1,0:T(8,128)S(1)} %get-tuple-element.112), channel_id=1, source_target_pairs={{4,0},{5,1},{6,2},{7,3},{20,16},{21,17},{22,18},{23,19}} | collective-permute-start | bytes 786440 | tf_op jit(solution)/shard_map/ppermute | solution.py:431
  76.0 0.2 collective-permute-done.19.refs_9_
  76.2 3.1 %backward.2 = (bf16[512,2048]{1,0:T(8,128)(2,1)}, bf16[512,2048]{1,0:T(8,128)(2,1)}) custom-call(s32[1]{0:T(128)} %bitcast.core_ref, bf16[512,2048]{1,0:T(8,128)(2,1)S(1)} %copy-done.2, bf16[8,512,128]{2,1,0:T(8,128)(2,1)S(1)} %get-tuple-element.86.refs_2_.refs_1_, bf16[8,512,128]{2,1,0:T(8,128)(2,1)S(1)} %get-tuple-element.102.refs_2_, ...), custom_call_target="tpu_custom_call" | custom-call | flops 536870912 | bytes 10485760 | tf_op jit(solution)/shard_map/backward/pallas_call | solution.py:335
  79.3 6.0 %collective-permute-done.17 = f32[4,128,128]{2,1,0:T(8,128)S(1)} collective-permute-done((f32[4,128,128]{2,1,0:T(8,128)S(1)}, f32[4,128,128]{2,1,0:T(8,128)S(1)}, u32[]{:S(2)}, u32[]{:S(2)}) %collective-permute-start.17) | collective-permute-done | bytes 262176 | tf_op jit(solution)/shard_map/ppermute | solution.py:431
  85.3 0.1 fusion
  85.3 0.1 collective-permute-start.20
  85.4 1.5 %collective-permute-done.20.refs_9_ = f32[4,128,128]{2,1,0:T(8,128)S(1)} collective-permute-done((f32[4,128,128]{2,1,0:T(8,128)S(1)}, f32[4,128,128]{2,1,0:T(8,128)S(1)}, u32[]{:S(2)}, u32[]{:S(2)}) %collective-permute-start.20) | collective-permute-done | bytes 262176 | tf_op jit(solution)/shard_map/ppermute | solution.py:446
  86.9 3.1 %backward.3 = (bf16[512,2048]{1,0:T(8,128)(2,1)}, bf16[512,2048]{1,0:T(8,128)(2,1)}) custom-call(s32[1]{0:T(128)} %bitcast.core_ref, bf16[512,2048]{1,0:T(8,128)(2,1)S(1)} %copy-done.2, bf16[8,512,128]{2,1,0:T(8,128)(2,1)S(1)} %get-tuple-element.85.refs_2_.refs_1_, ...), custom_call_target="tpu_custom_call", output_to_operand_aliasing={{0}: (11, {}), {1}: (12, {})} | custom-call | flops 536870912 | bytes 10485760 | tf_op jit(solution)/shard_map/backward/pallas_call | solution.py:335
  (13 shorter events, 0.3 us)
Async XLA Ops:
  5.7 1.3 %collective-permute-start = (f32[16,128]{1,0:T(8,128)S(1)}, f32[16,128]{1,0:T(8,128)S(1)}, u32[]{:S(2)}, u32[]{:S(2)}) collective-permute-start(f32[16,128]{1,0:T(8,128)S(1)} %get-tuple-element.63), channel_id=1, source_target_pairs={{0,1},{1,0},{2,3},{3,2},{4,5},{5,4},{6,7},{7,6},{8,9},{9,8},{10,11... | collective-permute-start | bytes 24584 | tf_op jit(solution)/shard_map/ppermute | solution.py:395
  6.2 6.6 %collective-permute-start.1 = (f32[4,128,128]{2,1,0:T(8,128)S(1)}, f32[4,128,128]{2,1,0:T(8,128)S(1)}, u32[]{:S(2)}, u32[]{:S(2)}) collective-permute-start(f32[4,128,128]{2,1,0:T(8,128)S(1)} %get-tuple-element.65), channel_id=1, source_target_pairs={{0,1},{1,0},{2,3},{3,2},{4,5},{5,4},{6,7},{7,6},{8,9},{9,8},{10,11... | collective-permute-start | bytes 786440 | tf_op jit(solution)/shard_map/ppermute | solution.py:408
  6.3 1.8 %collective-permute-start.2 = (f32[4,128,128]{2,1,0:T(8,128)S(1)}, f32[4,128,128]{2,1,0:T(8,128)S(1)}, u32[]{:S(2)}, u32[]{:S(2)}) collective-permute-start(f32[4,128,128]{2,1,0:T(8,128)S(1)} %get-tuple-element.67), channel_id=1, source_target_pairs={{0,1},{1,0},{2,3},{3,2},{4,5},{5,4},{6,7},{7,6},{8,9},{9,8},{10,11... | collective-permute-start | bytes 786440 | tf_op jit(solution)/shard_map/ppermute | solution.py:408
  8.2 11.3 %collective-permute-start.4 = (f32[4,128,128]{2,1,0:T(8,128)S(1)}, f32[4,128,128]{2,1,0:T(8,128)S(1)}, u32[]{:S(2)}, u32[]{:S(2)}) collective-permute-start(f32[4,128,128]{2,1,0:T(8,128)S(1)} %select_add_fusion.3), channel_id=1, source_target_pairs={{0,4},{1,5},{2,6},{3,7},{16,20},{17,21},{18,22},{19,23}} | collective-permute-start | bytes 786440 | tf_op jit(solution)/shard_map/ppermute | solution.py:431
  12.9 11.6 %collective-permute-start.3 = (f32[4,128,128]{2,1,0:T(8,128)S(1)}, f32[4,128,128]{2,1,0:T(8,128)S(1)}, u32[]{:S(2)}, u32[]{:S(2)}) collective-permute-start(f32[4,128,128]{2,1,0:T(8,128)S(1)} %select_add_fusion.2), channel_id=1, source_target_pairs={{0,4},{1,5},{2,6},{3,7},{16,20},{17,21},{18,22},{19,23}} | collective-permute-start | bytes 786440 | tf_op jit(solution)/shard_map/ppermute | solution.py:431
  19.5 13.6 %collective-permute-start.6 = (f32[4,128,128]{2,1,0:T(8,128)S(1)}, f32[4,128,128]{2,1,0:T(8,128)S(1)}, u32[]{:S(2)}, u32[]{:S(2)}) collective-permute-start(f32[4,128,128]{2,1,0:T(8,128)S(1)} %multiply_add_fusion.11), channel_id=1, source_target_pairs={{4,8},{5,9},{6,10},{7,11},{20,24},{21,25},{22,26},{23,27}} | collective-permute-start | bytes 786440 | tf_op jit(solution)/shard_map/ppermute | solution.py:431
  24.5 9.4 %collective-permute-start.5 = (f32[4,128,128]{2,1,0:T(8,128)S(1)}, f32[4,128,128]{2,1,0:T(8,128)S(1)}, u32[]{:S(2)}, u32[]{:S(2)}) collective-permute-start(f32[4,128,128]{2,1,0:T(8,128)S(1)} %multiply_add_fusion.10.refs_8_), channel_id=1, source_target_pairs={{4,8},{5,9},{6,10},{7,11},{20,24},{21,25},{22,26},{23,27}} | collective-permute-start | bytes 786440 | tf_op jit(solution)/shard_map/ppermute | solution.py:431
  33.1 2.7 %copy-start.3 = (bf16[512,2048]{1,0:T(8,128)(2,1)S(1)}, bf16[512,2048]{1,0:T(8,128)(2,1)}, u32[]{:S(2)}) copy-start(bf16[512,2048]{1,0:T(8,128)(2,1)} %refs_2_.9) | copy-start | bytes 6291460
  33.2 0.9 collective-permute-start.8
  34.1 1.6 %collective-permute-start.9 = (f32[4,128,128]{2,1,0:T(8,128)S(1)}, f32[4,128,128]{2,1,0:T(8,128)S(1)}, u32[]{:S(2)}, u32[]{:S(2)}) collective-permute-start(f32[4,128,128]{2,1,0:T(8,128)S(1)} %get-tuple-element.132), channel_id=1, source_target_pairs={{0,1},{1,0},{2,3},{3,2},{4,5},{5,4},{6,7},{7,6},{8,9},{9,8},{10,11... | collective-permute-start | bytes 786440 | tf_op jit(solution)/shard_map/ppermute | solution.py:446
  34.2 4.8 %collective-permute-start.7 = (f32[4,128,128]{2,1,0:T(8,128)S(1)}, f32[4,128,128]{2,1,0:T(8,128)S(1)}, u32[]{:S(2)}, u32[]{:S(2)}) collective-permute-start(f32[4,128,128]{2,1,0:T(8,128)S(1)} %get-tuple-element.116), channel_id=1, source_target_pairs={{8,12},{9,13},{10,14},{11,15},{24,28},{25,29},{26,30},{27,31}} | collective-permute-start | bytes 786440 | tf_op jit(solution)/shard_map/ppermute | solution.py:431
  39.1 1.6 %collective-permute-start.11 = (f32[4,128,128]{2,1,0:T(8,128)S(1)}, f32[4,128,128]{2,1,0:T(8,128)S(1)}, u32[]{:S(2)}, u32[]{:S(2)}) collective-permute-start(f32[4,128,128]{2,1,0:T(8,128)S(1)} %get-tuple-element.83), channel_id=1, source_target_pairs={{0,1},{1,0},{2,3},{3,2},{4,5},{5,4},{6,7},{7,6},{8,9},{9,8},{10,11... | collective-permute-start | bytes 786440 | tf_op jit(solution)/shard_map/ppermute | solution.py:408
  39.3 2.1 %collective-permute-start.10 = (f32[4,128,128]{2,1,0:T(8,128)S(1)}, f32[4,128,128]{2,1,0:T(8,128)S(1)}, u32[]{:S(2)}, u32[]{:S(2)}) collective-permute-start(f32[4,128,128]{2,1,0:T(8,128)S(1)} %get-tuple-element.130), channel_id=1, source_target_pairs={{0,1},{1,0},{2,3},{3,2},{4,5},{5,4},{6,7},{7,6},{8,9},{9,8},{10,11... | collective-permute-start | bytes 786440 | tf_op jit(solution)/shard_map/ppermute | solution.py:446
  40.7 4.3 %collective-permute-start.13 = (f32[4,128,128]{2,1,0:T(8,128)S(1)}, f32[4,128,128]{2,1,0:T(8,128)S(1)}, u32[]{:S(2)}, u32[]{:S(2)}) collective-permute-start(f32[4,128,128]{2,1,0:T(8,128)S(1)} %select_add_fusion.1.refs_8_), channel_id=1, source_target_pairs={{12,8},{13,9},{14,10},{15,11},{28,24},{29,25},{30,26},{31,27}} | collective-permute-start | bytes 786440 | tf_op jit(solution)/shard_map/ppermute | solution.py:431
  41.4 7.9 %copy-start.1 = (bf16[512,2048]{1,0:T(8,128)(2,1)S(1)}, bf16[512,2048]{1,0:T(8,128)(2,1)}, u32[]{:S(2)}) copy-start(bf16[512,2048]{1,0:T(8,128)(2,1)} %refs_1_.7) | copy-start | bytes 6291460
  44.8 4.5 %copy-start = (bf16[512,2048]{1,0:T(8,128)(2,1)S(1)}, bf16[512,2048]{1,0:T(8,128)(2,1)}, u32[]{:S(2)}) copy-start(bf16[512,2048]{1,0:T(8,128)(2,1)} %refs_0_.11) | copy-start | bytes 6291460
  44.8 1.6 %collective-permute-start.12 = (f32[4,128,128]{2,1,0:T(8,128)S(1)}, f32[4,128,128]{2,1,0:T(8,128)S(1)}, u32[]{:S(2)}, u32[]{:S(2)}) collective-permute-start(f32[4,128,128]{2,1,0:T(8,128)S(1)} %get-tuple-element.87), channel_id=1, source_target_pairs={{0,1},{1,0},{2,3},{3,2},{4,5},{5,4},{6,7},{7,6},{8,9},{9,8},{10,11... | collective-permute-start | bytes 786440 | tf_op jit(solution)/shard_map/ppermute | solution.py:408
  45.1 2.1 %collective-permute-start.15 = (f32[4,128,128]{2,1,0:T(8,128)S(1)}, f32[4,128,128]{2,1,0:T(8,128)S(1)}, u32[]{:S(2)}, u32[]{:S(2)}) collective-permute-start(f32[4,128,128]{2,1,0:T(8,128)S(1)} %multiply_add_fusion.5), channel_id=1, source_target_pairs={{8,4},{9,5},{10,6},{11,7},{24,20},{25,21},{26,22},{27,23}} | collective-permute-start | bytes 786440 | tf_op jit(solution)/shard_map/ppermute | solution.py:431
  46.5 0.8 collective-permute-start.14
  47.3 8.8 %collective-permute-start.16 = (f32[4,128,128]{2,1,0:T(8,128)S(1)}, f32[4,128,128]{2,1,0:T(8,128)S(1)}, u32[]{:S(2)}, u32[]{:S(2)}) collective-permute-start(f32[4,128,128]{2,1,0:T(8,128)S(1)} %multiply_add_fusion.3.refs_10_), channel_id=1, source_target_pairs={{8,4},{9,5},{10,6},{11,7},{24,20},{25,21},{26,22},{27,23}} | collective-permute-start | bytes 786440 | tf_op jit(solution)/shard_map/ppermute | solution.py:431
  48.0 26.6 %collective-permute-start.18 = (f32[4,128,128]{2,1,0:T(8,128)S(1)}, f32[4,128,128]{2,1,0:T(8,128)S(1)}, u32[]{:S(2)}, u32[]{:S(2)}) collective-permute-start(f32[4,128,128]{2,1,0:T(8,128)S(1)} %get-tuple-element.114), channel_id=1, source_target_pairs={{4,0},{5,1},{6,2},{7,3},{20,16},{21,17},{22,18},{23,19}} | collective-permute-start | bytes 786440 | tf_op jit(solution)/shard_map/ppermute | solution.py:431
  56.1 20.1 %copy-start.2 = (bf16[512,2048]{1,0:T(8,128)(2,1)S(1)}, bf16[512,2048]{1,0:T(8,128)(2,1)}, u32[]{:S(2)}) copy-start(bf16[512,2048]{1,0:T(8,128)(2,1)} %refs_0_.13) | copy-start | bytes 6291460
  74.6 1.6 %collective-permute-start.19 = (f32[4,128,128]{2,1,0:T(8,128)S(1)}, f32[4,128,128]{2,1,0:T(8,128)S(1)}, u32[]{:S(2)}, u32[]{:S(2)}) collective-permute-start(f32[4,128,128]{2,1,0:T(8,128)S(1)} %get-tuple-element.128), channel_id=1, source_target_pairs={{0,1},{1,0},{2,3},{3,2},{4,5},{5,4},{6,7},{7,6},{8,9},{9,8},{10,11... | collective-permute-start | bytes 786440 | tf_op jit(solution)/shard_map/ppermute | solution.py:446
  74.7 10.6 %collective-permute-start.17 = (f32[4,128,128]{2,1,0:T(8,128)S(1)}, f32[4,128,128]{2,1,0:T(8,128)S(1)}, u32[]{:S(2)}, u32[]{:S(2)}) collective-permute-start(f32[4,128,128]{2,1,0:T(8,128)S(1)} %get-tuple-element.112), channel_id=1, source_target_pairs={{4,0},{5,1},{6,2},{7,3},{20,16},{21,17},{22,18},{23,19}} | collective-permute-start | bytes 786440 | tf_op jit(solution)/shard_map/ppermute | solution.py:431
  85.3 1.6 %collective-permute-start.20 = (f32[4,128,128]{2,1,0:T(8,128)S(1)}, f32[4,128,128]{2,1,0:T(8,128)S(1)}, u32[]{:S(2)}, u32[]{:S(2)}) collective-permute-start(f32[4,128,128]{2,1,0:T(8,128)S(1)} %get-tuple-element.126), channel_id=1, source_target_pairs={{0,1},{1,0},{2,3},{3,2},{4,5},{5,4},{6,7},{7,6},{8,9},{9,8},{10,11... | collective-permute-start | bytes 786440 | tf_op jit(solution)/shard_map/ppermute | solution.py:446

commit v7 on v6

--- a/solution.py
+++ b/solution.py
@@ -471,6 +471,24 @@
 
     normed = None
     incoming, middles, backs = [], [], []
+    query_gradient = None
+    dattends = []
+
+    def query_of(group, token):
+        return call(
+            query_kernel, group,
+            ["rows", "rows", "headed", "run", "table", "bias", "bias", "states", "mine", "other"],
+            ["rows", "headed"],
+            (rows_shape, headed(BF16)),
+            (
+                key_in, value_in, middles[group][0], run, table, weight_bias, enter_bias, insides[group][0],
+                *incoming[group],
+            ),
+            "query", 3, 8,
+            aliases=(query_gradient,),
+            tokens=[token],
+        )
+
     for group in range(groups):
         incoming.append(carries[group].finish(token))
         prefix, inside, qd = insides[group][:3]
@@ -487,26 +505,12 @@
         token = mine
         middles.append((grad, suffix))
         backs.append(Carry(group, mine, other, True))
+        if group < groups - 1:
+            query_gradient, dattend = query_of(group, token)
+            dattends.append(dattend)
+            token = dattend
         if group == 0:
             backs[0].hop(0)
-
-    query_gradient = None
-    dattends = []
-
-    def query_of(group, token):
-        return call(
-            query_kernel, group,
-            ["rows", "rows", "headed", "run", "table", "bias", "bias", "states", "mine", "other"],
-            ["rows", "headed"],
-            (rows_shape, headed(BF16)),
-            (
-                key_in, value_in, middles[group][0], run, table, weight_bias, enter_bias, insides[group][0],
-                *incoming[group],
-            ),
-            "query", 3, 8,
-            aliases=(query_gradient,),
-            tokens=[token],
-        )
 
     for index in hops:
         for place, back in enumerate(backs):

time: 90.4 us -> 89.6 us (level)
    ppermute x4, waiting for transfers between devices: 2.49 us -> 1.13 us  [__init__(): self.mine, self.got = (mine, lax.ppermute(other, 'ctx', swap))]
where the time goes in v7:
time: 89.6 us; the launch traced here: 89.2 us
  waiting for transfers between devices  38.5 us (43%)
  Pallas kernels  32.4 us (36%)
  starting transfers between devices  16.4 us (18%)
  between operations  0.95 us (1%)
  other arithmetic  0.93 us (1%)
    ppermute x12, waiting for transfers between devices, hop(): self.landed.append(lax.ppermute(self.sent, 'seq', [self.hops[index]]))  34.1 us
    pallas_call x9, Pallas kernels, call_heads(): pl.pallas_call(functools.partial(with_rows, kernel, dims, group, which, l...  32.4 us
    ppermute x12, starting transfers between devices, hop(): self.landed.append(lax.ppermute(self.sent, 'seq', [self.hops[index]]))  14.1 us
    ppermute x4, waiting for transfers between devices, finish(): return (keep, lax.ppermute(send, 'ctx', swap))  3.01 us
  transfers between devices with their start and end apart: 21, of which 11 were waited for; matrix products, arithmetic and copies ran while one was open for 1% of the time, Pallas kernels for 27%

profile of v7, /device:TPU:0, one launch (start us, length us, event | category | flops | bytes accessed | tf_op | source)
XLA Modules:
  0.0 89.2 jit_solution(3420189878326075961)
XLA Ops:
  0.6 5.1 %begin.1 = (f32[4,128,128]{2,1,0:T(8,128)S(1)}, f32[4,128,128]{2,1,0:T(8,128)S(1)}, f32[4,128,128]{2,1,0:T(8,128)S(1)}, f32[4,128,128]{2,1,0:T(8,128)S(1)}, f32[...) custom-call(s32[1]{0:T(128)} %bitcast.core_ref, ...), custom_call_target="tpu_custom_call" | custom-call | flops 134217728 | bytes 4194304 | tf_op jit(solution)/shard_map/begin/pallas_call | solution.py:335
  5.7 0.5 collective-permute-start
  6.2 0.1 collective-permute-start.2
  6.3 0.4 collective-permute-start.1
  6.7 0.3 collective-permute-done
  7.1 0.7 collective-permute-done.2
  7.8 4.6 %collective-permute-start.4 = (f32[4,128,128]{2,1,0:T(8,128)S(1)}, f32[4,128,128]{2,1,0:T(8,128)S(1)}, u32[]{:S(2)}, u32[]{:S(2)}) collective-permute-start(f32[4,128,128]{2,1,0:T(8,128)S(1)} %select_add_fusion.3), channel_id=1, source_target_pairs={{0,4},{1,5},{2,6},{3,7},{16,20},{17,21},{18,22},{19,23}} | collective-permute-start | bytes 786440 | tf_op jit(solution)/shard_map/ppermute | solution.py:431
  12.5 0.0 collective-permute-done.1
  12.5 1.3 %collective-permute-start.3 = (f32[4,128,128]{2,1,0:T(8,128)S(1)}, f32[4,128,128]{2,1,0:T(8,128)S(1)}, u32[]{:S(2)}, u32[]{:S(2)}) collective-permute-start(f32[4,128,128]{2,1,0:T(8,128)S(1)} %select_add_fusion.2), channel_id=1, source_target_pairs={{0,4},{1,5},{2,6},{3,7},{16,20},{17,21},{18,22},{19,23}} | collective-permute-start | bytes 786440 | tf_op jit(solution)/shard_map/ppermute | solution.py:431
  13.8 5.2 %collective-permute-done.4 = f32[4,128,128]{2,1,0:T(8,128)S(1)} collective-permute-done((f32[4,128,128]{2,1,0:T(8,128)S(1)}, f32[4,128,128]{2,1,0:T(8,128)S(1)}, u32[]{:S(2)}, u32[]{:S(2)}) %collective-permute-start.4) | collective-permute-done | bytes 262176 | tf_op jit(solution)/shard_map/ppermute | solution.py:431
  19.1 0.7 collective-permute-start.6
  19.8 4.3 %collective-permute-done.3 = f32[4,128,128]{2,1,0:T(8,128)S(1)} collective-permute-done((f32[4,128,128]{2,1,0:T(8,128)S(1)}, f32[4,128,128]{2,1,0:T(8,128)S(1)}, u32[]{:S(2)}, u32[]{:S(2)}) %collective-permute-start.3) | collective-permute-done | bytes 262176 | tf_op jit(solution)/shard_map/ppermute | solution.py:431
  24.2 0.7 collective-permute-start.5
  24.9 3.9 %inside.2 = (f32[8,3,128,128]{3,2,1,0:T(8,128)S(1)}, f32[8,512,128]{2,1,0:T(8,128)S(1)}, bf16[8,512,128]{2,1,0:T(8,128)(2,1)S(1)}, bf16[8,512,128]{2,1,0:T(8,128...) custom-call(s32[1]{0:T(128)} %bitcast.core_ref, bf16[512,2048]{1,0:T(8,128)(2,1)} %refs_0_.13, ...), custom_call_target="tpu_custom_call" | custom-call | flops 536870912 | bytes 10485760 | tf_op jit(solution)/shard_map/inside/pallas_call | solution.py:335
  28.8 3.9 %inside.3 = (f32[8,3,128,128]{3,2,1,0:T(8,128)S(1)}, f32[8,512,128]{2,1,0:T(8,128)S(1)}, bf16[8,512,128]{2,1,0:T(8,128)(2,1)S(1)}, bf16[8,512,128]{2,1,0:T(8,128...) custom-call(s32[1]{0:T(128)} %bitcast.core_ref, bf16[512,2048]{1,0:T(8,128)(2,1)} %refs_0_.13, ...), custom_call_target="tpu_custom_call" | custom-call | flops 536870912 | bytes 10485760 | tf_op jit(solution)/shard_map/inside/pallas_call | solution.py:335
  32.7 0.0 collective-permute-done.6
  32.7 0.0 copy-start.3
  32.7 0.1 multiply_add_fusion.9
  32.8 0.8 collective-permute-start.8
  33.6 0.0 collective-permute-done.5
  33.6 0.1 multiply_add_fusion.8
  33.7 0.0 collective-permute-done.8
  33.7 0.1 fusion.6
  33.8 0.1 collective-permute-start.9
  33.9 0.7 collective-permute-start.7
  34.5 0.8 collective-permute-done.9.refs_6_.refs_9_
  35.4 0.0 copy-done.3
  35.4 3.4 %forward.2 = (bf16[512,2048]{1,0:T(8,128)(2,1)}, bf16[8,512,128]{2,1,0:T(8,128)(2,1)S(1)}, f32[8,3,128,128]{3,2,1,0:T(8,128)S(1)}, f32[4,128,128]{2,1,0:T(8,128)S(1)}, f32[4,128,128]{2,1,0:T(8,128)S(1)}) custom-call(s32[1]{0:T(128)} %bitcast.core_ref, f32[8,512,128]{2,1,0:T(8,128)S(1)} %get-tuple-element.77.refs_0_, ...), custom_call_target="tpu_custom_call" | custom-call | flops 268435456 | bytes 8388608 | tf_op jit(solution)/shard_map/forward/pallas_call | solution.py:335
  38.8 0.2 collective-permute-start.11
  38.9 0.0 copy-done
  38.9 0.0 copy-done.1
  38.9 3.3 %query.2 = (bf16[512,2048]{1,0:T(8,128)(2,1)}, bf16[8,512,128]{2,1,0:T(8,128)(2,1)S(1)}) custom-call(s32[1]{0:T(128)} %bitcast.core_ref, bf16[512,2048]{1,0:T(8,128)(2,1)S(1)} %copy-done, bf16[512,2048]{1,0:T(8,128)(2,1)S(1)} %copy-done.1, bf16[8,512,128]{2,1,0:T(8,128)(2,1)S(1)} %get-tuple-element.80.refs_2_.refs_1_, ...), custom_call_target="tpu_custom_call" | custom-call | flops 402653184 | bytes 8388608 | tf_op jit(solution)/shard_map/query/pallas_call | solution.py:335
  42.3 0.0 collective-permute-done.7
  42.3 0.1 fusion.4
  42.4 0.4 collective-permute-start.10
  42.8 0.0 collective-permute-done.11
  42.9 0.7 collective-permute-start.13
  43.5 0.4 collective-permute-done.10.refs_6_.refs_9_
  44.0 3.3 %forward.3 = (bf16[512,2048]{1,0:T(8,128)(2,1)}, bf16[8,512,128]{2,1,0:T(8,128)(2,1)S(1)}, f32[8,3,128,128]{3,2,1,0:T(8,128)S(1)}, f32[4,128,128]{2,1,0:T(8,128)S(1)}, f32[4,128,128]{2,1,0:T(8,128)S(1)}) custom-call(s32[1]{0:T(128)} %bitcast.core_ref, f32[8,512,128]{2,1,0:T(8,128)S(1)} %get-tuple-element.72.refs_0_, ...), custom_call_target="tpu_custom_call", output_to_operand_aliasing={{0}: (8, {})} | custom-call | flops 268435456 | bytes 8388608 | tf_op jit(solution)/shard_map/forward/pallas_call | solution.py:335
  47.3 0.4 collective-permute-start.12
  47.7 0.0 collective-permute-done.13
  47.8 0.7 collective-permute-start.15
  48.4 0.4 collective-permute-done.12
  48.9 0.7 collective-permute-start.14
  49.6 0.0 collective-permute-done.15
  49.6 0.1 multiply_add_fusion.4
  49.7 0.0 collective-permute-done.14
  49.7 0.7 collective-permute-start.16
  50.4 1.3 %collective-permute-start.18 = (f32[4,128,128]{2,1,0:T(8,128)S(1)}, f32[4,128,128]{2,1,0:T(8,128)S(1)}, u32[]{:S(2)}, u32[]{:S(2)}) collective-permute-start(f32[4,128,128]{2,1,0:T(8,128)S(1)} %get-tuple-element.114), channel_id=1, source_target_pairs={{4,0},{5,1},{6,2},{7,3},{20,16},{21,17},{22,18},{23,19}} | collective-permute-start | bytes 786440 | tf_op jit(solution)/shard_map/ppermute | solution.py:431
  51.7 3.4 %query.3 = (bf16[512,2048]{1,0:T(8,128)(2,1)}, bf16[8,512,128]{2,1,0:T(8,128)(2,1)S(1)}) custom-call(s32[1]{0:T(128)} %bitcast.core_ref, bf16[512,2048]{1,0:T(8,128)(2,1)S(1)} %copy-done, bf16[512,2048]{1,0:T(8,128)(2,1)S(1)} %copy-done.1, bf16[8,512,128]{2,1,0:T(8,128)(2,1)S(1)} %get-tuple-element.87.refs_2_.refs_1_, ...), custom_call_target="tpu_custom_call", output_to_operand_aliasing={{0}: (11, {})} | custom-call | flops 402653184 | bytes 8388608 | tf_op jit(solution)/shard_map/query/pallas_call | solution.py:335
  55.1 0.0 copy-start.2
  55.1 0.0 collective-permute-done.16
  55.2 0.1 multiply_add_fusion.2
  55.2 18.5 %collective-permute-done.18 = f32[4,128,128]{2,1,0:T(8,128)S(1)} collective-permute-done((f32[4,128,128]{2,1,0:T(8,128)S(1)}, f32[4,128,128]{2,1,0:T(8,128)S(1)}, u32[]{:S(2)}, u32[]{:S(2)}) %collective-permute-start.18) | collective-permute-done | bytes 262176 | tf_op jit(solution)/shard_map/ppermute | solution.py:431
  73.7 0.1 fusion.2
  73.8 0.1 collective-permute-start.19
  73.9 1.3 %collective-permute-start.17 = (f32[4,128,128]{2,1,0:T(8,128)S(1)}, f32[4,128,128]{2,1,0:T(8,128)S(1)}, u32[]{:S(2)}, u32[]{:S(2)}) collective-permute-start(f32[4,128,128]{2,1,0:T(8,128)S(1)} %get-tuple-element.112), channel_id=1, source_target_pairs={{4,0},{5,1},{6,2},{7,3},{20,16},{21,17},{22,18},{23,19}} | collective-permute-start | bytes 786440 | tf_op jit(solution)/shard_map/ppermute | solution.py:431
  75.2 0.2 collective-permute-done.19.refs_9_
  75.4 3.1 %backward.2 = (bf16[512,2048]{1,0:T(8,128)(2,1)}, bf16[512,2048]{1,0:T(8,128)(2,1)}) custom-call(s32[1]{0:T(128)} %bitcast.core_ref, bf16[512,2048]{1,0:T(8,128)(2,1)S(1)} %copy-done.2, bf16[8,512,128]{2,1,0:T(8,128)(2,1)S(1)} %get-tuple-element.80.refs_2_.refs_1_, bf16[8,512,128]{2,1,0:T(8,128)(2,1)S(1)} %get-tuple-element.102.refs_2_, ...), custom_call_target="tpu_custom_call" | custom-call | flops 536870912 | bytes 10485760 | tf_op jit(solution)/shard_map/backward/pallas_call | solution.py:335
  78.5 6.0 %collective-permute-done.17 = f32[4,128,128]{2,1,0:T(8,128)S(1)} collective-permute-done((f32[4,128,128]{2,1,0:T(8,128)S(1)}, f32[4,128,128]{2,1,0:T(8,128)S(1)}, u32[]{:S(2)}, u32[]{:S(2)}) %collective-permute-start.17) | collective-permute-done | bytes 262176 | tf_op jit(solution)/shard_map/ppermute | solution.py:431
  84.5 0.1 fusion
  84.5 0.1 collective-permute-start.20
  84.6 1.5 %collective-permute-done.20.refs_9_ = f32[4,128,128]{2,1,0:T(8,128)S(1)} collective-permute-done((f32[4,128,128]{2,1,0:T(8,128)S(1)}, f32[4,128,128]{2,1,0:T(8,128)S(1)}, u32[]{:S(2)}, u32[]{:S(2)}) %collective-permute-start.20) | collective-permute-done | bytes 262176 | tf_op jit(solution)/shard_map/ppermute | solution.py:446
  86.1 3.1 %backward.3 = (bf16[512,2048]{1,0:T(8,128)(2,1)}, bf16[512,2048]{1,0:T(8,128)(2,1)}) custom-call(s32[1]{0:T(128)} %bitcast.core_ref, bf16[512,2048]{1,0:T(8,128)(2,1)S(1)} %copy-done.2, bf16[8,512,128]{2,1,0:T(8,128)(2,1)S(1)} %get-tuple-element.87.refs_2_.refs_1_, ...), custom_call_target="tpu_custom_call", output_to_operand_aliasing={{0}: (11, {}), {1}: (12, {})} | custom-call | flops 536870912 | bytes 10485760 | tf_op jit(solution)/shard_map/backward/pallas_call | solution.py:335
  (13 shorter events, 0.3 us)
Async XLA Ops:
  5.7 1.3 %collective-permute-start = (f32[16,128]{1,0:T(8,128)S(1)}, f32[16,128]{1,0:T(8,128)S(1)}, u32[]{:S(2)}, u32[]{:S(2)}) collective-permute-start(f32[16,128]{1,0:T(8,128)S(1)} %get-tuple-element.63), channel_id=1, source_target_pairs={{0,1},{1,0},{2,3},{3,2},{4,5},{5,4},{6,7},{7,6},{8,9},{9,8},{10,11... | collective-permute-start | bytes 24584 | tf_op jit(solution)/shard_map/ppermute | solution.py:395
  6.2 1.5 %collective-permute-start.2 = (f32[4,128,128]{2,1,0:T(8,128)S(1)}, f32[4,128,128]{2,1,0:T(8,128)S(1)}, u32[]{:S(2)}, u32[]{:S(2)}) collective-permute-start(f32[4,128,128]{2,1,0:T(8,128)S(1)} %get-tuple-element.67), channel_id=1, source_target_pairs={{0,1},{1,0},{2,3},{3,2},{4,5},{5,4},{6,7},{7,6},{8,9},{9,8},{10,11... | collective-permute-start | bytes 786440 | tf_op jit(solution)/shard_map/ppermute | solution.py:408
  6.3 6.2 %collective-permute-start.1 = (f32[4,128,128]{2,1,0:T(8,128)S(1)}, f32[4,128,128]{2,1,0:T(8,128)S(1)}, u32[]{:S(2)}, u32[]{:S(2)}) collective-permute-start(f32[4,128,128]{2,1,0:T(8,128)S(1)} %get-tuple-element.65), channel_id=1, source_target_pairs={{0,1},{1,0},{2,3},{3,2},{4,5},{5,4},{6,7},{7,6},{8,9},{9,8},{10,11... | collective-permute-start | bytes 786440 | tf_op jit(solution)/shard_map/ppermute | solution.py:408
  7.8 11.3 %collective-permute-start.4 = (f32[4,128,128]{2,1,0:T(8,128)S(1)}, f32[4,128,128]{2,1,0:T(8,128)S(1)}, u32[]{:S(2)}, u32[]{:S(2)}) collective-permute-start(f32[4,128,128]{2,1,0:T(8,128)S(1)} %select_add_fusion.3), channel_id=1, source_target_pairs={{0,4},{1,5},{2,6},{3,7},{16,20},{17,21},{18,22},{19,23}} | collective-permute-start | bytes 786440 | tf_op jit(solution)/shard_map/ppermute | solution.py:431
  12.5 11.6 %collective-permute-start.3 = (f32[4,128,128]{2,1,0:T(8,128)S(1)}, f32[4,128,128]{2,1,0:T(8,128)S(1)}, u32[]{:S(2)}, u32[]{:S(2)}) collective-permute-start(f32[4,128,128]{2,1,0:T(8,128)S(1)} %select_add_fusion.2), channel_id=1, source_target_pairs={{0,4},{1,5},{2,6},{3,7},{16,20},{17,21},{18,22},{19,23}} | collective-permute-start | bytes 786440 | tf_op jit(solution)/shard_map/ppermute | solution.py:431
  19.1 13.6 %collective-permute-start.6 = (f32[4,128,128]{2,1,0:T(8,128)S(1)}, f32[4,128,128]{2,1,0:T(8,128)S(1)}, u32[]{:S(2)}, u32[]{:S(2)}) collective-permute-start(f32[4,128,128]{2,1,0:T(8,128)S(1)} %multiply_add_fusion.11), channel_id=1, source_target_pairs={{4,8},{5,9},{6,10},{7,11},{20,24},{21,25},{22,26},{23,27}} | collective-permute-start | bytes 786440 | tf_op jit(solution)/shard_map/ppermute | solution.py:431
  24.2 9.4 %collective-permute-start.5 = (f32[4,128,128]{2,1,0:T(8,128)S(1)}, f32[4,128,128]{2,1,0:T(8,128)S(1)}, u32[]{:S(2)}, u32[]{:S(2)}) collective-permute-start(f32[4,128,128]{2,1,0:T(8,128)S(1)} %multiply_add_fusion.10.refs_8_), channel_id=1, source_target_pairs={{4,8},{5,9},{6,10},{7,11},{20,24},{21,25},{22,26},{23,27}} | collective-permute-start | bytes 786440 | tf_op jit(solution)/shard_map/ppermute | solution.py:431
  32.7 2.7 %copy-start.3 = (bf16[512,2048]{1,0:T(8,128)(2,1)S(1)}, bf16[512,2048]{1,0:T(8,128)(2,1)}, u32[]{:S(2)}) copy-start(bf16[512,2048]{1,0:T(8,128)(2,1)} %refs_2_.9) | copy-start | bytes 6291460
  32.8 0.9 %collective-permute-start.8 = (f32[4,128,128]{2,1,0:T(8,128)S(1)}, f32[4,128,128]{2,1,0:T(8,128)S(1)}, u32[]{:S(2)}, u32[]{:S(2)}) collective-permute-start(f32[4,128,128]{2,1,0:T(8,128)S(1)} %get-tuple-element.118), channel_id=1, source_target_pairs={{8,12},{9,13},{10,14},{11,15},{24,28},{25,29},{26,30},{27,31}} | collective-permute-start | bytes 786440 | tf_op jit(solution)/shard_map/ppermute | solution.py:431
  33.8 1.6 %collective-permute-start.9 = (f32[4,128,128]{2,1,0:T(8,128)S(1)}, f32[4,128,128]{2,1,0:T(8,128)S(1)}, u32[]{:S(2)}, u32[]{:S(2)}) collective-permute-start(f32[4,128,128]{2,1,0:T(8,128)S(1)} %get-tuple-element.132), channel_id=1, source_target_pairs={{0,1},{1,0},{2,3},{3,2},{4,5},{5,4},{6,7},{7,6},{8,9},{9,8},{10,11... | collective-permute-start | bytes 786440 | tf_op jit(solution)/shard_map/ppermute | solution.py:446
  33.9 8.4 %collective-permute-start.7 = (f32[4,128,128]{2,1,0:T(8,128)S(1)}, f32[4,128,128]{2,1,0:T(8,128)S(1)}, u32[]{:S(2)}, u32[]{:S(2)}) collective-permute-start(f32[4,128,128]{2,1,0:T(8,128)S(1)} %get-tuple-element.116), channel_id=1, source_target_pairs={{8,12},{9,13},{10,14},{11,15},{24,28},{25,29},{26,30},{27,31}} | collective-permute-start | bytes 786440 | tf_op jit(solution)/shard_map/ppermute | solution.py:431
  35.4 3.5 %copy-start = (bf16[512,2048]{1,0:T(8,128)(2,1)S(1)}, bf16[512,2048]{1,0:T(8,128)(2,1)}, u32[]{:S(2)}) copy-start(bf16[512,2048]{1,0:T(8,128)(2,1)} %refs_0_.11) | copy-start | bytes 6291460
  35.4 3.5 %copy-start.1 = (bf16[512,2048]{1,0:T(8,128)(2,1)S(1)}, bf16[512,2048]{1,0:T(8,128)(2,1)}, u32[]{:S(2)}) copy-start(bf16[512,2048]{1,0:T(8,128)(2,1)} %refs_1_.7) | copy-start | bytes 6291460
  38.8 4.1 %collective-permute-start.11 = (f32[4,128,128]{2,1,0:T(8,128)S(1)}, f32[4,128,128]{2,1,0:T(8,128)S(1)}, u32[]{:S(2)}, u32[]{:S(2)}) collective-permute-start(f32[4,128,128]{2,1,0:T(8,128)S(1)} %get-tuple-element.85), channel_id=1, source_target_pairs={{0,1},{1,0},{2,3},{3,2},{4,5},{5,4},{6,7},{7,6},{8,9},{9,8},{10,11... | collective-permute-start | bytes 786440 | tf_op jit(solution)/shard_map/ppermute | solution.py:408
  42.4 1.6 %collective-permute-start.10 = (f32[4,128,128]{2,1,0:T(8,128)S(1)}, f32[4,128,128]{2,1,0:T(8,128)S(1)}, u32[]{:S(2)}, u32[]{:S(2)}) collective-permute-start(f32[4,128,128]{2,1,0:T(8,128)S(1)} %get-tuple-element.130), channel_id=1, source_target_pairs={{0,1},{1,0},{2,3},{3,2},{4,5},{5,4},{6,7},{7,6},{8,9},{9,8},{10,11... | collective-permute-start | bytes 786440 | tf_op jit(solution)/shard_map/ppermute | solution.py:446
  42.9 4.8 %collective-permute-start.13 = (f32[4,128,128]{2,1,0:T(8,128)S(1)}, f32[4,128,128]{2,1,0:T(8,128)S(1)}, u32[]{:S(2)}, u32[]{:S(2)}) collective-permute-start(f32[4,128,128]{2,1,0:T(8,128)S(1)} %select_add_fusion.1.refs_8_), channel_id=1, source_target_pairs={{12,8},{13,9},{14,10},{15,11},{28,24},{29,25},{30,26},{31,27}} | collective-permute-start | bytes 786440 | tf_op jit(solution)/shard_map/ppermute | solution.py:431
  47.3 1.6 %collective-permute-start.12 = (f32[4,128,128]{2,1,0:T(8,128)S(1)}, f32[4,128,128]{2,1,0:T(8,128)S(1)}, u32[]{:S(2)}, u32[]{:S(2)}) collective-permute-start(f32[4,128,128]{2,1,0:T(8,128)S(1)} %get-tuple-element.89), channel_id=1, source_target_pairs={{0,1},{1,0},{2,3},{3,2},{4,5},{5,4},{6,7},{7,6},{8,9},{9,8},{10,11... | collective-permute-start | bytes 786440 | tf_op jit(solution)/shard_map/ppermute | solution.py:408
  47.8 1.8 %collective-permute-start.15 = (f32[4,128,128]{2,1,0:T(8,128)S(1)}, f32[4,128,128]{2,1,0:T(8,128)S(1)}, u32[]{:S(2)}, u32[]{:S(2)}) collective-permute-start(f32[4,128,128]{2,1,0:T(8,128)S(1)} %multiply_add_fusion.5), channel_id=1, source_target_pairs={{8,4},{9,5},{10,6},{11,7},{24,20},{25,21},{26,22},{27,23}} | collective-permute-start | bytes 786440 | tf_op jit(solution)/shard_map/ppermute | solution.py:431
  48.9 0.8 collective-permute-start.14
  49.7 5.4 %collective-permute-start.16 = (f32[4,128,128]{2,1,0:T(8,128)S(1)}, f32[4,128,128]{2,1,0:T(8,128)S(1)}, u32[]{:S(2)}, u32[]{:S(2)}) collective-permute-start(f32[4,128,128]{2,1,0:T(8,128)S(1)} %multiply_add_fusion.3.refs_11_), channel_id=1, source_target_pairs={{8,4},{9,5},{10,6},{11,7},{24,20},{25,21},{26,22},{27,23}} | collective-permute-start | bytes 786440 | tf_op jit(solution)/shard_map/ppermute | solution.py:431
  50.4 23.3 %collective-permute-start.18 = (f32[4,128,128]{2,1,0:T(8,128)S(1)}, f32[4,128,128]{2,1,0:T(8,128)S(1)}, u32[]{:S(2)}, u32[]{:S(2)}) collective-permute-start(f32[4,128,128]{2,1,0:T(8,128)S(1)} %get-tuple-element.114), channel_id=1, source_target_pairs={{4,0},{5,1},{6,2},{7,3},{20,16},{21,17},{22,18},{23,19}} | collective-permute-start | bytes 786440 | tf_op jit(solution)/shard_map/ppermute | solution.py:431
  55.1 20.3 %copy-start.2 = (bf16[512,2048]{1,0:T(8,128)(2,1)S(1)}, bf16[512,2048]{1,0:T(8,128)(2,1)}, u32[]{:S(2)}) copy-start(bf16[512,2048]{1,0:T(8,128)(2,1)} %refs_0_.13) | copy-start | bytes 6291460
  73.8 1.6 %collective-permute-start.19 = (f32[4,128,128]{2,1,0:T(8,128)S(1)}, f32[4,128,128]{2,1,0:T(8,128)S(1)}, u32[]{:S(2)}, u32[]{:S(2)}) collective-permute-start(f32[4,128,128]{2,1,0:T(8,128)S(1)} %get-tuple-element.128), channel_id=1, source_target_pairs={{0,1},{1,0},{2,3},{3,2},{4,5},{5,4},{6,7},{7,6},{8,9},{9,8},{10,11... | collective-permute-start | bytes 786440 | tf_op jit(solution)/shard_map/ppermute | solution.py:446
  73.9 10.6 %collective-permute-start.17 = (f32[4,128,128]{2,1,0:T(8,128)S(1)}, f32[4,128,128]{2,1,0:T(8,128)S(1)}, u32[]{:S(2)}, u32[]{:S(2)}) collective-permute-start(f32[4,128,128]{2,1,0:T(8,128)S(1)} %get-tuple-element.112), channel_id=1, source_target_pairs={{4,0},{5,1},{6,2},{7,3},{20,16},{21,17},{22,18},{23,19}} | collective-permute-start | bytes 786440 | tf_op jit(solution)/shard_map/ppermute | solution.py:431
  84.5 1.6 %collective-permute-start.20 = (f32[4,128,128]{2,1,0:T(8,128)S(1)}, f32[4,128,128]{2,1,0:T(8,128)S(1)}, u32[]{:S(2)}, u32[]{:S(2)}) collective-permute-start(f32[4,128,128]{2,1,0:T(8,128)S(1)} %get-tuple-element.126), channel_id=1, source_target_pairs={{0,1},{1,0},{2,3},{3,2},{4,5},{5,4},{6,7},{7,6},{8,9},{9,8},{10,11... | collective-permute-start | bytes 786440 | tf_op jit(solution)/shard_map/ppermute | solution.py:446

commit v8 on v7

--- a/solution.py
+++ b/solution.py
@@ -48,16 +48,16 @@
     gain = jnp.ones((heads, C), F32)
     each = range(chunks)
     spans = [pl.ds(j * C, C) for j in each]
-    runs = [exact_dot(decay_ref[:, span], sums) for span in spans]
+    runs = [exact_dot(decay_ref[:, span], upper) for span in spans]
     starts = jnp.concatenate([start_ref[:, span].astype(F32) for span in spans] * (8 // chunks), axis=0)
     docs_all = dot(starts.astype(BF16), sums.astype(BF16))
     for j in each:
         span = spans[j]
-        last = runs[j][:, C:]
+        last = jnp.broadcast_to(runs[j][:, C - 1 :], (heads, C))
         docs, docs_last = docs_all[j : j + 1, :C], docs_all[j : j + 1, C:]
         passing = jnp.where(docs_last == 0.0, jnp.exp(last), 0.0)
         gain = gain * passing
-        run_ref[:, 0, span] = runs[j][:, :C]
+        run_ref[:, 0, span] = runs[j]
         table_ref[:, j, :] = passing
         table_ref[:, chunks + j, :] = last
         docs_column = columns(docs)

time: 89.6 us -> 89.6 us (level)
  no operation moved by 1% of the time
where the time goes in v8:
time: 89.6 us; the launch traced here: 89.2 us
  waiting for transfers between devices  38.5 us (43%)
  Pallas kernels  32.4 us (36%)
  starting transfers between devices  16.4 us (18%)
  between operations  0.95 us (1%)
  other arithmetic  0.93 us (1%)
    ppermute x12, waiting for transfers between devices, hop(): self.landed.append(lax.ppermute(self.sent, 'seq', [self.hops[index]]))  34.1 us
    pallas_call x9, Pallas kernels, call_heads(): pl.pallas_call(functools.partial(with_rows, kernel, dims, group, which, l...  32.4 us
    ppermute x12, starting transfers between devices, hop(): self.landed.append(lax.ppermute(self.sent, 'seq', [self.hops[index]]))  14.1 us
    ppermute x4, waiting for transfers between devices, finish(): return (keep, lax.ppermute(send, 'ctx', swap))  3.01 us
  transfers between devices with their start and end apart: 21, of which 11 were waited for; matrix products, arithmetic and copies ran while one was open for 1% of the time, Pallas kernels for 27%

profile of v8, /device:TPU:0, one launch (start us, length us, event | category | flops | bytes accessed | tf_op | source)
XLA Modules:
  0.0 89.2 jit_solution(6869425041387248607)
XLA Ops:
  0.6 5.1 %begin.1 = (f32[4,128,128]{2,1,0:T(8,128)S(1)}, f32[4,128,128]{2,1,0:T(8,128)S(1)}, f32[4,128,128]{2,1,0:T(8,128)S(1)}, f32[4,128,128]{2,1,0:T(8,128)S(1)}, f32[...) custom-call(s32[1]{0:T(128)} %bitcast.core_ref, ...), custom_call_target="tpu_custom_call" | custom-call | flops 134217728 | bytes 4194304 | tf_op jit(solution)/shard_map/begin/pallas_call | solution.py:335
  5.7 0.5 collective-permute-start
  6.2 0.1 collective-permute-start.2
  6.3 0.4 collective-permute-start.1
  6.7 0.3 collective-permute-done
  7.1 0.7 collective-permute-done.2
  7.8 4.6 %collective-permute-start.4 = (f32[4,128,128]{2,1,0:T(8,128)S(1)}, f32[4,128,128]{2,1,0:T(8,128)S(1)}, u32[]{:S(2)}, u32[]{:S(2)}) collective-permute-start(f32[4,128,128]{2,1,0:T(8,128)S(1)} %select_add_fusion.3), channel_id=1, source_target_pairs={{0,4},{1,5},{2,6},{3,7},{16,20},{17,21},{18,22},{19,23}} | collective-permute-start | bytes 786440 | tf_op jit(solution)/shard_map/ppermute | solution.py:431
  12.5 0.0 collective-permute-done.1
  12.5 1.3 %collective-permute-start.3 = (f32[4,128,128]{2,1,0:T(8,128)S(1)}, f32[4,128,128]{2,1,0:T(8,128)S(1)}, u32[]{:S(2)}, u32[]{:S(2)}) collective-permute-start(f32[4,128,128]{2,1,0:T(8,128)S(1)} %select_add_fusion.2), channel_id=1, source_target_pairs={{0,4},{1,5},{2,6},{3,7},{16,20},{17,21},{18,22},{19,23}} | collective-permute-start | bytes 786440 | tf_op jit(solution)/shard_map/ppermute | solution.py:431
  13.8 5.2 %collective-permute-done.4 = f32[4,128,128]{2,1,0:T(8,128)S(1)} collective-permute-done((f32[4,128,128]{2,1,0:T(8,128)S(1)}, f32[4,128,128]{2,1,0:T(8,128)S(1)}, u32[]{:S(2)}, u32[]{:S(2)}) %collective-permute-start.4) | collective-permute-done | bytes 262176 | tf_op jit(solution)/shard_map/ppermute | solution.py:431
  19.1 0.7 collective-permute-start.6
  19.8 4.3 %collective-permute-done.3 = f32[4,128,128]{2,1,0:T(8,128)S(1)} collective-permute-done((f32[4,128,128]{2,1,0:T(8,128)S(1)}, f32[4,128,128]{2,1,0:T(8,128)S(1)}, u32[]{:S(2)}, u32[]{:S(2)}) %collective-permute-start.3) | collective-permute-done | bytes 262176 | tf_op jit(solution)/shard_map/ppermute | solution.py:431
  24.2 0.7 collective-permute-start.5
  24.9 3.9 %inside.2 = (f32[8,3,128,128]{3,2,1,0:T(8,128)S(1)}, f32[8,512,128]{2,1,0:T(8,128)S(1)}, bf16[8,512,128]{2,1,0:T(8,128)(2,1)S(1)}, bf16[8,512,128]{2,1,0:T(8,128...) custom-call(s32[1]{0:T(128)} %bitcast.core_ref, bf16[512,2048]{1,0:T(8,128)(2,1)} %refs_0_.13, ...), custom_call_target="tpu_custom_call" | custom-call | flops 536870912 | bytes 10485760 | tf_op jit(solution)/shard_map/inside/pallas_call | solution.py:335
  28.8 3.9 %inside.3 = (f32[8,3,128,128]{3,2,1,0:T(8,128)S(1)}, f32[8,512,128]{2,1,0:T(8,128)S(1)}, bf16[8,512,128]{2,1,0:T(8,128)(2,1)S(1)}, bf16[8,512,128]{2,1,0:T(8,128...) custom-call(s32[1]{0:T(128)} %bitcast.core_ref, bf16[512,2048]{1,0:T(8,128)(2,1)} %refs_0_.13, ...), custom_call_target="tpu_custom_call" | custom-call | flops 536870912 | bytes 10485760 | tf_op jit(solution)/shard_map/inside/pallas_call | solution.py:335
  32.7 0.0 collective-permute-done.6
  32.7 0.0 copy-start.3
  32.7 0.1 multiply_add_fusion.9
  32.8 0.8 collective-permute-start.8
  33.6 0.0 collective-permute-done.5
  33.6 0.1 multiply_add_fusion.8
  33.7 0.0 collective-permute-done.8
  33.7 0.1 fusion.6
  33.8 0.1 collective-permute-start.9
  33.9 0.7 collective-permute-start.7
  34.5 0.8 collective-permute-done.9.refs_6_.refs_9_
  35.4 0.0 copy-done.3
  35.4 3.4 %forward.2 = (bf16[512,2048]{1,0:T(8,128)(2,1)}, bf16[8,512,128]{2,1,0:T(8,128)(2,1)S(1)}, f32[8,3,128,128]{3,2,1,0:T(8,128)S(1)}, f32[4,128,128]{2,1,0:T(8,128)S(1)}, f32[4,128,128]{2,1,0:T(8,128)S(1)}) custom-call(s32[1]{0:T(128)} %bitcast.core_ref, f32[8,512,128]{2,1,0:T(8,128)S(1)} %get-tuple-element.77.refs_0_, ...), custom_call_target="tpu_custom_call" | custom-call | flops 268435456 | bytes 8388608 | tf_op jit(solution)/shard_map/forward/pallas_call | solution.py:335
  38.8 0.2 collective-permute-start.11
  38.9 0.0 copy-done
  38.9 0.0 copy-done.1
  38.9 3.3 %query.2 = (bf16[512,2048]{1,0:T(8,128)(2,1)}, bf16[8,512,128]{2,1,0:T(8,128)(2,1)S(1)}) custom-call(s32[1]{0:T(128)} %bitcast.core_ref, bf16[512,2048]{1,0:T(8,128)(2,1)S(1)} %copy-done, bf16[512,2048]{1,0:T(8,128)(2,1)S(1)} %copy-done.1, bf16[8,512,128]{2,1,0:T(8,128)(2,1)S(1)} %get-tuple-element.80.refs_2_.refs_1_, ...), custom_call_target="tpu_custom_call" | custom-call | flops 402653184 | bytes 8388608 | tf_op jit(solution)/shard_map/query/pallas_call | solution.py:335
  42.3 0.0 collective-permute-done.7
  42.3 0.1 fusion.4
  42.4 0.4 collective-permute-start.10
  42.8 0.0 collective-permute-done.11
  42.9 0.7 collective-permute-start.13
  43.5 0.4 collective-permute-done.10.refs_6_.refs_9_
  44.0 3.3 %forward.3 = (bf16[512,2048]{1,0:T(8,128)(2,1)}, bf16[8,512,128]{2,1,0:T(8,128)(2,1)S(1)}, f32[8,3,128,128]{3,2,1,0:T(8,128)S(1)}, f32[4,128,128]{2,1,0:T(8,128)S(1)}, f32[4,128,128]{2,1,0:T(8,128)S(1)}) custom-call(s32[1]{0:T(128)} %bitcast.core_ref, f32[8,512,128]{2,1,0:T(8,128)S(1)} %get-tuple-element.72.refs_0_, ...), custom_call_target="tpu_custom_call", output_to_operand_aliasing={{0}: (8, {})} | custom-call | flops 268435456 | bytes 8388608 | tf_op jit(solution)/shard_map/forward/pallas_call | solution.py:335
  47.3 0.4 collective-permute-start.12
  47.7 0.0 collective-permute-done.13
  47.8 0.7 collective-permute-start.15
  48.4 0.4 collective-permute-done.12
  48.9 0.7 collective-permute-start.14
  49.6 0.0 collective-permute-done.15
  49.6 0.1 multiply_add_fusion.4
  49.7 0.0 collective-permute-done.14
  49.7 0.7 collective-permute-start.16
  50.4 1.3 %collective-permute-start.18 = (f32[4,128,128]{2,1,0:T(8,128)S(1)}, f32[4,128,128]{2,1,0:T(8,128)S(1)}, u32[]{:S(2)}, u32[]{:S(2)}) collective-permute-start(f32[4,128,128]{2,1,0:T(8,128)S(1)} %get-tuple-element.114), channel_id=1, source_target_pairs={{4,0},{5,1},{6,2},{7,3},{20,16},{21,17},{22,18},{23,19}} | collective-permute-start | bytes 786440 | tf_op jit(solution)/shard_map/ppermute | solution.py:431
  51.7 3.4 %query.3 = (bf16[512,2048]{1,0:T(8,128)(2,1)}, bf16[8,512,128]{2,1,0:T(8,128)(2,1)S(1)}) custom-call(s32[1]{0:T(128)} %bitcast.core_ref, bf16[512,2048]{1,0:T(8,128)(2,1)S(1)} %copy-done, bf16[512,2048]{1,0:T(8,128)(2,1)S(1)} %copy-done.1, bf16[8,512,128]{2,1,0:T(8,128)(2,1)S(1)} %get-tuple-element.87.refs_2_.refs_1_, ...), custom_call_target="tpu_custom_call", output_to_operand_aliasing={{0}: (11, {})} | custom-call | flops 402653184 | bytes 8388608 | tf_op jit(solution)/shard_map/query/pallas_call | solution.py:335
  55.1 0.0 copy-start.2
  55.1 0.0 collective-permute-done.16
  55.2 0.1 multiply_add_fusion.2
  55.2 18.5 %collective-permute-done.18 = f32[4,128,128]{2,1,0:T(8,128)S(1)} collective-permute-done((f32[4,128,128]{2,1,0:T(8,128)S(1)}, f32[4,128,128]{2,1,0:T(8,128)S(1)}, u32[]{:S(2)}, u32[]{:S(2)}) %collective-permute-start.18) | collective-permute-done | bytes 262176 | tf_op jit(solution)/shard_map/ppermute | solution.py:431
  73.7 0.1 fusion.2
  73.8 0.1 collective-permute-start.19
  73.9 1.3 %collective-permute-start.17 = (f32[4,128,128]{2,1,0:T(8,128)S(1)}, f32[4,128,128]{2,1,0:T(8,128)S(1)}, u32[]{:S(2)}, u32[]{:S(2)}) collective-permute-start(f32[4,128,128]{2,1,0:T(8,128)S(1)} %get-tuple-element.112), channel_id=1, source_target_pairs={{4,0},{5,1},{6,2},{7,3},{20,16},{21,17},{22,18},{23,19}} | collective-permute-start | bytes 786440 | tf_op jit(solution)/shard_map/ppermute | solution.py:431
  75.2 0.2 collective-permute-done.19.refs_9_
  75.4 3.1 %backward.2 = (bf16[512,2048]{1,0:T(8,128)(2,1)}, bf16[512,2048]{1,0:T(8,128)(2,1)}) custom-call(s32[1]{0:T(128)} %bitcast.core_ref, bf16[512,2048]{1,0:T(8,128)(2,1)S(1)} %copy-done.2, bf16[8,512,128]{2,1,0:T(8,128)(2,1)S(1)} %get-tuple-element.80.refs_2_.refs_1_, bf16[8,512,128]{2,1,0:T(8,128)(2,1)S(1)} %get-tuple-element.102.refs_2_, ...), custom_call_target="tpu_custom_call" | custom-call | flops 536870912 | bytes 10485760 | tf_op jit(solution)/shard_map/backward/pallas_call | solution.py:335
  78.5 6.0 %collective-permute-done.17 = f32[4,128,128]{2,1,0:T(8,128)S(1)} collective-permute-done((f32[4,128,128]{2,1,0:T(8,128)S(1)}, f32[4,128,128]{2,1,0:T(8,128)S(1)}, u32[]{:S(2)}, u32[]{:S(2)}) %collective-permute-start.17) | collective-permute-done | bytes 262176 | tf_op jit(solution)/shard_map/ppermute | solution.py:431
  84.5 0.1 fusion
  84.5 0.1 collective-permute-start.20
  84.6 1.5 %collective-permute-done.20.refs_9_ = f32[4,128,128]{2,1,0:T(8,128)S(1)} collective-permute-done((f32[4,128,128]{2,1,0:T(8,128)S(1)}, f32[4,128,128]{2,1,0:T(8,128)S(1)}, u32[]{:S(2)}, u32[]{:S(2)}) %collective-permute-start.20) | collective-permute-done | bytes 262176 | tf_op jit(solution)/shard_map/ppermute | solution.py:446
  86.1 3.1 %backward.3 = (bf16[512,2048]{1,0:T(8,128)(2,1)}, bf16[512,2048]{1,0:T(8,128)(2,1)}) custom-call(s32[1]{0:T(128)} %bitcast.core_ref, bf16[512,2048]{1,0:T(8,128)(2,1)S(1)} %copy-done.2, bf16[8,512,128]{2,1,0:T(8,128)(2,1)S(1)} %get-tuple-element.87.refs_2_.refs_1_, ...), custom_call_target="tpu_custom_call", output_to_operand_aliasing={{0}: (11, {}), {1}: (12, {})} | custom-call | flops 536870912 | bytes 10485760 | tf_op jit(solution)/shard_map/backward/pallas_call | solution.py:335
  (13 shorter events, 0.3 us)
Async XLA Ops:
  5.7 1.3 %collective-permute-start = (f32[16,128]{1,0:T(8,128)S(1)}, f32[16,128]{1,0:T(8,128)S(1)}, u32[]{:S(2)}, u32[]{:S(2)}) collective-permute-start(f32[16,128]{1,0:T(8,128)S(1)} %get-tuple-element.63), channel_id=1, source_target_pairs={{0,1},{1,0},{2,3},{3,2},{4,5},{5,4},{6,7},{7,6},{8,9},{9,8},{10,11... | collective-permute-start | bytes 24584 | tf_op jit(solution)/shard_map/ppermute | solution.py:395
  6.2 1.5 %collective-permute-start.2 = (f32[4,128,128]{2,1,0:T(8,128)S(1)}, f32[4,128,128]{2,1,0:T(8,128)S(1)}, u32[]{:S(2)}, u32[]{:S(2)}) collective-permute-start(f32[4,128,128]{2,1,0:T(8,128)S(1)} %get-tuple-element.67), channel_id=1, source_target_pairs={{0,1},{1,0},{2,3},{3,2},{4,5},{5,4},{6,7},{7,6},{8,9},{9,8},{10,11... | collective-permute-start | bytes 786440 | tf_op jit(solution)/shard_map/ppermute | solution.py:408
  6.3 6.2 %collective-permute-start.1 = (f32[4,128,128]{2,1,0:T(8,128)S(1)}, f32[4,128,128]{2,1,0:T(8,128)S(1)}, u32[]{:S(2)}, u32[]{:S(2)}) collective-permute-start(f32[4,128,128]{2,1,0:T(8,128)S(1)} %get-tuple-element.65), channel_id=1, source_target_pairs={{0,1},{1,0},{2,3},{3,2},{4,5},{5,4},{6,7},{7,6},{8,9},{9,8},{10,11... | collective-permute-start | bytes 786440 | tf_op jit(solution)/shard_map/ppermute | solution.py:408
  7.8 11.3 %collective-permute-start.4 = (f32[4,128,128]{2,1,0:T(8,128)S(1)}, f32[4,128,128]{2,1,0:T(8,128)S(1)}, u32[]{:S(2)}, u32[]{:S(2)}) collective-permute-start(f32[4,128,128]{2,1,0:T(8,128)S(1)} %select_add_fusion.3), channel_id=1, source_target_pairs={{0,4},{1,5},{2,6},{3,7},{16,20},{17,21},{18,22},{19,23}} | collective-permute-start | bytes 786440 | tf_op jit(solution)/shard_map/ppermute | solution.py:431
  12.5 11.6 %collective-permute-start.3 = (f32[4,128,128]{2,1,0:T(8,128)S(1)}, f32[4,128,128]{2,1,0:T(8,128)S(1)}, u32[]{:S(2)}, u32[]{:S(2)}) collective-permute-start(f32[4,128,128]{2,1,0:T(8,128)S(1)} %select_add_fusion.2), channel_id=1, source_target_pairs={{0,4},{1,5},{2,6},{3,7},{16,20},{17,21},{18,22},{19,23}} | collective-permute-start | bytes 786440 | tf_op jit(solution)/shard_map/ppermute | solution.py:431
  19.1 13.6 %collective-permute-start.6 = (f32[4,128,128]{2,1,0:T(8,128)S(1)}, f32[4,128,128]{2,1,0:T(8,128)S(1)}, u32[]{:S(2)}, u32[]{:S(2)}) collective-permute-start(f32[4,128,128]{2,1,0:T(8,128)S(1)} %multiply_add_fusion.11), channel_id=1, source_target_pairs={{4,8},{5,9},{6,10},{7,11},{20,24},{21,25},{22,26},{23,27}} | collective-permute-start | bytes 786440 | tf_op jit(solution)/shard_map/ppermute | solution.py:431
  24.2 9.4 %collective-permute-start.5 = (f32[4,128,128]{2,1,0:T(8,128)S(1)}, f32[4,128,128]{2,1,0:T(8,128)S(1)}, u32[]{:S(2)}, u32[]{:S(2)}) collective-permute-start(f32[4,128,128]{2,1,0:T(8,128)S(1)} %multiply_add_fusion.10.refs_8_), channel_id=1, source_target_pairs={{4,8},{5,9},{6,10},{7,11},{20,24},{21,25},{22,26},{23,27}} | collective-permute-start | bytes 786440 | tf_op jit(solution)/shard_map/ppermute | solution.py:431
  32.7 2.7 %copy-start.3 = (bf16[512,2048]{1,0:T(8,128)(2,1)S(1)}, bf16[512,2048]{1,0:T(8,128)(2,1)}, u32[]{:S(2)}) copy-start(bf16[512,2048]{1,0:T(8,128)(2,1)} %refs_2_.9) | copy-start | bytes 6291460
  32.8 0.9 %collective-permute-start.8 = (f32[4,128,128]{2,1,0:T(8,128)S(1)}, f32[4,128,128]{2,1,0:T(8,128)S(1)}, u32[]{:S(2)}, u32[]{:S(2)}) collective-permute-start(f32[4,128,128]{2,1,0:T(8,128)S(1)} %get-tuple-element.118), channel_id=1, source_target_pairs={{8,12},{9,13},{10,14},{11,15},{24,28},{25,29},{26,30},{27,31}} | collective-permute-start | bytes 786440 | tf_op jit(solution)/shard_map/ppermute | solution.py:431
  33.8 1.6 %collective-permute-start.9 = (f32[4,128,128]{2,1,0:T(8,128)S(1)}, f32[4,128,128]{2,1,0:T(8,128)S(1)}, u32[]{:S(2)}, u32[]{:S(2)}) collective-permute-start(f32[4,128,128]{2,1,0:T(8,128)S(1)} %get-tuple-element.132), channel_id=1, source_target_pairs={{0,1},{1,0},{2,3},{3,2},{4,5},{5,4},{6,7},{7,6},{8,9},{9,8},{10,11... | collective-permute-start | bytes 786440 | tf_op jit(solution)/shard_map/ppermute | solution.py:446
  33.9 8.4 %collective-permute-start.7 = (f32[4,128,128]{2,1,0:T(8,128)S(1)}, f32[4,128,128]{2,1,0:T(8,128)S(1)}, u32[]{:S(2)}, u32[]{:S(2)}) collective-permute-start(f32[4,128,128]{2,1,0:T(8,128)S(1)} %get-tuple-element.116), channel_id=1, source_target_pairs={{8,12},{9,13},{10,14},{11,15},{24,28},{25,29},{26,30},{27,31}} | collective-permute-start | bytes 786440 | tf_op jit(solution)/shard_map/ppermute | solution.py:431
  35.4 3.5 %copy-start = (bf16[512,2048]{1,0:T(8,128)(2,1)S(1)}, bf16[512,2048]{1,0:T(8,128)(2,1)}, u32[]{:S(2)}) copy-start(bf16[512,2048]{1,0:T(8,128)(2,1)} %refs_0_.11) | copy-start | bytes 6291460
  35.4 3.5 %copy-start.1 = (bf16[512,2048]{1,0:T(8,128)(2,1)S(1)}, bf16[512,2048]{1,0:T(8,128)(2,1)}, u32[]{:S(2)}) copy-start(bf16[512,2048]{1,0:T(8,128)(2,1)} %refs_1_.7) | copy-start | bytes 6291460
  38.8 4.1 %collective-permute-start.11 = (f32[4,128,128]{2,1,0:T(8,128)S(1)}, f32[4,128,128]{2,1,0:T(8,128)S(1)}, u32[]{:S(2)}, u32[]{:S(2)}) collective-permute-start(f32[4,128,128]{2,1,0:T(8,128)S(1)} %get-tuple-element.85), channel_id=1, source_target_pairs={{0,1},{1,0},{2,3},{3,2},{4,5},{5,4},{6,7},{7,6},{8,9},{9,8},{10,11... | collective-permute-start | bytes 786440 | tf_op jit(solution)/shard_map/ppermute | solution.py:408
  42.4 1.6 %collective-permute-start.10 = (f32[4,128,128]{2,1,0:T(8,128)S(1)}, f32[4,128,128]{2,1,0:T(8,128)S(1)}, u32[]{:S(2)}, u32[]{:S(2)}) collective-permute-start(f32[4,128,128]{2,1,0:T(8,128)S(1)} %get-tuple-element.130), channel_id=1, source_target_pairs={{0,1},{1,0},{2,3},{3,2},{4,5},{5,4},{6,7},{7,6},{8,9},{9,8},{10,11... | collective-permute-start | bytes 786440 | tf_op jit(solution)/shard_map/ppermute | solution.py:446
  42.9 4.8 %collective-permute-start.13 = (f32[4,128,128]{2,1,0:T(8,128)S(1)}, f32[4,128,128]{2,1,0:T(8,128)S(1)}, u32[]{:S(2)}, u32[]{:S(2)}) collective-permute-start(f32[4,128,128]{2,1,0:T(8,128)S(1)} %select_add_fusion.1.refs_8_), channel_id=1, source_target_pairs={{12,8},{13,9},{14,10},{15,11},{28,24},{29,25},{30,26},{31,27}} | collective-permute-start | bytes 786440 | tf_op jit(solution)/shard_map/ppermute | solution.py:431
  47.3 1.6 %collective-permute-start.12 = (f32[4,128,128]{2,1,0:T(8,128)S(1)}, f32[4,128,128]{2,1,0:T(8,128)S(1)}, u32[]{:S(2)}, u32[]{:S(2)}) collective-permute-start(f32[4,128,128]{2,1,0:T(8,128)S(1)} %get-tuple-element.89), channel_id=1, source_target_pairs={{0,1},{1,0},{2,3},{3,2},{4,5},{5,4},{6,7},{7,6},{8,9},{9,8},{10,11... | collective-permute-start | bytes 786440 | tf_op jit(solution)/shard_map/ppermute | solution.py:408
  47.8 1.8 %collective-permute-start.15 = (f32[4,128,128]{2,1,0:T(8,128)S(1)}, f32[4,128,128]{2,1,0:T(8,128)S(1)}, u32[]{:S(2)}, u32[]{:S(2)}) collective-permute-start(f32[4,128,128]{2,1,0:T(8,128)S(1)} %multiply_add_fusion.5), channel_id=1, source_target_pairs={{8,4},{9,5},{10,6},{11,7},{24,20},{25,21},{26,22},{27,23}} | collective-permute-start | bytes 786440 | tf_op jit(solution)/shard_map/ppermute | solution.py:431
  48.9 0.8 collective-permute-start.14
  49.7 5.4 %collective-permute-start.16 = (f32[4,128,128]{2,1,0:T(8,128)S(1)}, f32[4,128,128]{2,1,0:T(8,128)S(1)}, u32[]{:S(2)}, u32[]{:S(2)}) collective-permute-start(f32[4,128,128]{2,1,0:T(8,128)S(1)} %multiply_add_fusion.3.refs_11_), channel_id=1, source_target_pairs={{8,4},{9,5},{10,6},{11,7},{24,20},{25,21},{26,22},{27,23}} | collective-permute-start | bytes 786440 | tf_op jit(solution)/shard_map/ppermute | solution.py:431
  50.4 23.3 %collective-permute-start.18 = (f32[4,128,128]{2,1,0:T(8,128)S(1)}, f32[4,128,128]{2,1,0:T(8,128)S(1)}, u32[]{:S(2)}, u32[]{:S(2)}) collective-permute-start(f32[4,128,128]{2,1,0:T(8,128)S(1)} %get-tuple-element.114), channel_id=1, source_target_pairs={{4,0},{5,1},{6,2},{7,3},{20,16},{21,17},{22,18},{23,19}} | collective-permute-start | bytes 786440 | tf_op jit(solution)/shard_map/ppermute | solution.py:431
  55.1 20.3 %copy-start.2 = (bf16[512,2048]{1,0:T(8,128)(2,1)S(1)}, bf16[512,2048]{1,0:T(8,128)(2,1)}, u32[]{:S(2)}) copy-start(bf16[512,2048]{1,0:T(8,128)(2,1)} %refs_0_.13) | copy-start | bytes 6291460
  73.8 1.6 %collective-permute-start.19 = (f32[4,128,128]{2,1,0:T(8,128)S(1)}, f32[4,128,128]{2,1,0:T(8,128)S(1)}, u32[]{:S(2)}, u32[]{:S(2)}) collective-permute-start(f32[4,128,128]{2,1,0:T(8,128)S(1)} %get-tuple-element.128), channel_id=1, source_target_pairs={{0,1},{1,0},{2,3},{3,2},{4,5},{5,4},{6,7},{7,6},{8,9},{9,8},{10,11... | collective-permute-start | bytes 786440 | tf_op jit(solution)/shard_map/ppermute | solution.py:446
  73.9 10.6 %collective-permute-start.17 = (f32[4,128,128]{2,1,0:T(8,128)S(1)}, f32[4,128,128]{2,1,0:T(8,128)S(1)}, u32[]{:S(2)}, u32[]{:S(2)}) collective-permute-start(f32[4,128,128]{2,1,0:T(8,128)S(1)} %get-tuple-element.112), channel_id=1, source_target_pairs={{4,0},{5,1},{6,2},{7,3},{20,16},{21,17},{22,18},{23,19}} | collective-permute-start | bytes 786440 | tf_op jit(solution)/shard_map/ppermute | solution.py:431
  84.5 1.6 %collective-permute-start.20 = (f32[4,128,128]{2,1,0:T(8,128)S(1)}, f32[4,128,128]{2,1,0:T(8,128)S(1)}, u32[]{:S(2)}, u32[]{:S(2)}) collective-permute-start(f32[4,128,128]{2,1,0:T(8,128)S(1)} %get-tuple-element.126), channel_id=1, source_target_pairs={{0,1},{1,0},{2,3},{3,2},{4,5},{5,4},{6,7},{7,6},{8,9},{9,8},{10,11... | collective-permute-start | bytes 786440 | tf_op jit(solution)/shard_map/ppermute | solution.py:446
